TPU v7x, 256 devices: a whole 4x4x8 slice. The times are simulated.
256 devices in a mesh: ctx: 32 (over z, x_lo, core), head: 8 (over x_hi, y).
Axes of the slice: x: 4 (x_hi: 2, x_lo: 2; x = x_hi * 2 + x_lo), y: 4, z: 8, core: 2. Of those that a mesh axis runs over, the one named last changes fastest.
Arguments:
- queries: bfloat16 [128, 128, 192], P('ctx', 'head'), may hold values from -200 to 200
- out_grad: bfloat16 [128, 128, 128], P('ctx', 'head'), may hold values from -6 to 6
- kv_up: bfloat16 [128, 512, 256], P('head'), may hold values from -0.25 to 0.25
- latent_cache: bfloat16 [32768, 576], P('ctx'), may hold values from -12 to 12
- token_ratio: float32 [128], P('ctx'), may hold values from -4 to 4
- pair_lens: int32 [4], replicated, may hold values from 1 to 64, 128 in all
- prompt_len: int32 [1], replicated, may hold values from 16384 to 32768
Outputs:
- query_grad: bfloat16 [128, 128, 192], P('ctx', 'head')
- cache_grad: bfloat16 [32768, 576], P(('ctx', 'head'))
All inputs are finite; a program needn't handle non-finite values.
Results may differ from a plain program's by a relative error of at most 0.029.
Values may be sent and summed in bfloat16 or wider, within the bound.
No kernel may reach another device: no remote copies, remote signals or barrier semaphores. Data moves between devices by JAX's collectives and lax.ppermute only.
A program may use at most 128 MiB of HBM per device.

v0:
```python
import functools

import jax
import jax.numpy as jnp
from jax import lax
from jax.experimental import pallas as pl
from jax.experimental.pallas import tpu as pltpu
from jax.sharding import PartitionSpec as P

BETA = 0.1
LOSS_SCALE = 2048.0
LOG2E = 1.4426950408889634
NEVER = -1e30
FLOOR = -1e29
F32 = jnp.float32
BF16 = jnp.bfloat16
CHUNK = 256
TOGETHER = 4
PACKED = 384
MIB = 1024 * 1024
ATTEND_MIB = 24
PROJECT_MIB = 8
WEIGH_MIB = 16
CACHE_MIB = 20


def permute(x, axis, to):
    return lax.ppermute(x, axis, [(i, to(i)) for i in range(lax.axis_size(axis))])


def in_order(mine, theirs, second, axis):
    return jnp.where(
        second,
        jnp.concatenate([theirs, mine], axis),
        jnp.concatenate([mine, theirs], axis),
    )


def join_stats(first, second):
    top = jnp.maximum(first[0:1], second[0:1])
    both = jnp.exp2(first[0:1] - top) * first + jnp.exp2(second[0:1] - top) * second
    return jnp.where(lax.broadcasted_iota(jnp.int32, both.shape, 0) == 0, top, both)


def join_kernel(first_ref, second_ref, out_ref):
    out_ref[...] = join_stats(first_ref[...], second_ref[...])


def join(first, second):
    vmem = pl.BlockSpec(memory_space=pltpu.VMEM)
    return pl.pallas_call(
        join_kernel,
        out_shape=jax.ShapeDtypeStruct(first.shape, F32),
        in_specs=[vmem, vmem],
        out_specs=vmem,
        compiler_params=pltpu.CompilerParams(vmem_limit_bytes=MIB),
    )(first, second)


def against(x, y):
    return lax.dot_general(x, y, (((1,), (1,)), ((), ())), preferred_element_type=F32)


def pack_kernel(where_ref, ratio_ref, queries_ref, out_grad_ref, mine_ref, theirs_ref):
    q_dev, heads, q_width = queries_ref.shape
    d_nope = out_grad_ref.shape[2]
    half = heads // 2
    d_rope = q_width - d_nope
    lane = lax.broadcasted_iota(jnp.int32, (heads, PACKED - 2 * d_nope - d_rope), 1)
    second = where_ref[0] == 1
    mine, theirs = [], []
    for j in range(q_dev):
        query = queries_ref[j].astype(F32)
        ratio = jnp.full(lane.shape, ratio_ref[j], F32)
        high = ratio.astype(BF16).astype(F32)
        middle = (ratio - high).astype(BF16).astype(F32)
        terms = jnp.where(lane == 0, high, jnp.where(lane == 1, middle, ratio - high - middle))
        terms = jnp.where(lane < 3, terms, 0.0)
        row = [query[:, :d_nope], out_grad_ref[j].astype(F32), query[:, d_nope:], terms]
        row = jnp.concatenate(row, axis=1)
        mine.append(jnp.where(second, row[half:], row[:half]))
        theirs.append(jnp.where(second, row[:half], row[half:]))
    mine_ref[...] = jnp.concatenate(mine, axis=0).astype(BF16)
    theirs_ref[...] = jnp.concatenate(theirs, axis=0).astype(BF16)


def pack(where, token_ratio, queries, out_grad):
    q_dev, heads = queries.shape[:2]
    smem = pl.BlockSpec(memory_space=pltpu.SMEM)
    vmem = pl.BlockSpec(memory_space=pltpu.VMEM)
    packed = jax.ShapeDtypeStruct((q_dev * heads // 2, PACKED), BF16)
    return pl.pallas_call(
        pack_kernel,
        out_shape=(packed, packed),
        in_specs=[smem, smem, vmem, vmem],
        out_specs=[vmem, vmem],
        compiler_params=pltpu.CompilerParams(vmem_limit_bytes=63 * MIB),
        cost_estimate=pl.CostEstimate(flops=0, bytes_accessed=32 * MIB, transcendentals=0),
    )(where, token_ratio, queries, out_grad)


def stage_kernel(cache_ref, out_ref):
    out_ref[...] = cache_ref[...].T


def stage(cache_t):
    c_width, keys = cache_t.shape
    vmem = pl.BlockSpec(memory_space=pltpu.VMEM)
    return pl.pallas_call(
        stage_kernel,
        out_shape=jax.ShapeDtypeStruct((keys, c_width), BF16),
        in_specs=[vmem],
        out_specs=vmem,
        compiler_params=pltpu.CompilerParams(vmem_limit_bytes=6 * MIB),
        cost_estimate=pl.CostEstimate(
            flops=keys * c_width, bytes_accessed=4 * keys * c_width, transcendentals=0
        ),
    )(cache_t)


def attend_kernel(score_scale, blocks, together, where_ref, *refs):
    ring_refs, refs = refs[:blocks], refs[blocks:]
    kv_ref, own_ref, other_ref, query_ref, grad_ref, expo_ref, spread_ref, stats_ref = refs[:8]
    ratio_ref, key_ref, raw, expo, dprod = refs[8:]
    size = ring_refs[0].shape[0]
    half, d_lat, d_nope = kv_ref.shape[0] // 2, kv_ref.shape[1], kv_ref.shape[2] // 2
    rows = size * blocks // half
    first_head = where_ref[0] * half
    d_rope = query_ref.shape[1] - d_lat
    keys = own_ref.shape[0]
    width = together * rows
    for k in range(blocks):
        first = pl.multiple_of(where_ref[4 + k] * size, size)
        for part in range(PACKED // 128):
            lanes = slice(part * 128, (part + 1) * 128)
            raw[part, pl.ds(first, size), :] = ring_refs[k][:, lanes].astype(F32)

    def of_head(h, part):
        return raw[part, pl.ds(h, rows, stride=half), :]

    terms = of_head(0, 2)
    lane = lax.broadcasted_iota(jnp.int32, terms.shape, 1)
    terms = jnp.where((lane >= d_rope) & (lane < d_rope + 3), terms, 0.0)
    ratio_ref[...] = jnp.broadcast_to(jnp.sum(terms, axis=1, keepdims=True), ratio_ref.shape)

    def fold(x, join):
        return join(join(x.reshape(CHUNK // 8, 8, width), axis=0), axis=0, keepdims=True)

    def group(p, carry):
        for j in range(together):
            h = p * together + j
            at = pl.ds(pl.multiple_of(h * rows, rows), rows)
            key_ref[h] = kv_ref[first_head + h, :, :d_nope]
            lat = against(of_head(h, 0).astype(BF16), key_ref[h])
            query_ref[at, :d_lat] = lat.astype(BF16)
            rope = of_head(h, 2)[:, :d_rope]
            query_ref[at, d_lat:] = rope.astype(BF16)
            lat = against(of_head(h, 1).astype(BF16), kv_ref[first_head + h, :, d_nope:])
            grad_ref[at, :] = lat.astype(BF16)
        columns = pl.ds(pl.multiple_of(p * width, width), width)
        tops, masses, dsums = [], [], []
        for c in range(2 * keys // CHUNK):
            first = c * CHUNK % keys
            ref, base = (own_ref, where_ref[1]) if c * CHUNK < keys else (other_ref, where_ref[2])
            score = against(ref[first : first + CHUNK, :], query_ref[columns, :]) * score_scale
            dp = against(ref[first : first + CHUNK, :d_lat], grad_ref[columns, :])
            key = base + first + lax.broadcasted_iota(jnp.int32, (CHUNK, 1), 0)
            score = jnp.where(key < where_ref[3], score, NEVER)
            top = jnp.maximum(fold(score, jnp.max), FLOOR)
            value = jnp.exp2(score - top)
            at = slice(c * CHUNK, (c + 1) * CHUNK)
            expo[at] = value
            dprod[at] = dp
            tops.append(top)
            masses.append(fold(value, jnp.sum))
            dsums.append(fold(value * dp, jnp.sum))
        top = functools.reduce(jnp.maximum, tops)
        factors = [jnp.exp2(t - top) for t in tops]
        mass = sum(f * m for f, m in zip(factors, masses))
        dsum = sum(f * d for f, d in zip(factors, dsums))
        centre = dsum / jnp.maximum(mass, 1e-30)
        for c, f in enumerate(factors):
            at = slice(c * CHUNK, (c + 1) * CHUNK)
            value = expo[at] * f
            expo_ref[at, columns] = value.astype(BF16)
            spread_ref[at, columns] = (value * (dprod[at] - centre)).astype(BF16)
        stats_ref[0:1, columns] = top
        stats_ref[1:2, columns] = mass
        stats_ref[2:3, columns] = dsum
        return carry

    lax.fori_loop(0, half // together, group, 0)


def attend(where, ring, kv_up, own, other, score_scale, together=TOGETHER):
    blocks, (size, packed) = len(ring), ring[0].shape
    half, d_lat = kv_up.shape[0] // 2, kv_up.shape[1]
    total = blocks * size
    rows = total // half
    keys, c_width = own.shape
    smem = pl.BlockSpec(memory_space=pltpu.SMEM)
    vmem = pl.BlockSpec(memory_space=pltpu.VMEM)
    return pl.pallas_call(
        functools.partial(attend_kernel, score_scale, blocks, together),
        out_shape=(
            jax.ShapeDtypeStruct((total, c_width), BF16),
            jax.ShapeDtypeStruct((total, d_lat), BF16),
            jax.ShapeDtypeStruct((2 * keys, total), BF16),
            jax.ShapeDtypeStruct((2 * keys, total), BF16),
            jax.ShapeDtypeStruct((3, total), F32),
            jax.ShapeDtypeStruct((rows, 128), F32),
            jax.ShapeDtypeStruct((half, d_lat, kv_up.shape[2] // 2), BF16),
        ),
        in_specs=[smem] + [vmem] * (blocks + 3),
        out_specs=[vmem] * 7,
        scratch_shapes=[
            pltpu.VMEM((packed // 128, total, 128), F32),
            pltpu.VMEM((2 * keys, together * rows), F32),
            pltpu.VMEM((2 * keys, together * rows), F32),
        ],
        compiler_params=pltpu.CompilerParams(vmem_limit_bytes=ATTEND_MIB * MIB),
        cost_estimate=pl.CostEstimate(
            flops=2 * 2 * keys * total * (c_width + d_lat),
            bytes_accessed=8 * keys * total,
            transcendentals=2 * keys * total,
        ),
    )(where, *ring, kv_up, own, other)


def project_kernel(p, own_ref, other_ref, spread_ref, expo_ref, key_ref, *out_refs):
    d_lat, d_nope = key_ref.shape[1:]
    keys = own_ref.shape[1]
    width = out_refs[0].shape[0]
    rows = spread_ref.shape[1] // key_ref.shape[0]
    columns = slice(p * width, (p + 1) * width)
    for terms_ref, out_ref in zip((spread_ref, expo_ref), out_refs):
        full = jnp.dot(own_ref[...], terms_ref[:keys, columns], preferred_element_type=F32)
        full = full + jnp.dot(
            other_ref[...], terms_ref[keys:, columns], preferred_element_type=F32
        )
        for j in range(width // rows):
            at = slice(j * rows, (j + 1) * rows)
            out_ref[at, :d_nope] = lax.dot_general(
                full[:d_lat, at].astype(BF16),
                key_ref[p * (width // rows) + j],
                (((0,), (0,)), ((), ())),
                preferred_element_type=F32,
            )
            out_ref[at, d_nope:] = full[d_lat:, at].T


def project(p, own_t, other_t, spread, expo, w_key, q_width):
    c_width, keys = own_t.shape
    width = 2 * spread.shape[1] // w_key.shape[0]
    vmem = pl.BlockSpec(memory_space=pltpu.VMEM)
    return pl.pallas_call(
        functools.partial(project_kernel, p),
        out_shape=(jax.ShapeDtypeStruct((width, q_width), F32),) * 2,
        in_specs=[vmem] * 5,
        out_specs=[vmem] * 2,
        compiler_params=pltpu.CompilerParams(vmem_limit_bytes=PROJECT_MIB * MIB),
        cost_estimate=pl.CostEstimate(
            flops=8 * keys * width * c_width, bytes_accessed=8 * keys * width, transcendentals=0
        ),
    )(own_t, other_t, spread, expo, w_key)


def row_gains(where_ref, lens_ref, ratio_ref, rows_of_core):
    rows = ratio_ref.shape[0]
    place = lax.broadcasted_iota(jnp.int32, (rows, 1), 0)
    turn = place % (2 * rows_of_core) >= rows_of_core
    swapped = jnp.where(turn, place - rows_of_core, place + rows_of_core)
    place = jnp.where(where_ref[0] == 1, swapped, place)
    ratio = ratio_ref[:, 0:1]
    segments = lens_ref.shape[0]
    members = []
    first = jnp.int32(0)
    for k in range(segments):
        last = first + lens_ref[k]
        members.append((place >= first) & (place < last))
        first = last
    sums = [jnp.sum(jnp.where(m, ratio, 0.0), axis=0, keepdims=True) for m in members]
    gains = jnp.zeros((rows, 1), F32)
    for p in range(segments // 2):
        margin = BETA * (sums[2 * p] - sums[2 * p + 1])
        weight = LOSS_SCALE * BETA / (1.0 + jnp.exp(margin))
        gains = jnp.where(members[2 * p], -weight, gains)
        gains = jnp.where(members[2 * p + 1], weight, gains)
    return gains


def weigh_kernel(scale, rows_of_core, where_ref, lens_ref, *refs):
    (joined_ref, last_ref, own_ref, ratio_ref, query_ref, grad_ref) = refs[:6]
    by_spread_refs, by_expo_refs = refs[6:-4:2], refs[7:-4:2]
    dq_keep_ref, dq_send_ref, with_spread_ref, with_expo_ref = refs[-4:]
    total = query_ref.shape[0]
    d_lat = grad_ref.shape[1]
    rows = ratio_ref.shape[0]
    half = total // rows
    gains = row_gains(where_ref, lens_ref, ratio_ref, rows_of_core)
    joined = join_stats(joined_ref[...], last_ref[...])
    centre = own_ref[2:3] / jnp.maximum(own_ref[1:2], 1e-30)
    factor = jnp.exp2(own_ref[0:1] - joined[0:1]) / joined[1:2]
    shift = joined[2:3] / joined[1:2] - centre
    sublane = lax.broadcasted_iota(jnp.int32, (8, total), 0)
    both = jnp.where(sublane == 0, factor, shift).T
    blocks, size = dq_keep_ref.shape[0], dq_keep_ref.shape[2] // 2
    second = where_ref[4 + blocks] == 1
    for h in range(half):
        at = slice(h * rows, (h + 1) * rows)
        part = slice((h % 2) * rows, (h % 2 + 1) * rows)
        factor = both[at, 0:1] * gains
        shift = both[at, 1:2]
        scaled = scale * factor
        dq = by_spread_refs[h // 2][part, :] - shift * by_expo_refs[h // 2][part, :]
        dq = scaled * dq
        if h % 2:
            for b in range(blocks):
                pieces = []
                for x in range(2):
                    first = (2 * b + x) * size
                    at_x = slice(first, first + size)
                    pieces.append(jnp.concatenate([before[at_x], dq[at_x]], axis=0))
                dq_keep_ref[b, h // 2] = jnp.where(second, pieces[1], pieces[0]).astype(BF16)
                dq_send_ref[b, h // 2] = jnp.where(second, pieces[0], pieces[1]).astype(BF16)
        before = dq
        query = scaled * query_ref[at, :].astype(F32)
        with_spread_ref[at, :] = query.astype(BF16)
        moved = shift * query
        with_expo_ref[at, :d_lat] = (
            factor * grad_ref[at, :].astype(F32) - moved[:, :d_lat]
        ).astype(BF16)
        with_expo_ref[at, d_lat:] = (-moved[:, d_lat:]).astype(BF16)


def weigh(where, lens, joined, last, stats, ratio, query, grad, projected, scale, blocks, q_dev):
    total, c_width = query.shape
    rows = ratio.shape[0]
    q_width = projected[0].shape[1]
    half = total // rows
    smem = pl.BlockSpec(memory_space=pltpu.SMEM)
    vmem = pl.BlockSpec(memory_space=pltpu.VMEM)
    dq = jax.ShapeDtypeStruct((blocks, half // 2, rows // blocks, q_width), BF16)
    weight = jax.ShapeDtypeStruct((total, c_width), BF16)
    inputs = (joined, last, stats, ratio, query, grad, *projected)
    return pl.pallas_call(
        functools.partial(weigh_kernel, scale, q_dev),
        out_shape=(dq, dq, weight, weight),
        in_specs=[smem, smem] + [vmem] * len(inputs),
        out_specs=[vmem] * 4,
        compiler_params=pltpu.CompilerParams(vmem_limit_bytes=WEIGH_MIB * MIB),
        cost_estimate=pl.CostEstimate(
            flops=10 * total * c_width, bytes_accessed=8 * total * c_width, transcendentals=0
        ),
    )(where, lens, *inputs)


def cache_kernel(part, d_lat, order_ref, spread_ref, expo_ref, with_spread_ref, with_expo_ref, *refs):
    adds, outs = refs[:-2], refs[-2:]
    keys = spread_ref.shape[3]

    def gather(ref):
        blocks = [ref[part, order_ref[i], order_ref[4 + i]] for i in range(4)]
        return jnp.concatenate(blocks, axis=0)

    out = jnp.dot(gather(spread_ref), with_spread_ref[...], preferred_element_type=F32)
    out = out + jnp.dot(gather(expo_ref), with_expo_ref[...], preferred_element_type=F32)
    rope = out.shape[1] - d_lat
    for i in range(4):
        first = (i % 2) * d_lat
        lat = slice(first, first + d_lat)
        first = 2 * d_lat + (i % 2) * rope
        tail = slice(first, first + rope)
        at = slice(i * keys, (i + 1) * keys)
        for lanes, value in ((lat, out[at, :d_lat]), (tail, out[at, d_lat:])):
            if adds:
                value = value + adds[i // 2][:, lanes].astype(F32)
            outs[i // 2][:, lanes] = value.astype(outs[i // 2].dtype)


def cache_terms(part, order, d_lat, spread, expo, with_spread, with_expo, dtypes, adds=()):
    total, c_width = with_spread.shape
    keys = spread.shape[3]
    smem = pl.BlockSpec(memory_space=pltpu.SMEM)
    vmem = pl.BlockSpec(memory_space=pltpu.VMEM)
    return pl.pallas_call(
        functools.partial(cache_kernel, part, d_lat),
        out_shape=[jax.ShapeDtypeStruct((keys, 2 * c_width), dtype) for dtype in dtypes],
        in_specs=[smem] + [vmem] * (4 + len(adds)),
        out_specs=[vmem, vmem],
        compiler_params=pltpu.CompilerParams(vmem_limit_bytes=CACHE_MIB * MIB),
        cost_estimate=pl.CostEstimate(
            flops=16 * keys * total * c_width,
            bytes_accessed=16 * keys * total,
            transcendentals=0,
        ),
    )(order, spread, expo, with_spread, with_expo, *adds)


def unfold(x, d_lat):
    rope = x.shape[1] // 2 - d_lat
    return [
        jnp.concatenate(
            [
                x[:, i * d_lat : (i + 1) * d_lat],
                x[:, 2 * d_lat + i * rope : 2 * d_lat + (i + 1) * rope],
            ],
            axis=1,
        )
        for i in range(2)
    ]


def fold_rows(x, d_lat, out_ref):
    size = x.shape[0] // 2
    rope = x.shape[1] - d_lat
    for i in range(2):
        part = x[i * size : (i + 1) * size].astype(BF16)
        out_ref[:, i * d_lat : (i + 1) * d_lat] = part[:, :d_lat]
        out_ref[:, 2 * d_lat + i * rope : 2 * d_lat + (i + 1) * rope] = part[:, d_lat:]


def forward_kernel(d_lat, keep_ref, arrived_ref, *out_refs):
    total = keep_ref[...].astype(F32) + arrived_ref[...].astype(F32)
    for block, out_ref in zip(unfold(total, d_lat), out_refs):
        fold_rows(block, d_lat, out_ref)


def turn_kernel(d_lat, own_ref, arrived_ref, send_ref, keep_ref):
    send, keep = unfold(own_ref[...] + arrived_ref[...].astype(F32), d_lat)
    fold_rows(send, d_lat, send_ref)
    keep_ref[...] = keep


def finish_kernel(d_lat, keep_ref, *refs):
    total = keep_ref[...]
    for arrived_ref in refs[:-1]:
        total = total + jnp.concatenate(unfold(arrived_ref[...].astype(F32), d_lat), axis=0)
    refs[-1][...] = total.T.astype(BF16)


def small(kernel, out_shape, *operands):
    vmem = pl.BlockSpec(memory_space=pltpu.VMEM)
    return pl.pallas_call(
        kernel,
        out_shape=out_shape,
        in_specs=[vmem] * len(operands),
        out_specs=jax.tree.map(lambda _: vmem, out_shape),
        compiler_params=pltpu.CompilerParams(vmem_limit_bytes=6 * MIB),
    )(*operands)


def per_device(queries, out_grad, kv_up, latent_cache, token_ratio, pair_lens, prompt_len):
    ctx_index = lax.axis_index("ctx")
    head_index = lax.axis_index("head")
    core = ctx_index & 1
    x_lo = (ctx_index >> 1) & 1
    z = ctx_index >> 2
    nz = lax.axis_size("ctx") // 4
    ny = lax.axis_size("head") // 2
    y = head_index & (ny - 1)
    x_hi = (head_index >= ny).astype(jnp.int32)
    other_core = lambda i: i ^ 1
    other_x_lo = lambda i: i ^ 2
    z_groups = [[4 * k + j for k in range(nz)] for j in range(4)]

    q_dev, heads, q_width = queries.shape
    p_dev, c_width = latent_cache.shape
    d_lat = kv_up.shape[1]
    d_rope = c_width - d_lat
    d_nope = q_width - d_rope
    half = heads // 2
    scale = q_width ** (-0.5)

    where = [core, ctx_index * p_dev, (ctx_index ^ 1) * p_dev, prompt_len[0]]
    where = where + [(z + k) & (nz - 1) for k in range(nz)] + [x_lo]
    where = jnp.stack(where).astype(jnp.int32)
    own_t = latent_cache.T
    other_t = permute(latent_cache, "ctx", other_core).T
    mine, theirs = pack(where, token_ratio, queries, out_grad)
    own_keys = stage(own_t)
    other_keys = stage(other_t)
    block = jnp.concatenate([mine, permute(theirs, "ctx", other_core)], 0)
    block = in_order(block, permute(block, "ctx", other_x_lo), x_lo == 1, 0)
    up = down = block
    ring = [block] + [None] * (nz - 1)
    for k in range(1, nz // 2 + 1):
        up = permute(up, "ctx", lambda i: (i + 4) % (4 * nz))
        ring[nz - k] = up
        if k < nz // 2:
            down = permute(down, "ctx", lambda i: (i - 4) % (4 * nz))
            ring[k] = down

    query, grad, expo, spread, stats, ratio, w_key = attend(
        where, ring, kv_up, own_keys, other_keys, scale * LOG2E
    )

    joined = stats
    projected = []
    pairings = [other_x_lo] + [lambda i, k=k: i ^ (4 << k) for k in range(nz.bit_length() - 1)]
    for p, pairing in enumerate(pairings):
        if p:
            joined = join(joined, last)
        last = permute(joined, "ctx", pairing)
        if p < half // 2:
            terms = project(p, own_t, other_t, spread, expo, w_key, q_width)
            last, *terms = lax.optimization_barrier((last, *terms))
            projected += terms
    dq_keep, dq_send, with_spread, with_expo = weigh(
        where, pair_lens, joined, last, stats, ratio, query, grad, projected, scale, nz, q_dev
    )
    dq_pair = permute(dq_send, "ctx", other_x_lo)
    keys = p_dev // (2 * ny)
    there, here = 1 - x_hi, x_hi
    along = [(y + k) & (ny - 1) for k in (0, 1, 2, 3)]
    orders = [
        [there, there, here, here, along[2], along[1], along[2], along[1]],
        [there, here, there, here, along[3], along[3], along[0], along[0]],
    ]
    orders = [jnp.stack(order).astype(jnp.int32) for order in orders]
    shape = (2, 2, ny, keys, spread.shape[1])
    operands = (d_lat, spread.reshape(shape), expo.reshape(shape), with_spread, with_expo)
    adds = []
    sends = cache_terms(1, orders[0], *operands, (BF16, BF16))
    later, *sends = lax.optimization_barrier((orders[1], *sends))
    adds.append([permute(x, "ctx", other_core) for x in sends])
    sends = cache_terms(1, later, *operands, (BF16, BF16))
    adds.append([permute(x, "ctx", other_core) for x in sends])
    to_x_hi = lambda x: permute(x, "head", lambda i: (i + ny) % (2 * ny))
    to_y = lambda x, k: permute(x, "head", lambda i: (i // ny) * ny + (i + k) % ny)
    send, keep = cache_terms(0, orders[0], *operands, (BF16, F32), adds[0])
    later, send = lax.optimization_barrier((orders[1], send))
    from_x_hi = to_x_hi(send)
    send, own = cache_terms(0, later, *operands, (BF16, F32), adds[1])
    dq = (dq_keep.astype(F32) + dq_pair.astype(F32)).astype(BF16)
    send, dq = lax.optimization_barrier((send, dq))
    from_y = to_y(send, 3)

    half_rows = jax.ShapeDtypeStruct((keys // 2, 2 * c_width), BF16)
    block = jax.ShapeDtypeStruct((keys, c_width), F32)
    sends = small(
        functools.partial(forward_kernel, d_lat), (half_rows, half_rows), keep, from_x_hi
    )
    arrived = [to_y(sends[0], 2), to_y(sends[1], 1)]
    send, keep = small(functools.partial(turn_kernel, d_lat), (half_rows, block), own, from_y)
    arrived.append(to_x_hi(send))
    cache_grad = small(
        functools.partial(finish_kernel, d_lat),
        jax.ShapeDtypeStruct((c_width, keys), BF16),
        keep,
        *arrived,
    ).T

    dq = lax.all_to_all(dq, "ctx", 0, 0, axis_index_groups=z_groups)
    dq = jnp.sum(dq.astype(F32), axis=0).astype(BF16).reshape(half, 2, q_dev, q_width)
    theirs = permute(dq[:, 1], "ctx", other_core)
    query_grad = jnp.transpose(in_order(dq[:, 0], theirs, core == 1, 0), (1, 0, 2))

    return (query_grad, cache_grad)


def solution(mesh):
    placed = (
        P("ctx", "head", None),
        P("ctx", "head", None),
        P("head", None, None),
        P("ctx", None),
        P("ctx"),
        P(),
        P(),
    )
    return jax.shard_map(
        per_device,
        mesh=mesh,
        in_specs=placed,
        out_specs=(P("ctx", "head", None), P(("ctx", "head"), None)),
        check_vma=False,
    )
```

profile of v0, /device:TPU:1, one launch (start us, length us, event | category | flops | bytes accessed | tf_op | source)
XLA Modules:
  0.0 114.1 jit_solution(14570374563063708811)
XLA Ops:
  0.6 3.3 %collective-permute-start.9 = (bf16[1024,576]{0,1:T(8,128)(2,1)}, bf16[1024,576]{0,1:T(8,128)(2,1)}, u32[]{:S(2)}, u32[]{:S(2)}) collective-permute-start(bf16[1024,576]{0,1:T(8,128)(2,1)} %param.10), channel_id=1, source_target_pairs={{0,8},{8,0},{16,24},{24,16},{32,40},{40,32},{48,56},{56,48},{64,72... | collective-permute-start | bytes 3538952 | tf_op jit(solution)/shard_map/ppermute | solution.py:28
  4.6 0.6 stack.93.where_ref
  5.2 1.5 %shard_map.86 = (bf16[32,384]{1,0:T(8,128)(2,1)}, bf16[32,384]{1,0:T(8,128)(2,1)}) custom-call(s32[13]{0:T(128)} %stack.93.where_ref, f32[4]{0:T(128)} %ratio_ref.1, bf16[4,16,192]{2,1,0:T(8,128)(2,1)} %queries_ref.1, bf16[4,16,128]{2,1,0:T(8,128)(2,1)} %out_grad_ref.1), custom_call_target="tpu_custom_call" | custom-call | bytes 33554432 | tf_op jit(solution)/shard_map/pallas_call | solution.py:92
  6.7 0.0 collective-permute-start
  6.7 1.4 %collective-permute-done = bf16[32,384]{1,0:T(8,128)(2,1)S(1)} collective-permute-done((bf16[32,384]{1,0:T(8,128)(2,1)}, bf16[32,384]{1,0:T(8,128)(2,1)S(1)}, u32[]{:S(2)}, u32[]{:S(2)}) %collective-permute-start) | collective-permute-done | bytes 24608 | tf_op jit(solution)/shard_map/ppermute | solution.py:28
  8.1 0.7 pad_maximum_fusion
  8.8 0.0 collective-permute-start.1
  8.8 2.9 %collective-permute-done.1 = bf16[64,384]{1,0:T(8,128)(2,1)S(1)} collective-permute-done((bf16[64,384]{1,0:T(8,128)(2,1)S(1)}, bf16[64,384]{1,0:T(8,128)(2,1)S(1)}, u32[]{:S(2)}, u32[]{:S(2)}) %collective-permute-start.1) | collective-permute-done | bytes 49184 | tf_op jit(solution)/shard_map/ppermute | solution.py:28
  11.7 0.8 maximum_select_fusion.refs_0_
  12.6 0.1 collective-permute-start.5
  12.7 3.9 %collective-permute-start.2 = (bf16[128,384]{1,0:T(8,128)(2,1)S(1)}, bf16[128,384]{1,0:T(8,128)(2,1)S(1)}, u32[]{:S(2)}, u32[]{:S(2)}) collective-permute-start(bf16[128,384]{1,0:T(8,128)(2,1)S(1)} %maximum_select_fusion.refs_0_), channel_id=1, source_target_pairs={{0,224},{8,232},{16,240},{24,248},{32,0},{40,8},{48,16},{56,24},{6... | collective-permute-start | bytes 294920 | tf_op jit(solution)/shard_map/ppermute | solution.py:28
  16.6 1.9 %collective-permute-done.5.refs_7_ = bf16[128,384]{1,0:T(8,128)(2,1)S(1)} collective-permute-done((bf16[128,384]{1,0:T(8,128)(2,1)S(1)}, bf16[128,384]{1,0:T(8,128)(2,1)S(1)}, u32[]{:S(2)}, u32[]{:S(2)}) %collective-permute-start.5) | collective-permute-done | bytes 98336 | tf_op jit(solution)/shard_map/ppermute | solution.py:28
  18.5 0.0 collective-permute-start.6
  18.5 0.0 collective-permute-done.2.refs_1_
  18.5 2.8 %collective-permute-start.3 = (bf16[128,384]{1,0:T(8,128)(2,1)S(1)}, bf16[128,384]{1,0:T(8,128)(2,1)S(1)}, u32[]{:S(2)}, u32[]{:S(2)}) collective-permute-start(bf16[128,384]{1,0:T(8,128)(2,1)S(1)} %collective-permute-done.2.refs_1_), channel_id=1, source_target_pairs={{0,224},{8,232},{16,240},{24,248},{32,0},{40,8},{48,16},{56,24},{6... | collective-permute-start | bytes 294920 | tf_op jit(solution)/shard_map/ppermute | solution.py:28
  21.3 1.9 %collective-permute-done.6.refs_6_ = bf16[128,384]{1,0:T(8,128)(2,1)S(1)} collective-permute-done((bf16[128,384]{1,0:T(8,128)(2,1)S(1)}, bf16[128,384]{1,0:T(8,128)(2,1)S(1)}, u32[]{:S(2)}, u32[]{:S(2)}) %collective-permute-start.6) | collective-permute-done | bytes 98336 | tf_op jit(solution)/shard_map/ppermute | solution.py:28
  23.2 0.0 collective-permute-start.7
  23.2 0.0 collective-permute-done.3.refs_2_
  23.2 2.8 %collective-permute-start.4 = (bf16[128,384]{1,0:T(8,128)(2,1)S(1)}, bf16[128,384]{1,0:T(8,128)(2,1)S(1)}, u32[]{:S(2)}, u32[]{:S(2)}) collective-permute-start(bf16[128,384]{1,0:T(8,128)(2,1)S(1)} %collective-permute-done.3.refs_2_), channel_id=1, source_target_pairs={{0,224},{8,232},{16,240},{24,248},{32,0},{40,8},{48,16},{56,24},{6... | collective-permute-start | bytes 294920 | tf_op jit(solution)/shard_map/ppermute | solution.py:28
  26.0 1.9 %collective-permute-done.7.refs_5_ = bf16[128,384]{1,0:T(8,128)(2,1)S(1)} collective-permute-done((bf16[128,384]{1,0:T(8,128)(2,1)S(1)}, bf16[128,384]{1,0:T(8,128)(2,1)S(1)}, u32[]{:S(2)}, u32[]{:S(2)}) %collective-permute-start.7) | collective-permute-done | bytes 98336 | tf_op jit(solution)/shard_map/ppermute | solution.py:28
  27.9 0.0 collective-permute-start.8
  27.9 0.1 stack.80.order_ref
  28.0 0.1 stack.77.order_ref
  28.0 1.3 %copy-done = bf16[1024,576]{0,1:T(8,128)(2,1)S(1)} copy-done((bf16[1024,576]{0,1:T(8,128)(2,1)S(1)}, bf16[1024,576]{0,1:T(8,128)(2,1)}, u32[]{:S(2)}) %copy-start) | copy-done | bytes 1179672
  29.3 0.4 shard_map.87.refs_9_
  29.7 0.0 collective-permute-done.9
  29.7 1.9 %shard_map.88.refs_10_ = bf16[1024,576]{1,0:T(8,128)(2,1)S(1)} custom-call(bf16[576,1024]{1,0:T(8,128)(2,1)} %bitcast.19.cache_ref.other_ref), custom_call_target="tpu_custom_call" | custom-call | flops 589824 | bytes 2359296 | tf_op jit(solution)/shard_map/pallas_call | solution.py:109
  31.6 0.0 copy-start.1
  31.6 1.1 collective-permute-done.8.refs_4_
  32.7 10.7 %shard_map.89 = (bf16[1024,576]{1,0:T(8,128)(2,1)S(1)}, bf16[1024,512]{1,0:T(8,128)(2,1)S(1)}, bf16[2048,1024]{1,0:T(8,128)(2,1)S(1)}, bf16[2048,1024]{1,0:T(8,1...) custom-call(s32[13]{0:T(128)S(1)} %copy-done.2, ...), custom_call_target="tpu_custom_call" | custom-call | flops 4563402752 | bytes 8388608 | tf_op jit(solution)/shard_map/pallas_call | solution.py:203
  43.5 1.3 %collective-permute-start.10 = (f32[3,1024]{1,0:T(4,128)S(1)}, f32[3,1024]{1,0:T(4,128)S(1)}, u32[]{:S(2)}, u32[]{:S(2)}) collective-permute-start(f32[3,1024]{1,0:T(4,128)S(1)} %get-tuple-element.58.first_ref.refs_2_), channel_id=1, source_target_pairs={{0,16},{8,24},{16,0},{24,8},{32,48},{40,56},{48,32},{56,40},{64,80... | collective-permute-start | bytes 36872 | tf_op jit(solution)/shard_map/ppermute | solution.py:28
  44.8 4.3 %shard_map.90 = (f32[256,192]{1,0:T(8,128)S(1)}, f32[256,192]{1,0:T(8,128)S(1)}) custom-call(bf16[576,1024]{1,0:T(8,128)(2,1)S(1)} %bitcast.40, bf16[576,1024]{1,0:T(8,128)(2,1)} %bitcast.19.cache_ref.other_ref, bf16[2048,1024]{1,0:T(8,128)(2,1)S(1)} %get-tuple-element.56.spread_ref, bf16[2048,1024]{1,0:T(8,128)(2,1)S(1)} %get-tuple-element.57.expo_ref, ...), custom_call_target="tpu_custom_call" | custom-call | flops 1207959552 | bytes 2097152 | tf_op jit(solution)/shard_map/pallas_call | solution.py:256
  49.2 0.1 collective-permute-start.11
  49.3 4.3 %shard_map.92 = (f32[256,192]{1,0:T(8,128)S(1)}, f32[256,192]{1,0:T(8,128)S(1)}) custom-call(bf16[576,1024]{1,0:T(8,128)(2,1)S(1)} %bitcast.41, bf16[576,1024]{1,0:T(8,128)(2,1)} %bitcast.19.cache_ref.other_ref, bf16[2048,1024]{1,0:T(8,128)(2,1)S(1)} %get-tuple-element.56.spread_ref, bf16[2048,1024]{1,0:T(8,128)(2,1)S(1)} %get-tuple-element.57.expo_ref, ...), custom_call_target="tpu_custom_call" | custom-call | flops 1207959552 | bytes 2097152 | tf_op jit(solution)/shard_map/pallas_call | solution.py:256
  53.6 3.8 %collective-permute-start.12 = (f32[3,1024]{1,0:T(4,128)S(1)}, f32[3,1024]{1,0:T(4,128)S(1)}, u32[]{:S(2)}, u32[]{:S(2)}) collective-permute-start(f32[3,1024]{1,0:T(4,128)S(1)} %shard_map.93.first_ref), channel_id=1, source_target_pairs={{0,64},{8,72},{16,80},{24,88},{32,96},{40,104},{48,112},{56,120},{... | collective-permute-start | bytes 36872 | tf_op jit(solution)/shard_map/ppermute | solution.py:28
  57.4 4.3 %shard_map.94 = (f32[256,192]{1,0:T(8,128)S(1)}, f32[256,192]{1,0:T(8,128)S(1)}) custom-call(bf16[576,1024]{1,0:T(8,128)(2,1)S(1)} %bitcast.42, bf16[576,1024]{1,0:T(8,128)(2,1)} %bitcast.19.cache_ref.other_ref, bf16[2048,1024]{1,0:T(8,128)(2,1)S(1)} %get-tuple-element.56.spread_ref, bf16[2048,1024]{1,0:T(8,128)(2,1)S(1)} %get-tuple-element.57.expo_ref, ...), custom_call_target="tpu_custom_call" | custom-call | flops 1207959552 | bytes 2097152 | tf_op jit(solution)/shard_map/pallas_call | solution.py:256
  61.8 0.0 copy-start.3
  61.8 1.7 %collective-permute-start.13 = (f32[3,1024]{1,0:T(4,128)S(1)}, f32[3,1024]{1,0:T(4,128)S(1)}, u32[]{:S(2)}, u32[]{:S(2)}) collective-permute-start(f32[3,1024]{1,0:T(4,128)S(1)} %shard_map.95.refs_0_), channel_id=1, source_target_pairs={{0,128},{8,136},{16,144},{24,152},{32,160},{40,168},{48,176},{56,1... | collective-permute-start | bytes 36872 | tf_op jit(solution)/shard_map/ppermute | solution.py:28
  63.5 4.3 %shard_map.96 = (f32[256,192]{1,0:T(8,128)S(1)}, f32[256,192]{1,0:T(8,128)S(1)}) custom-call(bf16[576,1024]{1,0:T(8,128)(2,1)S(1)} %bitcast.43, bf16[576,1024]{1,0:T(8,128)(2,1)} %bitcast.19.cache_ref.other_ref, bf16[2048,1024]{1,0:T(8,128)(2,1)S(1)} %get-tuple-element.56.spread_ref, bf16[2048,1024]{1,0:T(8,128)(2,1)S(1)} %get-tuple-element.57.expo_ref, ...), custom_call_target="tpu_custom_call" | custom-call | flops 1207959552 | bytes 2097152 | tf_op jit(solution)/shard_map/pallas_call | solution.py:256
  67.9 0.8 collective-permute-done.13.refs_1_
  68.6 1.7 %shard_map.97 = (bf16[8,4,16,192]{3,2,1,0:T(8,128)(2,1)S(1)}, bf16[8,4,16,192]{3,2,1,0:T(8,128)(2,1)S(1)}, bf16[1024,576]{1,0:T(8,128)(2,1)S(1)}, bf16[1024,576]{1,0:T(8,128)(2,1)S(1)}) custom-call(s32[13]{0:T(128)S(1)} %copy-done.2, s32[4]{0:T(128)S(1)} %copy-done.3, f32[3,1024]{1,0:T(4,128)S(1)} %shard_map.95.refs_0_, ...), custom_call_target="tpu_custom_call" | custom-call | flops 5898240 | bytes 4718592 | tf_op jit(solution)/shard_map/pallas_call | solution.py:346
  70.3 0.3 collective-permute-start.18
  70.7 2.4 %shard_map.98 = (bf16[128,1152]{1,0:T(8,128)(2,1)S(1)}, bf16[128,1152]{1,0:T(8,128)(2,1)S(1)}) custom-call(s32[8]{0:T(128)S(1)} %stack.80.order_ref, bf16[2,2,4,128,1024]{4,3,2,1,0:T(8,128)(2,1)S(1)} %bitcast.35, bf16[2,2,4,128,1024]{4,3,2,1,0:T(8,128)(2,1)S(1)} %bitcast.31, bf16[1024,576]{1,0:T(8,128)(2,1)S(1)} %get-tuple-element.83.with_spread_ref, ...), custom_call_target="tpu_custom_call" | custom-call | flops 1207959552 | bytes 2097152 | tf_op jit(solution)/shard_map/pallas_call | solution.py:386
  73.1 7.9 %collective-permute-start.14 = (bf16[128,1152]{1,0:T(8,128)(2,1)S(1)}, bf16[128,1152]{1,0:T(8,128)(2,1)S(1)}, u32[]{:S(2)}, u32[]{:S(2)}) collective-permute-start(bf16[128,1152]{1,0:T(8,128)(2,1)S(1)} %get-tuple-element.87), channel_id=1, source_target_pairs={{0,8},{8,0},{16,24},{24,16},{32,40},{40,32},{48,56},{56,48},{64,72... | collective-permute-start | bytes 884744 | tf_op jit(solution)/shard_map/ppermute | solution.py:28
  81.0 0.1 collective-permute-start.15
  81.1 2.4 %shard_map.100 = (bf16[128,1152]{1,0:T(8,128)(2,1)S(1)}, bf16[128,1152]{1,0:T(8,128)(2,1)S(1)}) custom-call(s32[8]{0:T(128)S(1)} %stack.77.order_ref, bf16[2,2,4,128,1024]{4,3,2,1,0:T(8,128)(2,1)S(1)} %bitcast.36, bf16[2,2,4,128,1024]{4,3,2,1,0:T(8,128)(2,1)S(1)} %bitcast.32, bf16[1024,576]{1,0:T(8,128)(2,1)S(1)} %get-tuple-element.83.with_spread_ref, ...), custom_call_target="tpu_custom_call" | custom-call | flops 1207959552 | bytes 2097152 | tf_op jit(solution)/shard_map/pallas_call | solution.py:386
  83.5 0.5 collective-permute-start.16
  84.0 0.1 collective-permute-start.17
  84.1 0.8 add_convert_fusion
  84.9 2.4 %shard_map.99 = (bf16[128,1152]{1,0:T(8,128)(2,1)S(1)}, f32[128,1152]{1,0:T(8,128)S(1)}) custom-call(s32[8]{0:T(128)S(1)} %stack.80.order_ref, bf16[2,2,4,128,1024]{4,3,2,1,0:T(8,128)(2,1)S(1)} %bitcast.37, bf16[2,2,4,128,1024]{4,3,2,1,0:T(8,128)(2,1)S(1)} %bitcast.33, bf16[1024,576]{1,0:T(8,128)(2,1)S(1)} %get-tuple-element.83.with_spread_ref, ...), custom_call_target="tpu_custom_call" | custom-call | flops 1207959552 | bytes 2097152 | tf_op jit(solution)/shard_map/pallas_call | solution.py:386
  87.3 2.4 %shard_map.101 = (bf16[128,1152]{1,0:T(8,128)(2,1)S(1)}, f32[128,1152]{1,0:T(8,128)S(1)}) custom-call(s32[8]{0:T(128)S(1)} %stack.77.order_ref, bf16[2,2,4,128,1024]{4,3,2,1,0:T(8,128)(2,1)S(1)} %bitcast.38, bf16[2,2,4,128,1024]{4,3,2,1,0:T(8,128)(2,1)S(1)} %bitcast.34, bf16[1024,576]{1,0:T(8,128)(2,1)S(1)} %get-tuple-element.83.with_spread_ref, ...), custom_call_target="tpu_custom_call" | custom-call | flops 1207959552 | bytes 2097152 | tf_op jit(solution)/shard_map/pallas_call | solution.py:386
  89.7 3.7 %all-to-all-start = ((bf16[8,4,16,192]{3,2,1,0:T(8,128)(2,1)}), bf16[8,4,16,192]{3,2,1,0:T(8,128)(2,1)S(1)}, u32[]{:S(2)}, u32[]{:S(2)}) async-start(bf16[8,4,16,192]{3,2,1,0:T(8,128)(2,1)} %add_convert_fusion), calls=%async_computation | async-start | bytes 524288 | tf_op jit(solution)/shard_map/all_to_all | solution.py:554
  93.4 2.7 %collective-permute-start.21 = (bf16[128,1152]{1,0:T(8,128)(2,1)S(1)}, bf16[128,1152]{1,0:T(8,128)(2,1)S(1)}, u32[]{:S(2)}, u32[]{:S(2)}) collective-permute-start(bf16[128,1152]{1,0:T(8,128)(2,1)S(1)} %get-tuple-element.102), channel_id=1, source_target_pairs={{0,4},{1,5},{2,6},{3,7},{4,0},{5,1},{6,2},{7,3},{8,12},{9,13},{10,... | collective-permute-start | bytes 884744 | tf_op jit(solution)/shard_map/ppermute | solution.py:28
  96.2 2.7 %collective-permute-start.20 = (bf16[128,1152]{1,0:T(8,128)(2,1)S(1)}, bf16[128,1152]{1,0:T(8,128)(2,1)S(1)}, u32[]{:S(2)}, u32[]{:S(2)}) collective-permute-start(bf16[128,1152]{1,0:T(8,128)(2,1)S(1)} %get-tuple-element.99), channel_id=1, source_target_pairs={{0,3},{1,0},{2,1},{3,2},{4,7},{5,4},{6,5},{7,6},{8,11},{9,8},{10,9... | collective-permute-start | bytes 884744 | tf_op jit(solution)/shard_map/ppermute | solution.py:28
  98.9 3.9 %collective-permute-done.21.arrived_ref = bf16[128,1152]{1,0:T(8,128)(2,1)S(1)} collective-permute-done((bf16[128,1152]{1,0:T(8,128)(2,1)S(1)}, bf16[128,1152]{1,0:T(8,128)(2,1)S(1)}, u32[]{:S(2)}, u32[]{:S(2)}) %collective-permute-start.21) | collective-permute-done | bytes 294944 | tf_op jit(solution)/shard_map/ppermute | solution.py:28
  102.8 0.1 shard_map.103
  102.9 2.9 %collective-permute-start.22 = (bf16[64,1152]{1,0:T(8,128)(2,1)S(1)}, bf16[64,1152]{1,0:T(8,128)(2,1)S(1)}, u32[]{:S(2)}, u32[]{:S(2)}) collective-permute-start(bf16[64,1152]{1,0:T(8,128)(2,1)S(1)} %get-tuple-element.103), channel_id=1, source_target_pairs={{0,2},{1,3},{2,0},{3,1},{4,6},{5,7},{6,4},{7,5},{8,10},{9,11},{10,... | collective-permute-start | bytes 442376 | tf_op jit(solution)/shard_map/ppermute | solution.py:28
  105.9 0.4 collective-permute-start.23
  106.3 0.1 shard_map.102
  106.4 2.8 %collective-permute-start.24 = (bf16[64,1152]{1,0:T(8,128)(2,1)S(1)}, bf16[64,1152]{1,0:T(8,128)(2,1)S(1)}, u32[]{:S(2)}, u32[]{:S(2)}) collective-permute-start(bf16[64,1152]{1,0:T(8,128)(2,1)S(1)} %get-tuple-element.105), channel_id=1, source_target_pairs={{0,4},{1,5},{2,6},{3,7},{4,0},{5,1},{6,2},{7,3},{8,12},{9,13},{10,... | collective-permute-start | bytes 442376 | tf_op jit(solution)/shard_map/ppermute | solution.py:28
  109.3 2.5 %collective-permute-start.19 = (bf16[8,4,192]{2,1,0:T(4,128)(2,1)S(1)}, bf16[8,4,192]{2,1,0:T(4,128)(2,1)S(1)}, u32[]{:S(2)}, u32[]{:S(2)}) collective-permute-start(bf16[8,4,192]{2,1,0:T(4,128)(2,1)S(1)} %get-tuple-element.108), channel_id=1, source_target_pairs={{0,8},{8,0},{16,24},{24,16},{32,40},{40,32},{48,56},{56,48},{64,72... | collective-permute-start | bytes 36872 | tf_op jit(solution)/shard_map/ppermute | solution.py:28
  111.8 0.8 collective-permute-done.19
  112.7 0.6 copy.10
  113.3 0.8 shard_map.104
  (28 shorter events, 0.2 us)
Async XLA Ops:
  0.6 29.1 %collective-permute-start.9 = (bf16[1024,576]{0,1:T(8,128)(2,1)}, bf16[1024,576]{0,1:T(8,128)(2,1)}, u32[]{:S(2)}, u32[]{:S(2)}) collective-permute-start(bf16[1024,576]{0,1:T(8,128)(2,1)} %param.10), channel_id=1, source_target_pairs={{0,8},{8,0},{16,24},{24,16},{32,40},{40,32},{48,56},{56,48},{64,72... | collective-permute-start | bytes 3538952 | tf_op jit(solution)/shard_map/ppermute | solution.py:28
  6.7 1.4 %collective-permute-start = (bf16[32,384]{1,0:T(8,128)(2,1)}, bf16[32,384]{1,0:T(8,128)(2,1)S(1)}, u32[]{:S(2)}, u32[]{:S(2)}) collective-permute-start(bf16[32,384]{1,0:T(8,128)(2,1)} %get-tuple-element.55), channel_id=1, source_target_pairs={{0,8},{8,0},{16,24},{24,16},{32,40},{40,32},{48,56},{56,48},{64,72... | collective-permute-start | bytes 73736 | tf_op jit(solution)/shard_map/ppermute | solution.py:28
  8.8 2.9 %collective-permute-start.1 = (bf16[64,384]{1,0:T(8,128)(2,1)S(1)}, bf16[64,384]{1,0:T(8,128)(2,1)S(1)}, u32[]{:S(2)}, u32[]{:S(2)}) collective-permute-start(bf16[64,384]{1,0:T(8,128)(2,1)S(1)} %pad_maximum_fusion), channel_id=1, source_target_pairs={{0,16},{8,24},{16,0},{24,8},{32,48},{40,56},{48,32},{56,40},{64,80... | collective-permute-start | bytes 147464 | tf_op jit(solution)/shard_map/ppermute | solution.py:28
  12.6 5.9 %collective-permute-start.5 = (bf16[128,384]{1,0:T(8,128)(2,1)S(1)}, bf16[128,384]{1,0:T(8,128)(2,1)S(1)}, u32[]{:S(2)}, u32[]{:S(2)}) collective-permute-start(bf16[128,384]{1,0:T(8,128)(2,1)S(1)} %maximum_select_fusion.refs_0_), channel_id=1, source_target_pairs={{0,32},{8,40},{16,48},{24,56},{32,64},{40,72},{48,80},{56,88},{64,... | collective-permute-start | bytes 294920 | tf_op jit(solution)/shard_map/ppermute | solution.py:28
  12.7 5.8 %collective-permute-start.2 = (bf16[128,384]{1,0:T(8,128)(2,1)S(1)}, bf16[128,384]{1,0:T(8,128)(2,1)S(1)}, u32[]{:S(2)}, u32[]{:S(2)}) collective-permute-start(bf16[128,384]{1,0:T(8,128)(2,1)S(1)} %maximum_select_fusion.refs_0_), channel_id=1, source_target_pairs={{0,224},{8,232},{16,240},{24,248},{32,0},{40,8},{48,16},{56,24},{6... | collective-permute-start | bytes 294920 | tf_op jit(solution)/shard_map/ppermute | solution.py:28
  18.5 4.7 %collective-permute-start.6 = (bf16[128,384]{1,0:T(8,128)(2,1)S(1)}, bf16[128,384]{1,0:T(8,128)(2,1)S(1)}, u32[]{:S(2)}, u32[]{:S(2)}) collective-permute-start(bf16[128,384]{1,0:T(8,128)(2,1)S(1)} %collective-permute-done.5.refs_7_), channel_id=1, source_target_pairs={{0,32},{8,40},{16,48},{24,56},{32,64},{40,72},{48,80},{56,88},{64,... | collective-permute-start | bytes 294920 | tf_op jit(solution)/shard_map/ppermute | solution.py:28
  18.5 4.7 %collective-permute-start.3 = (bf16[128,384]{1,0:T(8,128)(2,1)S(1)}, bf16[128,384]{1,0:T(8,128)(2,1)S(1)}, u32[]{:S(2)}, u32[]{:S(2)}) collective-permute-start(bf16[128,384]{1,0:T(8,128)(2,1)S(1)} %collective-permute-done.2.refs_1_), channel_id=1, source_target_pairs={{0,224},{8,232},{16,240},{24,248},{32,0},{40,8},{48,16},{56,24},{6... | collective-permute-start | bytes 294920 | tf_op jit(solution)/shard_map/ppermute | solution.py:28
  23.2 4.7 %collective-permute-start.7 = (bf16[128,384]{1,0:T(8,128)(2,1)S(1)}, bf16[128,384]{1,0:T(8,128)(2,1)S(1)}, u32[]{:S(2)}, u32[]{:S(2)}) collective-permute-start(bf16[128,384]{1,0:T(8,128)(2,1)S(1)} %collective-permute-done.6.refs_6_), channel_id=1, source_target_pairs={{0,32},{8,40},{16,48},{24,56},{32,64},{40,72},{48,80},{56,88},{64,... | collective-permute-start | bytes 294920 | tf_op jit(solution)/shard_map/ppermute | solution.py:28
  23.2 8.4 %collective-permute-start.4 = (bf16[128,384]{1,0:T(8,128)(2,1)S(1)}, bf16[128,384]{1,0:T(8,128)(2,1)S(1)}, u32[]{:S(2)}, u32[]{:S(2)}) collective-permute-start(bf16[128,384]{1,0:T(8,128)(2,1)S(1)} %collective-permute-done.3.refs_2_), channel_id=1, source_target_pairs={{0,224},{8,232},{16,240},{24,248},{32,0},{40,8},{48,16},{56,24},{6... | collective-permute-start | bytes 294920 | tf_op jit(solution)/shard_map/ppermute | solution.py:28
  27.9 4.8 %collective-permute-start.8 = (bf16[128,384]{1,0:T(8,128)(2,1)S(1)}, bf16[128,384]{1,0:T(8,128)(2,1)S(1)}, u32[]{:S(2)}, u32[]{:S(2)}) collective-permute-start(bf16[128,384]{1,0:T(8,128)(2,1)S(1)} %collective-permute-done.7.refs_5_), channel_id=1, source_target_pairs={{0,32},{8,40},{16,48},{24,56},{32,64},{40,72},{48,80},{56,88},{64,... | collective-permute-start | bytes 294920 | tf_op jit(solution)/shard_map/ppermute | solution.py:28
  28.0 1.3 %copy-start = (bf16[1024,576]{0,1:T(8,128)(2,1)S(1)}, bf16[1024,576]{0,1:T(8,128)(2,1)}, u32[]{:S(2)}) copy-start(bf16[1024,576]{0,1:T(8,128)(2,1)} %param.10) | copy-start | bytes 3538948
  29.3 3.4 %copy-start.4 = (bf16[16,512,256]{2,1,0:T(8,128)(2,1)S(1)}, bf16[16,512,256]{2,1,0:T(8,128)(2,1)}, u32[]{:S(2)}) copy-start(bf16[16,512,256]{2,1,0:T(8,128)(2,1)} %refs_8_.1) | copy-start | bytes 12582916
  29.7 3.0 %copy-start.2 = (s32[13]{0:T(128)S(1)}, s32[13]{0:T(128)}, u32[]{:S(2)}) copy-start(s32[13]{0:T(128)} %stack.93.where_ref) | copy-start | bytes 160
  31.6 13.1 %copy-start.1 = (bf16[1024,576]{0,1:T(8,128)(2,1)S(1)}, bf16[1024,576]{0,1:T(8,128)(2,1)}, u32[]{:S(2)}) copy-start(bf16[1024,576]{0,1:T(8,128)(2,1)} %param.10) | copy-start | bytes 3538948
  43.5 5.6 %collective-permute-start.10 = (f32[3,1024]{1,0:T(4,128)S(1)}, f32[3,1024]{1,0:T(4,128)S(1)}, u32[]{:S(2)}, u32[]{:S(2)}) collective-permute-start(f32[3,1024]{1,0:T(4,128)S(1)} %get-tuple-element.58.first_ref.refs_2_), channel_id=1, source_target_pairs={{0,16},{8,24},{16,0},{24,8},{32,48},{40,56},{48,32},{56,40},{64,80... | collective-permute-start | bytes 36872 | tf_op jit(solution)/shard_map/ppermute | solution.py:28
  49.2 4.5 %collective-permute-start.11 = (f32[3,1024]{1,0:T(4,128)S(1)}, f32[3,1024]{1,0:T(4,128)S(1)}, u32[]{:S(2)}, u32[]{:S(2)}) collective-permute-start(f32[3,1024]{1,0:T(4,128)S(1)} %shard_map.91.first_ref), channel_id=1, source_target_pairs={{0,32},{8,40},{16,48},{24,56},{32,0},{40,8},{48,16},{56,24},{64,96... | collective-permute-start | bytes 36872 | tf_op jit(solution)/shard_map/ppermute | solution.py:28
  53.6 8.1 %collective-permute-start.12 = (f32[3,1024]{1,0:T(4,128)S(1)}, f32[3,1024]{1,0:T(4,128)S(1)}, u32[]{:S(2)}, u32[]{:S(2)}) collective-permute-start(f32[3,1024]{1,0:T(4,128)S(1)} %shard_map.93.first_ref), channel_id=1, source_target_pairs={{0,64},{8,72},{16,80},{24,88},{32,96},{40,104},{48,112},{56,120},{... | collective-permute-start | bytes 36872 | tf_op jit(solution)/shard_map/ppermute | solution.py:28
  61.8 6.8 %copy-start.3 = (s32[4]{0:T(128)S(1)}, s32[4]{0:T(128)}, u32[]{:S(2)}) copy-start(s32[4]{0:T(128)} %lens_ref.1) | copy-start | bytes 52
  61.8 6.8 %collective-permute-start.13 = (f32[3,1024]{1,0:T(4,128)S(1)}, f32[3,1024]{1,0:T(4,128)S(1)}, u32[]{:S(2)}, u32[]{:S(2)}) collective-permute-start(f32[3,1024]{1,0:T(4,128)S(1)} %shard_map.95.refs_0_), channel_id=1, source_target_pairs={{0,128},{8,136},{16,144},{24,152},{32,160},{40,168},{48,176},{56,1... | collective-permute-start | bytes 36872 | tf_op jit(solution)/shard_map/ppermute | solution.py:28
  70.3 13.8 %collective-permute-start.18 = (bf16[8,4,16,192]{3,2,1,0:T(8,128)(2,1)S(1)}, bf16[8,4,16,192]{3,2,1,0:T(8,128)(2,1)S(1)}, u32[]{:S(2)}, u32[]{:S(2)}) collective-permute-start(bf16[8,4,16,192]{3,2,1,0:T(8,128)(2,1)S(1)} %get-tuple-element.96), channel_id=1, source_target_pairs={{0,16},{8,24},{16,0},{24,8},{32,48},{40,56},{48,32},{56,40},{64,80... | collective-permute-start | bytes 589832 | tf_op jit(solution)/shard_map/ppermute | solution.py:28
  73.1 11.8 %collective-permute-start.14 = (bf16[128,1152]{1,0:T(8,128)(2,1)S(1)}, bf16[128,1152]{1,0:T(8,128)(2,1)S(1)}, u32[]{:S(2)}, u32[]{:S(2)}) collective-permute-start(bf16[128,1152]{1,0:T(8,128)(2,1)S(1)} %get-tuple-element.87), channel_id=1, source_target_pairs={{0,8},{8,0},{16,24},{24,16},{32,40},{40,32},{48,56},{56,48},{64,72... | collective-permute-start | bytes 884744 | tf_op jit(solution)/shard_map/ppermute | solution.py:28
  81.0 3.9 %collective-permute-start.15 = (bf16[128,1152]{1,0:T(8,128)(2,1)S(1)}, bf16[128,1152]{1,0:T(8,128)(2,1)S(1)}, u32[]{:S(2)}, u32[]{:S(2)}) collective-permute-start(bf16[128,1152]{1,0:T(8,128)(2,1)S(1)} %get-tuple-element.88), channel_id=1, source_target_pairs={{0,8},{8,0},{16,24},{24,16},{32,40},{40,32},{48,56},{56,48},{64,72... | collective-permute-start | bytes 884744 | tf_op jit(solution)/shard_map/ppermute | solution.py:28
  83.5 3.8 %collective-permute-start.16 = (bf16[128,1152]{1,0:T(8,128)(2,1)S(1)}, bf16[128,1152]{1,0:T(8,128)(2,1)S(1)}, u32[]{:S(2)}, u32[]{:S(2)}) collective-permute-start(bf16[128,1152]{1,0:T(8,128)(2,1)S(1)} %get-tuple-element.92), channel_id=1, source_target_pairs={{0,8},{8,0},{16,24},{24,16},{32,40},{40,32},{48,56},{56,48},{64,72... | collective-permute-start | bytes 884744 | tf_op jit(solution)/shard_map/ppermute | solution.py:28
  84.0 3.3 %collective-permute-start.17 = (bf16[128,1152]{1,0:T(8,128)(2,1)S(1)}, bf16[128,1152]{1,0:T(8,128)(2,1)S(1)}, u32[]{:S(2)}, u32[]{:S(2)}) collective-permute-start(bf16[128,1152]{1,0:T(8,128)(2,1)S(1)} %get-tuple-element.93), channel_id=1, source_target_pairs={{0,8},{8,0},{16,24},{24,16},{32,40},{40,32},{48,56},{56,48},{64,72... | collective-permute-start | bytes 884744 | tf_op jit(solution)/shard_map/ppermute | solution.py:28
  89.7 19.5 %all-to-all-start = ((bf16[8,4,16,192]{3,2,1,0:T(8,128)(2,1)}), bf16[8,4,16,192]{3,2,1,0:T(8,128)(2,1)S(1)}, u32[]{:S(2)}, u32[]{:S(2)}) async-start(bf16[8,4,16,192]{3,2,1,0:T(8,128)(2,1)} %add_convert_fusion), calls=%async_computation | async-start | bytes 524288 | tf_op jit(solution)/shard_map/all_to_all | solution.py:554
  93.4 9.4 %collective-permute-start.21 = (bf16[128,1152]{1,0:T(8,128)(2,1)S(1)}, bf16[128,1152]{1,0:T(8,128)(2,1)S(1)}, u32[]{:S(2)}, u32[]{:S(2)}) collective-permute-start(bf16[128,1152]{1,0:T(8,128)(2,1)S(1)} %get-tuple-element.102), channel_id=1, source_target_pairs={{0,4},{1,5},{2,6},{3,7},{4,0},{5,1},{6,2},{7,3},{8,12},{9,13},{10,... | collective-permute-start | bytes 884744 | tf_op jit(solution)/shard_map/ppermute | solution.py:28
  96.2 10.1 %collective-permute-start.20 = (bf16[128,1152]{1,0:T(8,128)(2,1)S(1)}, bf16[128,1152]{1,0:T(8,128)(2,1)S(1)}, u32[]{:S(2)}, u32[]{:S(2)}) collective-permute-start(bf16[128,1152]{1,0:T(8,128)(2,1)S(1)} %get-tuple-element.99), channel_id=1, source_target_pairs={{0,3},{1,0},{2,1},{3,2},{4,7},{5,4},{6,5},{7,6},{8,11},{9,8},{10,9... | collective-permute-start | bytes 884744 | tf_op jit(solution)/shard_map/ppermute | solution.py:28
  102.9 10.4 %collective-permute-start.22 = (bf16[64,1152]{1,0:T(8,128)(2,1)S(1)}, bf16[64,1152]{1,0:T(8,128)(2,1)S(1)}, u32[]{:S(2)}, u32[]{:S(2)}) collective-permute-start(bf16[64,1152]{1,0:T(8,128)(2,1)S(1)} %get-tuple-element.103), channel_id=1, source_target_pairs={{0,2},{1,3},{2,0},{3,1},{4,6},{5,7},{6,4},{7,5},{8,10},{9,11},{10,... | collective-permute-start | bytes 442376 | tf_op jit(solution)/shard_map/ppermute | solution.py:28
  105.9 7.4 %collective-permute-start.23 = (bf16[64,1152]{1,0:T(8,128)(2,1)S(1)}, bf16[64,1152]{1,0:T(8,128)(2,1)S(1)}, u32[]{:S(2)}, u32[]{:S(2)}) collective-permute-start(bf16[64,1152]{1,0:T(8,128)(2,1)S(1)} %get-tuple-element.104), channel_id=1, source_target_pairs={{0,1},{1,2},{2,3},{3,0},{4,5},{5,6},{6,7},{7,4},{8,9},{9,10},{10,1... | collective-permute-start | bytes 442376 | tf_op jit(solution)/shard_map/ppermute | solution.py:28
  106.4 6.9 %collective-permute-start.24 = (bf16[64,1152]{1,0:T(8,128)(2,1)S(1)}, bf16[64,1152]{1,0:T(8,128)(2,1)S(1)}, u32[]{:S(2)}, u32[]{:S(2)}) collective-permute-start(bf16[64,1152]{1,0:T(8,128)(2,1)S(1)} %get-tuple-element.105), channel_id=1, source_target_pairs={{0,4},{1,5},{2,6},{3,7},{4,0},{5,1},{6,2},{7,3},{8,12},{9,13},{10,... | collective-permute-start | bytes 442376 | tf_op jit(solution)/shard_map/ppermute | solution.py:28
  109.3 3.3 %collective-permute-start.19 = (bf16[8,4,192]{2,1,0:T(4,128)(2,1)S(1)}, bf16[8,4,192]{2,1,0:T(4,128)(2,1)S(1)}, u32[]{:S(2)}, u32[]{:S(2)}) collective-permute-start(bf16[8,4,192]{2,1,0:T(4,128)(2,1)S(1)} %get-tuple-element.108), channel_id=1, source_target_pairs={{0,8},{8,0},{16,24},{24,16},{32,40},{40,32},{48,56},{56,48},{64,72... | collective-permute-start | bytes 36872 | tf_op jit(solution)/shard_map/ppermute | solution.py:28
where the time goes:
time: 115 us; the launch traced here: 114 us
  starting transfers between devices  46.5 us (40%)
  Pallas kernels  44.3 us (39%)
  waiting for transfers between devices  16.7 us (15%)
  local copies, waits for them, and re-layouts  2.7 us (2%)
  other arithmetic  2.43 us (2%)
  between operations  1.51 us (1%)
    ppermute x25, starting transfers between devices, permute(): lax.ppermute(x, axis, [(i, to(i)) for i in range(lax.axis_size(axis))])  42.8 us
    pallas_call x4, Pallas kernels, project(): pl.pallas_call(functools.partial(project_kernel, p), out_shape=(jax.Shape...  17.4 us
    ppermute x25, waiting for transfers between devices, permute(): lax.ppermute(x, axis, [(i, to(i)) for i in range(lax.axis_size(axis))])  16.7 us
    pallas_call x1, Pallas kernels, attend(): pl.pallas_call(functools.partial(attend_kernel, score_scale, blocks, toge...  10.7 us
    pallas_call x4, Pallas kernels, cache_terms(): pl.pallas_call(functools.partial(cache_kernel, part, d_lat), out_shape=[j...  9.64 us
    all_to_all x1, starting transfers between devices, per_device(): dq = lax.all_to_all(dq, 'ctx', 0, 0, axis_index_groups=z_groups)  3.68 us
  transfers between devices with their start and end apart: 26, of which 9 were waited for; matrix products, arithmetic and copies ran while one was open for 3% of the time, Pallas kernels for 25%

commit v1 on v0

--- a/solution.py
+++ b/solution.py
@@ -94,7 +94,7 @@
         out_shape=(packed, packed),
         in_specs=[smem, smem, vmem, vmem],
         out_specs=[vmem, vmem],
-        compiler_params=pltpu.CompilerParams(vmem_limit_bytes=63 * MIB),
+        compiler_params=pltpu.CompilerParams(vmem_limit_bytes=2 * MIB),
         cost_estimate=pl.CostEstimate(flops=0, bytes_accessed=32 * MIB, transcendentals=0),
     )(where, token_ratio, queries, out_grad)
 
@@ -475,13 +475,14 @@
     where = [core, ctx_index * p_dev, (ctx_index ^ 1) * p_dev, prompt_len[0]]
     where = where + [(z + k) & (nz - 1) for k in range(nz)] + [x_lo]
     where = jnp.stack(where).astype(jnp.int32)
+    mine, theirs = pack(where, token_ratio, queries, out_grad)
+    block = jnp.concatenate([mine, permute(theirs, "ctx", other_core)], 0)
+    block = in_order(block, permute(block, "ctx", other_x_lo), x_lo == 1, 0)
+    block, latent_cache = lax.optimization_barrier((block, latent_cache))
     own_t = latent_cache.T
     other_t = permute(latent_cache, "ctx", other_core).T
-    mine, theirs = pack(where, token_ratio, queries, out_grad)
     own_keys = stage(own_t)
     other_keys = stage(other_t)
-    block = jnp.concatenate([mine, permute(theirs, "ctx", other_core)], 0)
-    block = in_order(block, permute(block, "ctx", other_x_lo), x_lo == 1, 0)
     up = down = block
     ring = [block] + [None] * (nz - 1)
     for k in range(1, nz // 2 + 1):

time: 115 us -> 110 us (0.957)
  Pallas kernels: 44.3 us -> 36.9 us
  waiting for transfers between devices: 16.7 us -> 20 us
  local copies, waits for them, and re-layouts: 2.7 us -> 4.33 us
  other arithmetic: 2.43 us -> 0.88 us
    pallas_call x4, Pallas kernels: 17.4 us -> 12.3 us  [project(): pl.pallas_call(functools.partial(project_kernel, p), out_shape=(jax.Shape...]
    ppermute x25, waiting for transfers between devices: 16.7 us -> 20 us  [permute(): lax.ppermute(x, axis, [(i, to(i)) for i in range(lax.axis_size(axis))])]
    unnamed x11 -> x15, local copies, waits for them, and re-layouts: 1.92 us -> 4.04 us
    pallas_call x2, Pallas kernels: 2.26 us -> 0.79 us  [stage(): pl.pallas_call(stage_kernel, out_shape=jax.ShapeDtypeStruct((keys, c_widt...]
    ppermute x25, starting transfers between devices: 42.8 us -> 41.6 us  [permute(): lax.ppermute(x, axis, [(i, to(i)) for i in range(lax.axis_size(axis))])]
  transfers between devices with their start and end apart: 26 -> 26, of which waited for: 9 -> 9; matrix products, arithmetic and copies ran while one was open for 3% -> 2% of each run, Pallas kernels for 25% -> 19%
where the time goes in v1:
time: 110 us
  starting transfers between devices  45.9 us (42%)
  Pallas kernels  36.9 us (34%)
  waiting for transfers between devices  20 us (18%)
  local copies, waits for them, and re-layouts  4.33 us (4%)
  between operations  1.52 us (1%)
    ppermute x25, starting transfers between devices, permute(): lax.ppermute(x, axis, [(i, to(i)) for i in range(lax.axis_size(axis))])  41.6 us
    ppermute x25, waiting for transfers between devices, permute(): lax.ppermute(x, axis, [(i, to(i)) for i in range(lax.axis_size(axis))])  20 us
    pallas_call x4, Pallas kernels, project(): pl.pallas_call(functools.partial(project_kernel, p), out_shape=(jax.Shape...  12.3 us
    pallas_call x1, Pallas kernels, attend(): pl.pallas_call(functools.partial(attend_kernel, score_scale, blocks, toge...  10.7 us
    pallas_call x4, Pallas kernels, cache_terms(): pl.pallas_call(functools.partial(cache_kernel, part, d_lat), out_shape=[j...  9.64 us
    all_to_all x1, starting transfers between devices, per_device(): dq = lax.all_to_all(dq, 'ctx', 0, 0, axis_index_groups=z_groups)  4.27 us
    unnamed x15, local copies, waits for them, and re-layouts  4.04 us
  transfers between devices with their start and end apart: 26, of which 9 were waited for; matrix products, arithmetic and copies ran while one was open for 2% of the time, Pallas kernels for 19%

profile of v1, /device:TPU:1, one launch (start us, length us, event | category | flops | bytes accessed | tf_op | source)
XLA Modules:
  0.0 109.5 jit_solution(9665100595366497963)
XLA Ops:
  1.3 0.1 stack.93.where_ref
  1.4 0.0 copy-start.2
  1.4 0.8 copy-done.2
  2.1 0.7 copy-done.3
  2.9 0.7 copy-done.4
  3.5 0.6 shard_map.86
  4.1 3.3 %collective-permute-start = (bf16[32,384]{1,0:T(8,128)(2,1)S(1)}, bf16[32,384]{1,0:T(8,128)(2,1)S(1)}, u32[]{:S(2)}, u32[]{:S(2)}) collective-permute-start(bf16[32,384]{1,0:T(8,128)(2,1)S(1)} %get-tuple-element.57), channel_id=1, source_target_pairs={{0,8},{8,0},{16,24},{24,16},{32,40},{40,32},{48,56},{56,48},{64,72... | collective-permute-start | bytes 73736 | tf_op jit(solution)/shard_map/ppermute | solution.py:28
  7.4 0.8 collective-permute-done
  8.3 0.0 collective-permute-start.1
  8.3 2.9 %collective-permute-done.1 = bf16[64,384]{1,0:T(8,128)(2,1)S(1)} collective-permute-done((bf16[64,384]{1,0:T(8,128)(2,1)S(1)}, bf16[64,384]{1,0:T(8,128)(2,1)S(1)}, u32[]{:S(2)}, u32[]{:S(2)}) %collective-permute-start.1) | collective-permute-done | bytes 49184 | tf_op jit(solution)/shard_map/ppermute | solution.py:28
  11.3 1.6 %collective-permute-start.9 = (bf16[1024,576]{0,1:T(8,128)(2,1)}, bf16[1024,576]{0,1:T(8,128)(2,1)S(1)}, u32[]{:S(2)}, u32[]{:S(2)}) collective-permute-start(bf16[1024,576]{0,1:T(8,128)(2,1)} %param.10), channel_id=1, source_target_pairs={{0,8},{8,0},{16,24},{24,16},{32,40},{40,32},{48,56},{56,48},{64,72... | collective-permute-start | bytes 3538952 | tf_op jit(solution)/shard_map/ppermute | solution.py:28
  12.8 0.0 collective-permute-start.5
  12.8 3.8 %collective-permute-start.2 = (bf16[128,384]{1,0:T(8,128)(2,1)S(1)}, bf16[128,384]{1,0:T(8,128)(2,1)S(1)}, u32[]{:S(2)}, u32[]{:S(2)}) collective-permute-start(bf16[128,384]{1,0:T(8,128)(2,1)S(1)} %maximum_select_fusion.refs_0_), channel_id=1, source_target_pairs={{0,224},{8,232},{16,240},{24,248},{32,0},{40,8},{48,16},{56,24},{6... | collective-permute-start | bytes 294920 | tf_op jit(solution)/shard_map/ppermute | solution.py:28
  16.7 3.1 %collective-permute-done.5.refs_7_ = bf16[128,384]{1,0:T(8,128)(2,1)S(1)} collective-permute-done((bf16[128,384]{1,0:T(8,128)(2,1)S(1)}, bf16[128,384]{1,0:T(8,128)(2,1)S(1)}, u32[]{:S(2)}, u32[]{:S(2)}) %collective-permute-start.5) | collective-permute-done | bytes 98336 | tf_op jit(solution)/shard_map/ppermute | solution.py:28
  19.7 0.0 collective-permute-start.6
  19.8 2.7 %collective-permute-start.3 = (bf16[128,384]{1,0:T(8,128)(2,1)S(1)}, bf16[128,384]{1,0:T(8,128)(2,1)S(1)}, u32[]{:S(2)}, u32[]{:S(2)}) collective-permute-start(bf16[128,384]{1,0:T(8,128)(2,1)S(1)} %collective-permute-done.2.refs_1_), channel_id=1, source_target_pairs={{0,224},{8,232},{16,240},{24,248},{32,0},{40,8},{48,16},{56,24},{6... | collective-permute-start | bytes 294920 | tf_op jit(solution)/shard_map/ppermute | solution.py:28
  22.4 2.0 %collective-permute-done.6.refs_6_ = bf16[128,384]{1,0:T(8,128)(2,1)S(1)} collective-permute-done((bf16[128,384]{1,0:T(8,128)(2,1)S(1)}, bf16[128,384]{1,0:T(8,128)(2,1)S(1)}, u32[]{:S(2)}, u32[]{:S(2)}) %collective-permute-start.6) | collective-permute-done | bytes 98336 | tf_op jit(solution)/shard_map/ppermute | solution.py:28
  24.4 0.0 collective-permute-start.7
  24.4 2.7 %collective-permute-start.4 = (bf16[128,384]{1,0:T(8,128)(2,1)S(1)}, bf16[128,384]{1,0:T(8,128)(2,1)S(1)}, u32[]{:S(2)}, u32[]{:S(2)}) collective-permute-start(bf16[128,384]{1,0:T(8,128)(2,1)S(1)} %collective-permute-done.3.refs_2_), channel_id=1, source_target_pairs={{0,224},{8,232},{16,240},{24,248},{32,0},{40,8},{48,16},{56,24},{6... | collective-permute-start | bytes 294920 | tf_op jit(solution)/shard_map/ppermute | solution.py:28
  27.1 2.0 %collective-permute-done.7.refs_5_ = bf16[128,384]{1,0:T(8,128)(2,1)S(1)} collective-permute-done((bf16[128,384]{1,0:T(8,128)(2,1)S(1)}, bf16[128,384]{1,0:T(8,128)(2,1)S(1)}, u32[]{:S(2)}, u32[]{:S(2)}) %collective-permute-start.7) | collective-permute-done | bytes 98336 | tf_op jit(solution)/shard_map/ppermute | solution.py:28
  29.1 0.0 collective-permute-start.8
  29.1 0.1 stack.80.order_ref
  29.2 0.1 stack.77.order_ref
  29.3 1.3 %copy-done = bf16[1024,576]{0,1:T(8,128)(2,1)S(1)} copy-done((bf16[1024,576]{0,1:T(8,128)(2,1)S(1)}, bf16[1024,576]{0,1:T(8,128)(2,1)}, u32[]{:S(2)}) %copy-start) | copy-done | bytes 1179672
  30.6 0.4 shard_map.87.refs_9_
  31.0 0.4 shard_map.88.refs_10_
  31.4 0.0 copy-start.1
  31.4 0.0 collective-permute-done.4.refs_3_
  31.4 2.4 %collective-permute-done.8.refs_4_ = bf16[128,384]{1,0:T(8,128)(2,1)S(1)} collective-permute-done((bf16[128,384]{1,0:T(8,128)(2,1)S(1)}, bf16[128,384]{1,0:T(8,128)(2,1)S(1)}, u32[]{:S(2)}, u32[]{:S(2)}) %collective-permute-start.8) | collective-permute-done | bytes 98336 | tf_op jit(solution)/shard_map/ppermute | solution.py:28
  33.8 10.7 %shard_map.89 = (bf16[1024,576]{1,0:T(8,128)(2,1)S(1)}, bf16[1024,512]{1,0:T(8,128)(2,1)S(1)}, bf16[2048,1024]{1,0:T(8,128)(2,1)S(1)}, bf16[2048,1024]{1,0:T(8,1...) custom-call(s32[13]{0:T(128)S(1)} %stack.93.where_ref, ...), custom_call_target="tpu_custom_call" | custom-call | flops 4563402752 | bytes 8388608 | tf_op jit(solution)/shard_map/pallas_call | solution.py:203
  44.5 1.3 %collective-permute-start.10 = (f32[3,1024]{1,0:T(4,128)S(1)}, f32[3,1024]{1,0:T(4,128)S(1)}, u32[]{:S(2)}, u32[]{:S(2)}) collective-permute-start(f32[3,1024]{1,0:T(4,128)S(1)} %get-tuple-element.62.first_ref.refs_2_), channel_id=1, source_target_pairs={{0,16},{8,24},{16,0},{24,8},{32,48},{40,56},{48,32},{56,40},{64,80... | collective-permute-start | bytes 36872 | tf_op jit(solution)/shard_map/ppermute | solution.py:28
  45.8 3.1 %shard_map.90 = (f32[256,192]{1,0:T(8,128)S(1)}, f32[256,192]{1,0:T(8,128)S(1)}) custom-call(bf16[576,1024]{1,0:T(8,128)(2,1)S(1)} %bitcast.40, bf16[576,1024]{1,0:T(8,128)(2,1)S(1)} %bitcast.45, bf16[2048,1024]{1,0:T(8,128)(2,1)S(1)} %get-tuple-element.60.spread_ref, bf16[2048,1024]{1,0:T(8,128)(2,1)S(1)} %get-tuple-element.61.expo_ref, ...), custom_call_target="tpu_custom_call" | custom-call | flops 1207959552 | bytes 2097152 | tf_op jit(solution)/shard_map/pallas_call | solution.py:256
  49.0 0.1 collective-permute-start.11
  49.1 3.1 %shard_map.92 = (f32[256,192]{1,0:T(8,128)S(1)}, f32[256,192]{1,0:T(8,128)S(1)}) custom-call(bf16[576,1024]{1,0:T(8,128)(2,1)S(1)} %bitcast.41, bf16[576,1024]{1,0:T(8,128)(2,1)S(1)} %bitcast.46, bf16[2048,1024]{1,0:T(8,128)(2,1)S(1)} %get-tuple-element.60.spread_ref, bf16[2048,1024]{1,0:T(8,128)(2,1)S(1)} %get-tuple-element.61.expo_ref, ...), custom_call_target="tpu_custom_call" | custom-call | flops 1207959552 | bytes 2097152 | tf_op jit(solution)/shard_map/pallas_call | solution.py:256
  52.2 3.4 %collective-permute-start.12 = (f32[3,1024]{1,0:T(4,128)S(1)}, f32[3,1024]{1,0:T(4,128)S(1)}, u32[]{:S(2)}, u32[]{:S(2)}) collective-permute-start(f32[3,1024]{1,0:T(4,128)S(1)} %shard_map.93.first_ref), channel_id=1, source_target_pairs={{0,64},{8,72},{16,80},{24,88},{32,96},{40,104},{48,112},{56,120},{... | collective-permute-start | bytes 36872 | tf_op jit(solution)/shard_map/ppermute | solution.py:28
  55.6 3.1 %shard_map.94 = (f32[256,192]{1,0:T(8,128)S(1)}, f32[256,192]{1,0:T(8,128)S(1)}) custom-call(bf16[576,1024]{1,0:T(8,128)(2,1)S(1)} %bitcast.42, bf16[576,1024]{1,0:T(8,128)(2,1)S(1)} %bitcast.47, bf16[2048,1024]{1,0:T(8,128)(2,1)S(1)} %get-tuple-element.60.spread_ref, bf16[2048,1024]{1,0:T(8,128)(2,1)S(1)} %get-tuple-element.61.expo_ref, ...), custom_call_target="tpu_custom_call" | custom-call | flops 1207959552 | bytes 2097152 | tf_op jit(solution)/shard_map/pallas_call | solution.py:256
  58.7 0.0 copy-start.5
  58.7 1.9 %collective-permute-start.13 = (f32[3,1024]{1,0:T(4,128)S(1)}, f32[3,1024]{1,0:T(4,128)S(1)}, u32[]{:S(2)}, u32[]{:S(2)}) collective-permute-start(f32[3,1024]{1,0:T(4,128)S(1)} %shard_map.95.refs_0_), channel_id=1, source_target_pairs={{0,128},{8,136},{16,144},{24,152},{32,160},{40,168},{48,176},{56,1... | collective-permute-start | bytes 36872 | tf_op jit(solution)/shard_map/ppermute | solution.py:28
  60.6 3.1 %shard_map.96 = (f32[256,192]{1,0:T(8,128)S(1)}, f32[256,192]{1,0:T(8,128)S(1)}) custom-call(bf16[576,1024]{1,0:T(8,128)(2,1)S(1)} %bitcast.43, bf16[576,1024]{1,0:T(8,128)(2,1)S(1)} %bitcast.48, bf16[2048,1024]{1,0:T(8,128)(2,1)S(1)} %get-tuple-element.60.spread_ref, bf16[2048,1024]{1,0:T(8,128)(2,1)S(1)} %get-tuple-element.61.expo_ref, ...), custom_call_target="tpu_custom_call" | custom-call | flops 1207959552 | bytes 2097152 | tf_op jit(solution)/shard_map/pallas_call | solution.py:256
  63.7 1.9 %collective-permute-done.13.refs_1_ = f32[3,1024]{1,0:T(4,128)S(1)} collective-permute-done((f32[3,1024]{1,0:T(4,128)S(1)}, f32[3,1024]{1,0:T(4,128)S(1)}, u32[]{:S(2)}, u32[]{:S(2)}) %collective-permute-start.13) | collective-permute-done | bytes 12320 | tf_op jit(solution)/shard_map/ppermute | solution.py:28
  65.5 1.7 %shard_map.97 = (bf16[8,4,16,192]{3,2,1,0:T(8,128)(2,1)S(1)}, bf16[8,4,16,192]{3,2,1,0:T(8,128)(2,1)S(1)}, bf16[1024,576]{1,0:T(8,128)(2,1)S(1)}, bf16[1024,576]{1,0:T(8,128)(2,1)S(1)}) custom-call(s32[13]{0:T(128)S(1)} %stack.93.where_ref, s32[4]{0:T(128)S(1)} %copy-done.5, f32[3,1024]{1,0:T(4,128)S(1)} %shard_map.95.refs_0_, ...), custom_call_target="tpu_custom_call" | custom-call | flops 5898240 | bytes 4718592 | tf_op jit(solution)/shard_map/pallas_call | solution.py:346
  67.2 0.3 collective-permute-start.18
  67.6 2.4 %shard_map.98 = (bf16[128,1152]{1,0:T(8,128)(2,1)S(1)}, bf16[128,1152]{1,0:T(8,128)(2,1)S(1)}) custom-call(s32[8]{0:T(128)S(1)} %stack.80.order_ref, bf16[2,2,4,128,1024]{4,3,2,1,0:T(8,128)(2,1)S(1)} %bitcast.35, bf16[2,2,4,128,1024]{4,3,2,1,0:T(8,128)(2,1)S(1)} %bitcast.31, bf16[1024,576]{1,0:T(8,128)(2,1)S(1)} %get-tuple-element.87.with_spread_ref, ...), custom_call_target="tpu_custom_call" | custom-call | flops 1207959552 | bytes 2097152 | tf_op jit(solution)/shard_map/pallas_call | solution.py:386
  70.0 5.9 %collective-permute-start.14 = (bf16[128,1152]{1,0:T(8,128)(2,1)S(1)}, bf16[128,1152]{1,0:T(8,128)(2,1)S(1)}, u32[]{:S(2)}, u32[]{:S(2)}) collective-permute-start(bf16[128,1152]{1,0:T(8,128)(2,1)S(1)} %get-tuple-element.91), channel_id=1, source_target_pairs={{0,8},{8,0},{16,24},{24,16},{32,40},{40,32},{48,56},{56,48},{64,72... | collective-permute-start | bytes 884744 | tf_op jit(solution)/shard_map/ppermute | solution.py:28
  75.9 0.1 collective-permute-start.15
  76.0 2.4 %shard_map.100 = (bf16[128,1152]{1,0:T(8,128)(2,1)S(1)}, bf16[128,1152]{1,0:T(8,128)(2,1)S(1)}) custom-call(s32[8]{0:T(128)S(1)} %stack.77.order_ref, bf16[2,2,4,128,1024]{4,3,2,1,0:T(8,128)(2,1)S(1)} %bitcast.36, bf16[2,2,4,128,1024]{4,3,2,1,0:T(8,128)(2,1)S(1)} %bitcast.32, bf16[1024,576]{1,0:T(8,128)(2,1)S(1)} %get-tuple-element.87.with_spread_ref, ...), custom_call_target="tpu_custom_call" | custom-call | flops 1207959552 | bytes 2097152 | tf_op jit(solution)/shard_map/pallas_call | solution.py:386
  78.4 0.5 collective-permute-start.16
  78.9 0.1 collective-permute-start.17
  79.0 0.8 add_convert_fusion
  79.8 2.4 %shard_map.99 = (bf16[128,1152]{1,0:T(8,128)(2,1)S(1)}, f32[128,1152]{1,0:T(8,128)S(1)}) custom-call(s32[8]{0:T(128)S(1)} %stack.80.order_ref, bf16[2,2,4,128,1024]{4,3,2,1,0:T(8,128)(2,1)S(1)} %bitcast.37, bf16[2,2,4,128,1024]{4,3,2,1,0:T(8,128)(2,1)S(1)} %bitcast.33, bf16[1024,576]{1,0:T(8,128)(2,1)S(1)} %get-tuple-element.87.with_spread_ref, ...), custom_call_target="tpu_custom_call" | custom-call | flops 1207959552 | bytes 2097152 | tf_op jit(solution)/shard_map/pallas_call | solution.py:386
  82.2 2.4 %shard_map.101 = (bf16[128,1152]{1,0:T(8,128)(2,1)S(1)}, f32[128,1152]{1,0:T(8,128)S(1)}) custom-call(s32[8]{0:T(128)S(1)} %stack.77.order_ref, bf16[2,2,4,128,1024]{4,3,2,1,0:T(8,128)(2,1)S(1)} %bitcast.38, bf16[2,2,4,128,1024]{4,3,2,1,0:T(8,128)(2,1)S(1)} %bitcast.34, bf16[1024,576]{1,0:T(8,128)(2,1)S(1)} %get-tuple-element.87.with_spread_ref, ...), custom_call_target="tpu_custom_call" | custom-call | flops 1207959552 | bytes 2097152 | tf_op jit(solution)/shard_map/pallas_call | solution.py:386
  84.6 4.3 %all-to-all-start = ((bf16[8,4,16,192]{3,2,1,0:T(8,128)(2,1)}), bf16[8,4,16,192]{3,2,1,0:T(8,128)(2,1)S(1)}, u32[]{:S(2)}, u32[]{:S(2)}) async-start(bf16[8,4,16,192]{3,2,1,0:T(8,128)(2,1)} %add_convert_fusion), calls=%async_computation | async-start | bytes 524288 | tf_op jit(solution)/shard_map/all_to_all | solution.py:555
  88.9 2.6 %collective-permute-start.21 = (bf16[128,1152]{1,0:T(8,128)(2,1)S(1)}, bf16[128,1152]{1,0:T(8,128)(2,1)S(1)}, u32[]{:S(2)}, u32[]{:S(2)}) collective-permute-start(bf16[128,1152]{1,0:T(8,128)(2,1)S(1)} %get-tuple-element.106), channel_id=1, source_target_pairs={{0,4},{1,5},{2,6},{3,7},{4,0},{5,1},{6,2},{7,3},{8,12},{9,13},{10,... | collective-permute-start | bytes 884744 | tf_op jit(solution)/shard_map/ppermute | solution.py:28
  91.6 2.7 %collective-permute-start.20 = (bf16[128,1152]{1,0:T(8,128)(2,1)S(1)}, bf16[128,1152]{1,0:T(8,128)(2,1)S(1)}, u32[]{:S(2)}, u32[]{:S(2)}) collective-permute-start(bf16[128,1152]{1,0:T(8,128)(2,1)S(1)} %get-tuple-element.103), channel_id=1, source_target_pairs={{0,3},{1,0},{2,1},{3,2},{4,7},{5,4},{6,5},{7,6},{8,11},{9,8},{10,9... | collective-permute-start | bytes 884744 | tf_op jit(solution)/shard_map/ppermute | solution.py:28
  94.3 4.0 %collective-permute-done.21.arrived_ref = bf16[128,1152]{1,0:T(8,128)(2,1)S(1)} collective-permute-done((bf16[128,1152]{1,0:T(8,128)(2,1)S(1)}, bf16[128,1152]{1,0:T(8,128)(2,1)S(1)}, u32[]{:S(2)}, u32[]{:S(2)}) %collective-permute-start.21) | collective-permute-done | bytes 294944 | tf_op jit(solution)/shard_map/ppermute | solution.py:28
  98.3 0.1 shard_map.103
  98.4 3.0 %collective-permute-start.22 = (bf16[64,1152]{1,0:T(8,128)(2,1)S(1)}, bf16[64,1152]{1,0:T(8,128)(2,1)S(1)}, u32[]{:S(2)}, u32[]{:S(2)}) collective-permute-start(bf16[64,1152]{1,0:T(8,128)(2,1)S(1)} %get-tuple-element.107), channel_id=1, source_target_pairs={{0,2},{1,3},{2,0},{3,1},{4,6},{5,7},{6,4},{7,5},{8,10},{9,11},{10,... | collective-permute-start | bytes 442376 | tf_op jit(solution)/shard_map/ppermute | solution.py:28
  101.4 0.4 collective-permute-start.23
  101.8 0.1 shard_map.102
  101.9 2.7 %collective-permute-start.24 = (bf16[64,1152]{1,0:T(8,128)(2,1)S(1)}, bf16[64,1152]{1,0:T(8,128)(2,1)S(1)}, u32[]{:S(2)}, u32[]{:S(2)}) collective-permute-start(bf16[64,1152]{1,0:T(8,128)(2,1)S(1)} %get-tuple-element.109), channel_id=1, source_target_pairs={{0,4},{1,5},{2,6},{3,7},{4,0},{5,1},{6,2},{7,3},{8,12},{9,13},{10,... | collective-permute-start | bytes 442376 | tf_op jit(solution)/shard_map/ppermute | solution.py:28
  104.7 2.5 %collective-permute-start.19 = (bf16[8,4,192]{2,1,0:T(4,128)(2,1)S(1)}, bf16[8,4,192]{2,1,0:T(4,128)(2,1)S(1)}, u32[]{:S(2)}, u32[]{:S(2)}) collective-permute-start(bf16[8,4,192]{2,1,0:T(4,128)(2,1)S(1)} %get-tuple-element.112), channel_id=1, source_target_pairs={{0,8},{8,0},{16,24},{24,16},{32,40},{40,32},{48,56},{56,48},{64,72... | collective-permute-start | bytes 36872 | tf_op jit(solution)/shard_map/ppermute | solution.py:28
  107.2 0.8 collective-permute-done.19
  108.1 0.6 copy.10
  108.7 0.8 shard_map.104
  (32 shorter events, 0.3 us)
Async XLA Ops:
  1.4 0.8 copy-start.2
  2.1 0.7 copy-start.3
  2.9 0.7 copy-start.4
  4.1 4.1 %collective-permute-start = (bf16[32,384]{1,0:T(8,128)(2,1)S(1)}, bf16[32,384]{1,0:T(8,128)(2,1)S(1)}, u32[]{:S(2)}, u32[]{:S(2)}) collective-permute-start(bf16[32,384]{1,0:T(8,128)(2,1)S(1)} %get-tuple-element.57), channel_id=1, source_target_pairs={{0,8},{8,0},{16,24},{24,16},{32,40},{40,32},{48,56},{56,48},{64,72... | collective-permute-start | bytes 73736 | tf_op jit(solution)/shard_map/ppermute | solution.py:28
  8.3 2.9 %collective-permute-start.1 = (bf16[64,384]{1,0:T(8,128)(2,1)S(1)}, bf16[64,384]{1,0:T(8,128)(2,1)S(1)}, u32[]{:S(2)}, u32[]{:S(2)}) collective-permute-start(bf16[64,384]{1,0:T(8,128)(2,1)S(1)} %pad_maximum_fusion), channel_id=1, source_target_pairs={{0,16},{8,24},{16,0},{24,8},{32,48},{40,56},{48,32},{56,40},{64,80... | collective-permute-start | bytes 147464 | tf_op jit(solution)/shard_map/ppermute | solution.py:28
  11.3 19.7 %collective-permute-start.9 = (bf16[1024,576]{0,1:T(8,128)(2,1)}, bf16[1024,576]{0,1:T(8,128)(2,1)S(1)}, u32[]{:S(2)}, u32[]{:S(2)}) collective-permute-start(bf16[1024,576]{0,1:T(8,128)(2,1)} %param.10), channel_id=1, source_target_pairs={{0,8},{8,0},{16,24},{24,16},{32,40},{40,32},{48,56},{56,48},{64,72... | collective-permute-start | bytes 3538952 | tf_op jit(solution)/shard_map/ppermute | solution.py:28
  12.8 6.9 %collective-permute-start.5 = (bf16[128,384]{1,0:T(8,128)(2,1)S(1)}, bf16[128,384]{1,0:T(8,128)(2,1)S(1)}, u32[]{:S(2)}, u32[]{:S(2)}) collective-permute-start(bf16[128,384]{1,0:T(8,128)(2,1)S(1)} %maximum_select_fusion.refs_0_), channel_id=1, source_target_pairs={{0,32},{8,40},{16,48},{24,56},{32,64},{40,72},{48,80},{56,88},{64,... | collective-permute-start | bytes 294920 | tf_op jit(solution)/shard_map/ppermute | solution.py:28
  12.8 6.9 %collective-permute-start.2 = (bf16[128,384]{1,0:T(8,128)(2,1)S(1)}, bf16[128,384]{1,0:T(8,128)(2,1)S(1)}, u32[]{:S(2)}, u32[]{:S(2)}) collective-permute-start(bf16[128,384]{1,0:T(8,128)(2,1)S(1)} %maximum_select_fusion.refs_0_), channel_id=1, source_target_pairs={{0,224},{8,232},{16,240},{24,248},{32,0},{40,8},{48,16},{56,24},{6... | collective-permute-start | bytes 294920 | tf_op jit(solution)/shard_map/ppermute | solution.py:28
  19.7 4.7 %collective-permute-start.6 = (bf16[128,384]{1,0:T(8,128)(2,1)S(1)}, bf16[128,384]{1,0:T(8,128)(2,1)S(1)}, u32[]{:S(2)}, u32[]{:S(2)}) collective-permute-start(bf16[128,384]{1,0:T(8,128)(2,1)S(1)} %collective-permute-done.5.refs_7_), channel_id=1, source_target_pairs={{0,32},{8,40},{16,48},{24,56},{32,64},{40,72},{48,80},{56,88},{64,... | collective-permute-start | bytes 294920 | tf_op jit(solution)/shard_map/ppermute | solution.py:28
  19.8 4.7 %collective-permute-start.3 = (bf16[128,384]{1,0:T(8,128)(2,1)S(1)}, bf16[128,384]{1,0:T(8,128)(2,1)S(1)}, u32[]{:S(2)}, u32[]{:S(2)}) collective-permute-start(bf16[128,384]{1,0:T(8,128)(2,1)S(1)} %collective-permute-done.2.refs_1_), channel_id=1, source_target_pairs={{0,224},{8,232},{16,240},{24,248},{32,0},{40,8},{48,16},{56,24},{6... | collective-permute-start | bytes 294920 | tf_op jit(solution)/shard_map/ppermute | solution.py:28
  24.4 4.7 %collective-permute-start.7 = (bf16[128,384]{1,0:T(8,128)(2,1)S(1)}, bf16[128,384]{1,0:T(8,128)(2,1)S(1)}, u32[]{:S(2)}, u32[]{:S(2)}) collective-permute-start(bf16[128,384]{1,0:T(8,128)(2,1)S(1)} %collective-permute-done.6.refs_6_), channel_id=1, source_target_pairs={{0,32},{8,40},{16,48},{24,56},{32,64},{40,72},{48,80},{56,88},{64,... | collective-permute-start | bytes 294920 | tf_op jit(solution)/shard_map/ppermute | solution.py:28
  24.4 7.0 %collective-permute-start.4 = (bf16[128,384]{1,0:T(8,128)(2,1)S(1)}, bf16[128,384]{1,0:T(8,128)(2,1)S(1)}, u32[]{:S(2)}, u32[]{:S(2)}) collective-permute-start(bf16[128,384]{1,0:T(8,128)(2,1)S(1)} %collective-permute-done.3.refs_2_), channel_id=1, source_target_pairs={{0,224},{8,232},{16,240},{24,248},{32,0},{40,8},{48,16},{56,24},{6... | collective-permute-start | bytes 294920 | tf_op jit(solution)/shard_map/ppermute | solution.py:28
  29.1 4.7 %collective-permute-start.8 = (bf16[128,384]{1,0:T(8,128)(2,1)S(1)}, bf16[128,384]{1,0:T(8,128)(2,1)S(1)}, u32[]{:S(2)}, u32[]{:S(2)}) collective-permute-start(bf16[128,384]{1,0:T(8,128)(2,1)S(1)} %collective-permute-done.7.refs_5_), channel_id=1, source_target_pairs={{0,32},{8,40},{16,48},{24,56},{32,64},{40,72},{48,80},{56,88},{64,... | collective-permute-start | bytes 294920 | tf_op jit(solution)/shard_map/ppermute | solution.py:28
  29.3 1.3 %copy-start = (bf16[1024,576]{0,1:T(8,128)(2,1)S(1)}, bf16[1024,576]{0,1:T(8,128)(2,1)}, u32[]{:S(2)}) copy-start(bf16[1024,576]{0,1:T(8,128)(2,1)} %param.10) | copy-start | bytes 3538948
  30.6 3.2 %copy-start.6 = (bf16[16,512,256]{2,1,0:T(8,128)(2,1)S(1)}, bf16[16,512,256]{2,1,0:T(8,128)(2,1)}, u32[]{:S(2)}) copy-start(bf16[16,512,256]{2,1,0:T(8,128)(2,1)} %refs_8_.1) | copy-start | bytes 12582916
  31.4 14.5 %copy-start.1 = (bf16[1024,576]{0,1:T(8,128)(2,1)S(1)}, bf16[1024,576]{0,1:T(8,128)(2,1)}, u32[]{:S(2)}) copy-start(bf16[1024,576]{0,1:T(8,128)(2,1)} %param.10) | copy-start | bytes 3538948
  44.5 4.4 %collective-permute-start.10 = (f32[3,1024]{1,0:T(4,128)S(1)}, f32[3,1024]{1,0:T(4,128)S(1)}, u32[]{:S(2)}, u32[]{:S(2)}) collective-permute-start(f32[3,1024]{1,0:T(4,128)S(1)} %get-tuple-element.62.first_ref.refs_2_), channel_id=1, source_target_pairs={{0,16},{8,24},{16,0},{24,8},{32,48},{40,56},{48,32},{56,40},{64,80... | collective-permute-start | bytes 36872 | tf_op jit(solution)/shard_map/ppermute | solution.py:28
  49.0 3.2 %collective-permute-start.11 = (f32[3,1024]{1,0:T(4,128)S(1)}, f32[3,1024]{1,0:T(4,128)S(1)}, u32[]{:S(2)}, u32[]{:S(2)}) collective-permute-start(f32[3,1024]{1,0:T(4,128)S(1)} %shard_map.91.first_ref), channel_id=1, source_target_pairs={{0,32},{8,40},{16,48},{24,56},{32,0},{40,8},{48,16},{56,24},{64,96... | collective-permute-start | bytes 36872 | tf_op jit(solution)/shard_map/ppermute | solution.py:28
  52.2 6.5 %collective-permute-start.12 = (f32[3,1024]{1,0:T(4,128)S(1)}, f32[3,1024]{1,0:T(4,128)S(1)}, u32[]{:S(2)}, u32[]{:S(2)}) collective-permute-start(f32[3,1024]{1,0:T(4,128)S(1)} %shard_map.93.first_ref), channel_id=1, source_target_pairs={{0,64},{8,72},{16,80},{24,88},{32,96},{40,104},{48,112},{56,120},{... | collective-permute-start | bytes 36872 | tf_op jit(solution)/shard_map/ppermute | solution.py:28
  58.7 6.8 %copy-start.5 = (s32[4]{0:T(128)S(1)}, s32[4]{0:T(128)}, u32[]{:S(2)}) copy-start(s32[4]{0:T(128)} %lens_ref.1) | copy-start | bytes 52
  58.7 6.8 %collective-permute-start.13 = (f32[3,1024]{1,0:T(4,128)S(1)}, f32[3,1024]{1,0:T(4,128)S(1)}, u32[]{:S(2)}, u32[]{:S(2)}) collective-permute-start(f32[3,1024]{1,0:T(4,128)S(1)} %shard_map.95.refs_0_), channel_id=1, source_target_pairs={{0,128},{8,136},{16,144},{24,152},{32,160},{40,168},{48,176},{56,1... | collective-permute-start | bytes 36872 | tf_op jit(solution)/shard_map/ppermute | solution.py:28
  67.2 11.8 %collective-permute-start.18 = (bf16[8,4,16,192]{3,2,1,0:T(8,128)(2,1)S(1)}, bf16[8,4,16,192]{3,2,1,0:T(8,128)(2,1)S(1)}, u32[]{:S(2)}, u32[]{:S(2)}) collective-permute-start(bf16[8,4,16,192]{3,2,1,0:T(8,128)(2,1)S(1)} %get-tuple-element.100), channel_id=1, source_target_pairs={{0,16},{8,24},{16,0},{24,8},{32,48},{40,56},{48,32},{56,40},{64,80... | collective-permute-start | bytes 589832 | tf_op jit(solution)/shard_map/ppermute | solution.py:28
  70.0 9.8 %collective-permute-start.14 = (bf16[128,1152]{1,0:T(8,128)(2,1)S(1)}, bf16[128,1152]{1,0:T(8,128)(2,1)S(1)}, u32[]{:S(2)}, u32[]{:S(2)}) collective-permute-start(bf16[128,1152]{1,0:T(8,128)(2,1)S(1)} %get-tuple-element.91), channel_id=1, source_target_pairs={{0,8},{8,0},{16,24},{24,16},{32,40},{40,32},{48,56},{56,48},{64,72... | collective-permute-start | bytes 884744 | tf_op jit(solution)/shard_map/ppermute | solution.py:28
  75.9 3.9 %collective-permute-start.15 = (bf16[128,1152]{1,0:T(8,128)(2,1)S(1)}, bf16[128,1152]{1,0:T(8,128)(2,1)S(1)}, u32[]{:S(2)}, u32[]{:S(2)}) collective-permute-start(bf16[128,1152]{1,0:T(8,128)(2,1)S(1)} %get-tuple-element.92), channel_id=1, source_target_pairs={{0,8},{8,0},{16,24},{24,16},{32,40},{40,32},{48,56},{56,48},{64,72... | collective-permute-start | bytes 884744 | tf_op jit(solution)/shard_map/ppermute | solution.py:28
  78.4 3.8 %collective-permute-start.16 = (bf16[128,1152]{1,0:T(8,128)(2,1)S(1)}, bf16[128,1152]{1,0:T(8,128)(2,1)S(1)}, u32[]{:S(2)}, u32[]{:S(2)}) collective-permute-start(bf16[128,1152]{1,0:T(8,128)(2,1)S(1)} %get-tuple-element.96), channel_id=1, source_target_pairs={{0,8},{8,0},{16,24},{24,16},{32,40},{40,32},{48,56},{56,48},{64,72... | collective-permute-start | bytes 884744 | tf_op jit(solution)/shard_map/ppermute | solution.py:28
  78.9 3.3 %collective-permute-start.17 = (bf16[128,1152]{1,0:T(8,128)(2,1)S(1)}, bf16[128,1152]{1,0:T(8,128)(2,1)S(1)}, u32[]{:S(2)}, u32[]{:S(2)}) collective-permute-start(bf16[128,1152]{1,0:T(8,128)(2,1)S(1)} %get-tuple-element.97), channel_id=1, source_target_pairs={{0,8},{8,0},{16,24},{24,16},{32,40},{40,32},{48,56},{56,48},{64,72... | collective-permute-start | bytes 884744 | tf_op jit(solution)/shard_map/ppermute | solution.py:28
  84.6 19.9 %all-to-all-start = ((bf16[8,4,16,192]{3,2,1,0:T(8,128)(2,1)}), bf16[8,4,16,192]{3,2,1,0:T(8,128)(2,1)S(1)}, u32[]{:S(2)}, u32[]{:S(2)}) async-start(bf16[8,4,16,192]{3,2,1,0:T(8,128)(2,1)} %add_convert_fusion), calls=%async_computation | async-start | bytes 524288 | tf_op jit(solution)/shard_map/all_to_all | solution.py:555
  88.9 9.4 %collective-permute-start.21 = (bf16[128,1152]{1,0:T(8,128)(2,1)S(1)}, bf16[128,1152]{1,0:T(8,128)(2,1)S(1)}, u32[]{:S(2)}, u32[]{:S(2)}) collective-permute-start(bf16[128,1152]{1,0:T(8,128)(2,1)S(1)} %get-tuple-element.106), channel_id=1, source_target_pairs={{0,4},{1,5},{2,6},{3,7},{4,0},{5,1},{6,2},{7,3},{8,12},{9,13},{10,... | collective-permute-start | bytes 884744 | tf_op jit(solution)/shard_map/ppermute | solution.py:28
  91.6 10.2 %collective-permute-start.20 = (bf16[128,1152]{1,0:T(8,128)(2,1)S(1)}, bf16[128,1152]{1,0:T(8,128)(2,1)S(1)}, u32[]{:S(2)}, u32[]{:S(2)}) collective-permute-start(bf16[128,1152]{1,0:T(8,128)(2,1)S(1)} %get-tuple-element.103), channel_id=1, source_target_pairs={{0,3},{1,0},{2,1},{3,2},{4,7},{5,4},{6,5},{7,6},{8,11},{9,8},{10,9... | collective-permute-start | bytes 884744 | tf_op jit(solution)/shard_map/ppermute | solution.py:28
  98.4 10.2 %collective-permute-start.22 = (bf16[64,1152]{1,0:T(8,128)(2,1)S(1)}, bf16[64,1152]{1,0:T(8,128)(2,1)S(1)}, u32[]{:S(2)}, u32[]{:S(2)}) collective-permute-start(bf16[64,1152]{1,0:T(8,128)(2,1)S(1)} %get-tuple-element.107), channel_id=1, source_target_pairs={{0,2},{1,3},{2,0},{3,1},{4,6},{5,7},{6,4},{7,5},{8,10},{9,11},{10,... | collective-permute-start | bytes 442376 | tf_op jit(solution)/shard_map/ppermute | solution.py:28
  101.4 7.3 %collective-permute-start.23 = (bf16[64,1152]{1,0:T(8,128)(2,1)S(1)}, bf16[64,1152]{1,0:T(8,128)(2,1)S(1)}, u32[]{:S(2)}, u32[]{:S(2)}) collective-permute-start(bf16[64,1152]{1,0:T(8,128)(2,1)S(1)} %get-tuple-element.108), channel_id=1, source_target_pairs={{0,1},{1,2},{2,3},{3,0},{4,5},{5,6},{6,7},{7,4},{8,9},{9,10},{10,1... | collective-permute-start | bytes 442376 | tf_op jit(solution)/shard_map/ppermute | solution.py:28
  101.9 6.8 %collective-permute-start.24 = (bf16[64,1152]{1,0:T(8,128)(2,1)S(1)}, bf16[64,1152]{1,0:T(8,128)(2,1)S(1)}, u32[]{:S(2)}, u32[]{:S(2)}) collective-permute-start(bf16[64,1152]{1,0:T(8,128)(2,1)S(1)} %get-tuple-element.109), channel_id=1, source_target_pairs={{0,4},{1,5},{2,6},{3,7},{4,0},{5,1},{6,2},{7,3},{8,12},{9,13},{10,... | collective-permute-start | bytes 442376 | tf_op jit(solution)/shard_map/ppermute | solution.py:28
  104.7 3.3 %collective-permute-start.19 = (bf16[8,4,192]{2,1,0:T(4,128)(2,1)S(1)}, bf16[8,4,192]{2,1,0:T(4,128)(2,1)S(1)}, u32[]{:S(2)}, u32[]{:S(2)}) collective-permute-start(bf16[8,4,192]{2,1,0:T(4,128)(2,1)S(1)} %get-tuple-element.112), channel_id=1, source_target_pairs={{0,8},{8,0},{16,24},{24,16},{32,40},{40,32},{48,56},{56,48},{64,72... | collective-permute-start | bytes 36872 | tf_op jit(solution)/shard_map/ppermute | solution.py:28

commit v2 on v1

--- a/solution.py
+++ b/solution.py
@@ -19,7 +19,7 @@
 PACKED = 384
 MIB = 1024 * 1024
 ATTEND_MIB = 24
-PROJECT_MIB = 8
+PROJECT_MIB = 10
 WEIGH_MIB = 16
 CACHE_MIB = 20
 
@@ -42,19 +42,19 @@
     return jnp.where(lax.broadcasted_iota(jnp.int32, both.shape, 0) == 0, top, both)
 
 
-def join_kernel(first_ref, second_ref, out_ref):
-    out_ref[...] = join_stats(first_ref[...], second_ref[...])
-
-
-def join(first, second):
+def join_kernel(*refs):
+    refs[-1][...] = functools.reduce(join_stats, [ref[...] for ref in refs[:-1]])
+
+
+def join(*parts):
     vmem = pl.BlockSpec(memory_space=pltpu.VMEM)
     return pl.pallas_call(
         join_kernel,
-        out_shape=jax.ShapeDtypeStruct(first.shape, F32),
-        in_specs=[vmem, vmem],
+        out_shape=jax.ShapeDtypeStruct(parts[0].shape, F32),
+        in_specs=[vmem] * len(parts),
         out_specs=vmem,
         compiler_params=pltpu.CompilerParams(vmem_limit_bytes=MIB),
-    )(first, second)
+    )(*parts)
 
 
 def against(x, y):
@@ -99,23 +99,31 @@
     )(where, token_ratio, queries, out_grad)
 
 
-def stage_kernel(cache_ref, out_ref):
-    out_ref[...] = cache_ref[...].T
-
-
-def stage(cache_t):
+def stage_kernel(cache_ref, *refs):
+    refs[-1][...] = cache_ref[...].T
+    if len(refs) == 3:
+        own_ref, both_ref = refs[:2]
+        keys = own_ref.shape[1]
+        both_ref[:, :keys] = own_ref[...]
+        both_ref[:, keys:] = cache_ref[...]
+
+
+def stage(cache_t, own_t=None):
     c_width, keys = cache_t.shape
     vmem = pl.BlockSpec(memory_space=pltpu.VMEM)
+    turned = jax.ShapeDtypeStruct((keys, c_width), BF16)
+    both = jax.ShapeDtypeStruct((c_width, 2 * keys), BF16)
+    operands, outs = ((cache_t,), (turned,)) if own_t is None else ((cache_t, own_t), (both, turned))
     return pl.pallas_call(
         stage_kernel,
-        out_shape=jax.ShapeDtypeStruct((keys, c_width), BF16),
-        in_specs=[vmem],
-        out_specs=vmem,
-        compiler_params=pltpu.CompilerParams(vmem_limit_bytes=6 * MIB),
+        out_shape=outs,
+        in_specs=[vmem] * len(operands),
+        out_specs=[vmem] * len(outs),
+        compiler_params=pltpu.CompilerParams(vmem_limit_bytes=10 * MIB),
         cost_estimate=pl.CostEstimate(
             flops=keys * c_width, bytes_accessed=4 * keys * c_width, transcendentals=0
         ),
-    )(cache_t)
+    )(*operands)
 
 
 def attend_kernel(score_scale, blocks, together, where_ref, *refs):
@@ -227,42 +235,29 @@
     )(where, *ring, kv_up, own, other)
 
 
-def project_kernel(p, own_ref, other_ref, spread_ref, expo_ref, key_ref, *out_refs):
-    d_lat, d_nope = key_ref.shape[1:]
-    keys = own_ref.shape[1]
-    width = out_refs[0].shape[0]
-    rows = spread_ref.shape[1] // key_ref.shape[0]
+def project_kernel(p, cache_ref, spread_ref, expo_ref, *out_refs):
+    width = out_refs[0].shape[1]
     columns = slice(p * width, (p + 1) * width)
     for terms_ref, out_ref in zip((spread_ref, expo_ref), out_refs):
-        full = jnp.dot(own_ref[...], terms_ref[:keys, columns], preferred_element_type=F32)
-        full = full + jnp.dot(
-            other_ref[...], terms_ref[keys:, columns], preferred_element_type=F32
+        out_ref[...] = jnp.dot(
+            cache_ref[...], terms_ref[:, columns], preferred_element_type=F32
         )
-        for j in range(width // rows):
-            at = slice(j * rows, (j + 1) * rows)
-            out_ref[at, :d_nope] = lax.dot_general(
-                full[:d_lat, at].astype(BF16),
-                key_ref[p * (width // rows) + j],
-                (((0,), (0,)), ((), ())),
-                preferred_element_type=F32,
-            )
-            out_ref[at, d_nope:] = full[d_lat:, at].T
-
-
-def project(p, own_t, other_t, spread, expo, w_key, q_width):
-    c_width, keys = own_t.shape
-    width = 2 * spread.shape[1] // w_key.shape[0]
+
+
+def project(p, parts, cache_t, spread, expo):
+    c_width, keys = cache_t.shape
+    width = spread.shape[1] // parts
     vmem = pl.BlockSpec(memory_space=pltpu.VMEM)
     return pl.pallas_call(
         functools.partial(project_kernel, p),
-        out_shape=(jax.ShapeDtypeStruct((width, q_width), F32),) * 2,
-        in_specs=[vmem] * 5,
+        out_shape=(jax.ShapeDtypeStruct((c_width, width), F32),) * 2,
+        in_specs=[vmem] * 3,
         out_specs=[vmem] * 2,
         compiler_params=pltpu.CompilerParams(vmem_limit_bytes=PROJECT_MIB * MIB),
         cost_estimate=pl.CostEstimate(
-            flops=8 * keys * width * c_width, bytes_accessed=8 * keys * width, transcendentals=0
+            flops=4 * keys * width * c_width, bytes_accessed=4 * keys * width, transcendentals=0
         ),
-    )(own_t, other_t, spread, expo, w_key)
+    )(cache_t, spread, expo)
 
 
 def row_gains(where_ref, lens_ref, ratio_ref, rows_of_core):
@@ -289,70 +284,107 @@
     return gains
 
 
+def row_factors(joined_refs, own_ref):
+    joined = functools.reduce(join_stats, [ref[...] for ref in joined_refs])
+    centre = own_ref[2:3] / jnp.maximum(own_ref[1:2], 1e-30)
+    factor = jnp.exp2(own_ref[0:1] - joined[0:1]) / joined[1:2]
+    return factor, joined[2:3] / joined[1:2] - centre
+
+
 def weigh_kernel(scale, rows_of_core, where_ref, lens_ref, *refs):
-    (joined_ref, last_ref, own_ref, ratio_ref, query_ref, grad_ref) = refs[:6]
-    by_spread_refs, by_expo_refs = refs[6:-4:2], refs[7:-4:2]
-    dq_keep_ref, dq_send_ref, with_spread_ref, with_expo_ref = refs[-4:]
+    joined_refs, (own_ref, ratio_ref, query_ref, grad_ref) = refs[:4], refs[4:8]
+    with_spread_ref, with_expo_ref, factors_ref = refs[8:]
     total = query_ref.shape[0]
     d_lat = grad_ref.shape[1]
     rows = ratio_ref.shape[0]
-    half = total // rows
     gains = row_gains(where_ref, lens_ref, ratio_ref, rows_of_core)
-    joined = join_stats(joined_ref[...], last_ref[...])
-    centre = own_ref[2:3] / jnp.maximum(own_ref[1:2], 1e-30)
-    factor = jnp.exp2(own_ref[0:1] - joined[0:1]) / joined[1:2]
-    shift = joined[2:3] / joined[1:2] - centre
+    factor, shift = row_factors(joined_refs, own_ref)
+    gains_row = jnp.broadcast_to(gains, (rows, 128)).T[0:1]
+    gains_row = jnp.concatenate([gains_row] * (total // rows), axis=1)
+    factors_ref[0:1] = scale * gains_row * factor
+    factors_ref[1:2] = shift
     sublane = lax.broadcasted_iota(jnp.int32, (8, total), 0)
     both = jnp.where(sublane == 0, factor, shift).T
-    blocks, size = dq_keep_ref.shape[0], dq_keep_ref.shape[2] // 2
-    second = where_ref[4 + blocks] == 1
-    for h in range(half):
+    for h in range(total // rows):
         at = slice(h * rows, (h + 1) * rows)
-        part = slice((h % 2) * rows, (h % 2 + 1) * rows)
         factor = both[at, 0:1] * gains
-        shift = both[at, 1:2]
-        scaled = scale * factor
-        dq = by_spread_refs[h // 2][part, :] - shift * by_expo_refs[h // 2][part, :]
-        dq = scaled * dq
-        if h % 2:
-            for b in range(blocks):
-                pieces = []
-                for x in range(2):
-                    first = (2 * b + x) * size
-                    at_x = slice(first, first + size)
-                    pieces.append(jnp.concatenate([before[at_x], dq[at_x]], axis=0))
-                dq_keep_ref[b, h // 2] = jnp.where(second, pieces[1], pieces[0]).astype(BF16)
-                dq_send_ref[b, h // 2] = jnp.where(second, pieces[0], pieces[1]).astype(BF16)
-        before = dq
-        query = scaled * query_ref[at, :].astype(F32)
+        query = scale * factor * query_ref[at, :].astype(F32)
         with_spread_ref[at, :] = query.astype(BF16)
-        moved = shift * query
+        moved = both[at, 1:2] * query
         with_expo_ref[at, :d_lat] = (
             factor * grad_ref[at, :].astype(F32) - moved[:, :d_lat]
         ).astype(BF16)
         with_expo_ref[at, d_lat:] = (-moved[:, d_lat:]).astype(BF16)
 
 
-def weigh(where, lens, joined, last, stats, ratio, query, grad, projected, scale, blocks, q_dev):
+def weigh(where, lens, joined, stats, ratio, query, grad, scale, q_dev):
     total, c_width = query.shape
-    rows = ratio.shape[0]
-    q_width = projected[0].shape[1]
-    half = total // rows
     smem = pl.BlockSpec(memory_space=pltpu.SMEM)
     vmem = pl.BlockSpec(memory_space=pltpu.VMEM)
-    dq = jax.ShapeDtypeStruct((blocks, half // 2, rows // blocks, q_width), BF16)
     weight = jax.ShapeDtypeStruct((total, c_width), BF16)
-    inputs = (joined, last, stats, ratio, query, grad, *projected)
+    inputs = (*joined, stats, ratio, query, grad)
     return pl.pallas_call(
         functools.partial(weigh_kernel, scale, q_dev),
-        out_shape=(dq, dq, weight, weight),
+        out_shape=(weight, weight, jax.ShapeDtypeStruct((2, total), F32)),
         in_specs=[smem, smem] + [vmem] * len(inputs),
-        out_specs=[vmem] * 4,
+        out_specs=[vmem] * 3,
         compiler_params=pltpu.CompilerParams(vmem_limit_bytes=WEIGH_MIB * MIB),
         cost_estimate=pl.CostEstimate(
             flops=10 * total * c_width, bytes_accessed=8 * total * c_width, transcendentals=0
         ),
     )(where, lens, *inputs)
+
+
+def query_kernel(where_ref, factors_ref, key_ref, *refs):
+    by_spread_refs, by_expo_refs = refs[:-2:2], refs[1:-2:2]
+    keep_ref, send_ref = refs[-2:]
+    half, d_lat = key_ref.shape[:2]
+    blocks, size = keep_ref.shape[0], keep_ref.shape[2] // 2
+    rows = 2 * size * blocks
+    second = where_ref[4 + blocks] == 1
+    together = half // len(by_spread_refs)
+    for p in range(half // 2):
+        part = 2 * p // together
+        columns = slice(p * 2 * rows, (p + 1) * 2 * rows)
+        first = (2 * p % together) * rows
+        inside = slice(first, first + 2 * rows)
+        full = factors_ref[1:2, columns] * by_expo_refs[part][:, inside]
+        full = factors_ref[0:1, columns] * (by_spread_refs[part][:, inside] - full)
+        heads = []
+        for j in range(2):
+            at = slice(j * rows, (j + 1) * rows)
+            nope = lax.dot_general(
+                full[:d_lat, at].astype(BF16),
+                key_ref[2 * p + j],
+                (((0,), (0,)), ((), ())),
+                preferred_element_type=F32,
+            )
+            heads.append(jnp.concatenate([nope, full[d_lat:, at].T], axis=1))
+        for b in range(blocks):
+            pieces = []
+            for x in range(2):
+                first = (2 * b + x) * size
+                pieces.append(jnp.concatenate([y[first : first + size] for y in heads], axis=0))
+            keep_ref[b, p] = jnp.where(second, pieces[1], pieces[0]).astype(BF16)
+            send_ref[b, p] = jnp.where(second, pieces[0], pieces[1]).astype(BF16)
+
+
+def query_terms(where, factors, w_key, projected, blocks, q_width):
+    half = w_key.shape[0]
+    rows = factors.shape[1] // half
+    smem = pl.BlockSpec(memory_space=pltpu.SMEM)
+    vmem = pl.BlockSpec(memory_space=pltpu.VMEM)
+    dq = jax.ShapeDtypeStruct((blocks, half // 2, rows // blocks, q_width), BF16)
+    return pl.pallas_call(
+        query_kernel,
+        out_shape=(dq, dq),
+        in_specs=[smem] + [vmem] * (2 + len(projected)),
+        out_specs=[vmem] * 2,
+        compiler_params=pltpu.CompilerParams(vmem_limit_bytes=WEIGH_MIB * MIB),
+        cost_estimate=pl.CostEstimate(
+            flops=4 * w_key.size * rows, bytes_accessed=8 * w_key.size, transcendentals=0
+        ),
+    )(where, factors, w_key, *projected)
 
 
 def cache_kernel(part, d_lat, order_ref, spread_ref, expo_ref, with_spread_ref, with_expo_ref, *refs):
@@ -481,35 +513,33 @@
     block, latent_cache = lax.optimization_barrier((block, latent_cache))
     own_t = latent_cache.T
     other_t = permute(latent_cache, "ctx", other_core).T
-    own_keys = stage(own_t)
-    other_keys = stage(other_t)
-    up = down = block
+    (own_keys,) = stage(own_t)
+    cache_t, other_keys = stage(other_t, own_t)
+    along_z = lambda x, k: permute(x, "ctx", lambda i: (i + 4 * k) % (4 * nz))
     ring = [block] + [None] * (nz - 1)
-    for k in range(1, nz // 2 + 1):
-        up = permute(up, "ctx", lambda i: (i + 4) % (4 * nz))
-        ring[nz - k] = up
-        if k < nz // 2:
-            down = permute(down, "ctx", lambda i: (i - 4) % (4 * nz))
-            ring[k] = down
+    ring[nz - 2], ring[2] = along_z(block, 2), along_z(block, -2)
+    ring[nz - 1], ring[1] = along_z(block, 1), along_z(block, -1)
+    ring[nz - 4] = along_z(ring[nz - 2], 2)
+    ring[nz - 3], ring[3] = along_z(ring[nz - 2], 1), along_z(ring[2], -1)
 
     query, grad, expo, spread, stats, ratio, w_key = attend(
         where, ring, kv_up, own_keys, other_keys, scale * LOG2E
     )
 
-    joined = stats
+    joined = [stats]
     projected = []
-    pairings = [other_x_lo] + [lambda i, k=k: i ^ (4 << k) for k in range(nz.bit_length() - 1)]
-    for p, pairing in enumerate(pairings):
-        if p:
-            joined = join(joined, last)
-        last = permute(joined, "ctx", pairing)
-        if p < half // 2:
-            terms = project(p, own_t, other_t, spread, expo, w_key, q_width)
-            last, *terms = lax.optimization_barrier((last, *terms))
-            projected += terms
-    dq_keep, dq_send, with_spread, with_expo = weigh(
-        where, pair_lens, joined, last, stats, ratio, query, grad, projected, scale, nz, q_dev
+    parts = 2
+    for group, partners in enumerate(((2, 4, 6), (8, 16, 24))):
+        mine = joined[0] if group == 0 else join(*joined)
+        joined = [permute(mine, "ctx", lambda i, k=k: i ^ k) for k in partners]
+        terms = project(group, parts, cache_t, spread, expo)
+        joined = lax.optimization_barrier((*joined, *terms))
+        projected += joined[len(partners) :]
+        joined = (mine, *joined[: len(partners)])
+    with_spread, with_expo, factors = weigh(
+        where, pair_lens, joined, stats, ratio, query, grad, scale, q_dev
     )
+    dq_keep, dq_send = query_terms(where, factors, w_key, projected, nz, q_width)
     dq_pair = permute(dq_send, "ctx", other_x_lo)
     keys = p_dev // (2 * ny)
     there, here = 1 - x_hi, x_hi

time: 110 us -> 104 us (0.945)
  Pallas kernels: 36.9 us -> 31.3 us
  waiting for transfers between devices: 20 us -> 15 us
  starting transfers between devices: 45.9 us -> 49.6 us
    pallas_call x4 -> x2, Pallas kernels: 12.3 us -> 5.19 us  [project(): pl.pallas_call(functools.partial(project_kernel, p), out_shape=(jax.Shape...]
    ppermute x25 -> x27, waiting for transfers between devices: 20 us -> 15 us  [permute(): lax.ppermute(x, axis, [(i, to(i)) for i in range(lax.axis_size(axis))])]
    ppermute x25 -> x27, starting transfers between devices: 41.6 us -> 45.4 us  [permute(): lax.ppermute(x, axis, [(i, to(i)) for i in range(lax.axis_size(axis))])]
    pallas_call x5 -> x4, Pallas kernels: 0.86 us -> 2.37 us  [the longest x1 1.41 us: query_terms(): pl.pallas_call(query_kernel, out_shape=(dq, dq), in_specs=[smem] + [vmem]...]
    unnamed x15 -> x13, local copies, waits for them, and re-layouts: 4.04 us -> 4.03 us
  transfers between devices with their start and end apart: 26 -> 28, of which waited for: 9 -> 7; matrix products, arithmetic and copies ran while one was open for 2% -> 2% of each run, Pallas kernels for 19% -> 13%
where the time goes in v2:
time: 104 us; the launch traced here: 103 us
  starting transfers between devices  49.6 us (48%)
  Pallas kernels  31.3 us (30%)
  waiting for transfers between devices  15 us (14%)
  local copies, waits for them, and re-layouts  4.32 us (4%)
  between operations  1.53 us (1%)
    ppermute x27, starting transfers between devices, permute(): lax.ppermute(x, axis, [(i, to(i)) for i in range(lax.axis_size(axis))])  45.4 us
    ppermute x27, waiting for transfers between devices, permute(): lax.ppermute(x, axis, [(i, to(i)) for i in range(lax.axis_size(axis))])  15 us
    pallas_call x1, Pallas kernels, attend(): pl.pallas_call(functools.partial(attend_kernel, score_scale, blocks, toge...  10.7 us
    pallas_call x4, Pallas kernels, cache_terms(): pl.pallas_call(functools.partial(cache_kernel, part, d_lat), out_shape=[j...  9.65 us
    pallas_call x2, Pallas kernels, project(): pl.pallas_call(functools.partial(project_kernel, p), out_shape=(jax.Shape...  5.19 us
    all_to_all x1, starting transfers between devices, per_device(): dq = lax.all_to_all(dq, 'ctx', 0, 0, axis_index_groups=z_groups)  4.2 us
    unnamed x13, local copies, waits for them, and re-layouts  4.03 us
  transfers between devices with their start and end apart: 28, of which 7 were waited for; matrix products, arithmetic and copies ran while one was open for 2% of the time, Pallas kernels for 13%

profile of v2, /device:TPU:1, one launch (start us, length us, event | category | flops | bytes accessed | tf_op | source)
XLA Modules:
  0.0 102.6 jit_solution(1237002802741802971)
XLA Ops:
  1.3 0.1 stack.93.where_ref
  1.4 0.0 copy-start.1
  1.4 0.8 copy-done.1
  2.1 0.7 copy-done.2
  2.9 0.7 copy-done.3
  3.5 0.6 shard_map.86
  4.1 3.3 %collective-permute-start = (bf16[32,384]{1,0:T(8,128)(2,1)S(1)}, bf16[32,384]{1,0:T(8,128)(2,1)S(1)}, u32[]{:S(2)}, u32[]{:S(2)}) collective-permute-start(bf16[32,384]{1,0:T(8,128)(2,1)S(1)} %get-tuple-element.54), channel_id=1, source_target_pairs={{0,8},{8,0},{16,24},{24,16},{32,40},{40,32},{48,56},{56,48},{64,72... | collective-permute-start | bytes 73736 | tf_op jit(solution)/shard_map/ppermute | solution.py:28
  7.4 0.8 collective-permute-done
  8.3 2.9 %collective-permute-done.1 = bf16[64,384]{1,0:T(8,128)(2,1)S(1)} collective-permute-done((bf16[64,384]{1,0:T(8,128)(2,1)S(1)}, bf16[64,384]{1,0:T(8,128)(2,1)S(1)}, u32[]{:S(2)}, u32[]{:S(2)}) %collective-permute-start.1) | collective-permute-done | bytes 49184 | tf_op jit(solution)/shard_map/ppermute | solution.py:28
  11.3 1.6 %collective-permute-start.9 = (bf16[1024,576]{0,1:T(8,128)(2,1)}, bf16[1024,576]{0,1:T(8,128)(2,1)S(1)}, u32[]{:S(2)}, u32[]{:S(2)}) collective-permute-start(bf16[1024,576]{0,1:T(8,128)(2,1)} %param.10), channel_id=1, source_target_pairs={{0,8},{8,0},{16,24},{24,16},{32,40},{40,32},{48,56},{56,48},{64,72... | collective-permute-start | bytes 3538952 | tf_op jit(solution)/shard_map/ppermute | solution.py:28
  12.8 4.3 %collective-permute-start.3 = (bf16[128,384]{1,0:T(8,128)(2,1)S(1)}, bf16[128,384]{1,0:T(8,128)(2,1)S(1)}, u32[]{:S(2)}, u32[]{:S(2)}) collective-permute-start(bf16[128,384]{1,0:T(8,128)(2,1)S(1)} %maximum_select_fusion.refs_0_), channel_id=1, source_target_pairs={{0,192},{8,200},{16,208},{24,216},{32,224},{40,232},{48,240},{56,2... | collective-permute-start | bytes 294920 | tf_op jit(solution)/shard_map/ppermute | solution.py:28
  17.1 0.0 collective-permute-start.5
  17.1 3.1 %collective-permute-start.2 = (bf16[128,384]{1,0:T(8,128)(2,1)S(1)}, bf16[128,384]{1,0:T(8,128)(2,1)S(1)}, u32[]{:S(2)}, u32[]{:S(2)}) collective-permute-start(bf16[128,384]{1,0:T(8,128)(2,1)S(1)} %maximum_select_fusion.refs_0_), channel_id=1, source_target_pairs={{0,224},{8,232},{16,240},{24,248},{32,0},{40,8},{48,16},{56,24},{6... | collective-permute-start | bytes 294920 | tf_op jit(solution)/shard_map/ppermute | solution.py:28
  20.3 0.1 collective-permute-done.3.refs_2_
  20.3 4.8 %collective-permute-start.4 = (bf16[128,384]{1,0:T(8,128)(2,1)S(1)}, bf16[128,384]{1,0:T(8,128)(2,1)S(1)}, u32[]{:S(2)}, u32[]{:S(2)}) collective-permute-start(bf16[128,384]{1,0:T(8,128)(2,1)S(1)} %collective-permute-done.3.refs_2_), channel_id=1, source_target_pairs={{0,224},{8,232},{16,240},{24,248},{32,0},{40,8},{48,16},{56,24},{6... | collective-permute-start | bytes 294920 | tf_op jit(solution)/shard_map/ppermute | solution.py:28
  25.2 0.0 collective-permute-done.5.refs_6_
  25.2 0.0 collective-permute-start.6
  25.2 0.0 collective-permute-done.9
  25.2 0.6 collective-permute-start.7
  25.8 0.1 stack.80.order_ref
  25.9 0.1 stack.77.order_ref
  25.9 1.3 %copy-done = bf16[1024,576]{0,1:T(8,128)(2,1)S(1)} copy-done((bf16[1024,576]{0,1:T(8,128)(2,1)S(1)}, bf16[1024,576]{0,1:T(8,128)(2,1)}, u32[]{:S(2)}) %copy-start) | copy-done | bytes 1179672
  27.2 0.4 shard_map.87.refs_9_
  27.6 0.5 shard_map.88
  28.1 0.0 collective-permute-done.2.refs_1_
  28.2 3.1 %collective-permute-done.6.refs_4_ = bf16[128,384]{1,0:T(8,128)(2,1)S(1)} collective-permute-done((bf16[128,384]{1,0:T(8,128)(2,1)S(1)}, bf16[128,384]{1,0:T(8,128)(2,1)S(1)}, u32[]{:S(2)}, u32[]{:S(2)}) %collective-permute-start.6) | collective-permute-done | bytes 98336 | tf_op jit(solution)/shard_map/ppermute | solution.py:28
  31.2 3.0 %collective-permute-done.7.refs_5_ = bf16[128,384]{1,0:T(8,128)(2,1)S(1)} collective-permute-done((bf16[128,384]{1,0:T(8,128)(2,1)S(1)}, bf16[128,384]{1,0:T(8,128)(2,1)S(1)}, u32[]{:S(2)}, u32[]{:S(2)}) %collective-permute-start.7) | collective-permute-done | bytes 98336 | tf_op jit(solution)/shard_map/ppermute | solution.py:28
  34.2 10.7 %shard_map.89 = (bf16[1024,576]{1,0:T(8,128)(2,1)S(1)}, bf16[1024,512]{1,0:T(8,128)(2,1)S(1)}, bf16[2048,1024]{1,0:T(8,128)(2,1)S(1)}, bf16[2048,1024]{1,0:T(8,1...) custom-call(s32[13]{0:T(128)S(1)} %stack.93.where_ref, ...), custom_call_target="tpu_custom_call" | custom-call | flops 4563402752 | bytes 8388608 | tf_op jit(solution)/shard_map/pallas_call | solution.py:211
  45.0 0.1 collective-permute-start.10
  45.1 0.1 collective-permute-start.11
  45.2 2.5 %collective-permute-start.12 = (f32[3,1024]{1,0:T(4,128)S(1)}, f32[3,1024]{1,0:T(4,128)S(1)}, u32[]{:S(2)}, u32[]{:S(2)}) collective-permute-start(f32[3,1024]{1,0:T(4,128)S(1)} %get-tuple-element.60.refs_0_.refs_4_), channel_id=1, source_target_pairs={{0,48},{8,56},{16,32},{24,40},{32,16},{40,24},{48,0},{56,8},{64,11... | collective-permute-start | bytes 36872 | tf_op jit(solution)/shard_map/ppermute | solution.py:28
  47.7 2.6 %shard_map.90 = (f32[576,512]{1,0:T(8,128)S(1)}, f32[576,512]{1,0:T(8,128)S(1)}) custom-call(bf16[576,2048]{1,0:T(8,128)(2,1)S(1)} %get-tuple-element.61.cache_ref, bf16[2048,1024]{1,0:T(8,128)(2,1)S(1)} %get-tuple-element.58.spread_ref, bf16[2048,1024]{1,0:T(8,128)(2,1)S(1)} %get-tuple-element.59.expo_ref), custom_call_target="tpu_custom_call" | custom-call | flops 2415919104 | bytes 4194304 | tf_op jit(solution)/shard_map/pallas_call | solution.py:251
  50.3 0.1 shard_map.91.refs_0_
  50.4 0.0 copy-start.4
  50.4 0.1 collective-permute-start.13
  50.5 2.2 %collective-permute-start.14 = (f32[3,1024]{1,0:T(4,128)S(1)}, f32[3,1024]{1,0:T(4,128)S(1)}, u32[]{:S(2)}, u32[]{:S(2)}) collective-permute-start(f32[3,1024]{1,0:T(4,128)S(1)} %shard_map.91.refs_0_), channel_id=1, source_target_pairs={{0,128},{8,136},{16,144},{24,152},{32,160},{40,168},{48,176},{56,1... | collective-permute-start | bytes 36872 | tf_op jit(solution)/shard_map/ppermute | solution.py:28
  52.7 3.5 %collective-permute-start.15 = (f32[3,1024]{1,0:T(4,128)S(1)}, f32[3,1024]{1,0:T(4,128)S(1)}, u32[]{:S(2)}, u32[]{:S(2)}) collective-permute-start(f32[3,1024]{1,0:T(4,128)S(1)} %shard_map.91.refs_0_), channel_id=1, source_target_pairs={{0,192},{8,200},{16,208},{24,216},{32,224},{40,232},{48,240},{56,2... | collective-permute-start | bytes 36872 | tf_op jit(solution)/shard_map/ppermute | solution.py:28
  56.1 2.6 %shard_map.92 = (f32[576,512]{1,0:T(8,128)S(1)}, f32[576,512]{1,0:T(8,128)S(1)}) custom-call(bf16[576,2048]{1,0:T(8,128)(2,1)S(1)} %get-tuple-element.61.cache_ref, bf16[2048,1024]{1,0:T(8,128)(2,1)S(1)} %get-tuple-element.58.spread_ref, bf16[2048,1024]{1,0:T(8,128)(2,1)S(1)} %get-tuple-element.59.expo_ref), custom_call_target="tpu_custom_call" | custom-call | flops 2415919104 | bytes 4194304 | tf_op jit(solution)/shard_map/pallas_call | solution.py:251
  58.8 1.7 %shard_map.93 = (bf16[1024,576]{1,0:T(8,128)(2,1)S(1)}, bf16[1024,576]{1,0:T(8,128)(2,1)S(1)}, f32[2,1024]{1,0:T(2,128)S(1)}) custom-call(s32[13]{0:T(128)S(1)} %stack.93.where_ref, s32[4]{0:T(128)S(1)} %copy-done.4, f32[3,1024]{1,0:T(4,128)S(1)} %shard_map.91.refs_0_, f32[3,1024]{1,0:T(4,128)S(1)} %collective-permute-done.13.refs_1_, ...), custom_call_target="tpu_custom_call" | custom-call | flops 5898240 | bytes 4718592 | tf_op jit(solution)/shard_map/pallas_call | solution.py:326
  60.5 1.4 %shard_map.98 = (bf16[8,4,16,192]{3,2,1,0:T(8,128)(2,1)S(1)}, bf16[8,4,16,192]{3,2,1,0:T(8,128)(2,1)S(1)}) custom-call(s32[13]{0:T(128)S(1)} %stack.93.where_ref, f32[2,1024]{1,0:T(2,128)S(1)} %get-tuple-element.87.factors_ref, bf16[8,512,128]{2,1,0:T(8,128)(2,1)S(1)} %get-tuple-element.88.key_ref, f32[576,512]{1,0:T(8,128)S(1)} %get-tuple-element.89.refs_0_, ...), custom_call_target="tpu_custom_call" | custom-call | flops 268435456 | bytes 4194304 | tf_op jit(solution)/shard_map/pallas_call | solution.py:378
  61.9 0.2 collective-permute-start.20
  62.1 2.4 %shard_map.94 = (bf16[128,1152]{1,0:T(8,128)(2,1)S(1)}, bf16[128,1152]{1,0:T(8,128)(2,1)S(1)}) custom-call(s32[8]{0:T(128)S(1)} %stack.80.order_ref, bf16[2,2,4,128,1024]{4,3,2,1,0:T(8,128)(2,1)S(1)} %bitcast.35, bf16[2,2,4,128,1024]{4,3,2,1,0:T(8,128)(2,1)S(1)} %bitcast.31, bf16[1024,576]{1,0:T(8,128)(2,1)S(1)} %get-tuple-element.75.with_spread_ref, ...), custom_call_target="tpu_custom_call" | custom-call | flops 1207959552 | bytes 2097152 | tf_op jit(solution)/shard_map/pallas_call | solution.py:418
  64.5 4.7 %collective-permute-start.16 = (bf16[128,1152]{1,0:T(8,128)(2,1)S(1)}, bf16[128,1152]{1,0:T(8,128)(2,1)S(1)}, u32[]{:S(2)}, u32[]{:S(2)}) collective-permute-start(bf16[128,1152]{1,0:T(8,128)(2,1)S(1)} %get-tuple-element.79), channel_id=1, source_target_pairs={{0,8},{8,0},{16,24},{24,16},{32,40},{40,32},{48,56},{56,48},{64,72... | collective-permute-start | bytes 884744 | tf_op jit(solution)/shard_map/ppermute | solution.py:28
  69.2 0.1 collective-permute-start.17
  69.3 2.4 %shard_map.96 = (bf16[128,1152]{1,0:T(8,128)(2,1)S(1)}, bf16[128,1152]{1,0:T(8,128)(2,1)S(1)}) custom-call(s32[8]{0:T(128)S(1)} %stack.77.order_ref, bf16[2,2,4,128,1024]{4,3,2,1,0:T(8,128)(2,1)S(1)} %bitcast.36, bf16[2,2,4,128,1024]{4,3,2,1,0:T(8,128)(2,1)S(1)} %bitcast.32, bf16[1024,576]{1,0:T(8,128)(2,1)S(1)} %get-tuple-element.75.with_spread_ref, ...), custom_call_target="tpu_custom_call" | custom-call | flops 1207959552 | bytes 2097152 | tf_op jit(solution)/shard_map/pallas_call | solution.py:418
  71.8 0.5 collective-permute-start.18
  72.3 0.1 collective-permute-start.19
  72.4 0.8 add_convert_fusion
  73.2 2.4 %shard_map.95 = (bf16[128,1152]{1,0:T(8,128)(2,1)S(1)}, f32[128,1152]{1,0:T(8,128)S(1)}) custom-call(s32[8]{0:T(128)S(1)} %stack.80.order_ref, bf16[2,2,4,128,1024]{4,3,2,1,0:T(8,128)(2,1)S(1)} %bitcast.37, bf16[2,2,4,128,1024]{4,3,2,1,0:T(8,128)(2,1)S(1)} %bitcast.33, bf16[1024,576]{1,0:T(8,128)(2,1)S(1)} %get-tuple-element.75.with_spread_ref, ...), custom_call_target="tpu_custom_call" | custom-call | flops 1207959552 | bytes 2097152 | tf_op jit(solution)/shard_map/pallas_call | solution.py:418
  75.6 2.4 %shard_map.97 = (bf16[128,1152]{1,0:T(8,128)(2,1)S(1)}, f32[128,1152]{1,0:T(8,128)S(1)}) custom-call(s32[8]{0:T(128)S(1)} %stack.77.order_ref, bf16[2,2,4,128,1024]{4,3,2,1,0:T(8,128)(2,1)S(1)} %bitcast.38, bf16[2,2,4,128,1024]{4,3,2,1,0:T(8,128)(2,1)S(1)} %bitcast.34, bf16[1024,576]{1,0:T(8,128)(2,1)S(1)} %get-tuple-element.75.with_spread_ref, ...), custom_call_target="tpu_custom_call" | custom-call | flops 1207959552 | bytes 2097152 | tf_op jit(solution)/shard_map/pallas_call | solution.py:418
  78.0 4.2 %all-to-all-start = ((bf16[8,4,16,192]{3,2,1,0:T(8,128)(2,1)}), bf16[8,4,16,192]{3,2,1,0:T(8,128)(2,1)S(1)}, u32[]{:S(2)}, u32[]{:S(2)}) async-start(bf16[8,4,16,192]{3,2,1,0:T(8,128)(2,1)} %add_convert_fusion), calls=%async_computation | async-start | bytes 524288 | tf_op jit(solution)/shard_map/all_to_all | solution.py:585
  82.2 2.5 %collective-permute-start.23 = (bf16[128,1152]{1,0:T(8,128)(2,1)S(1)}, bf16[128,1152]{1,0:T(8,128)(2,1)S(1)}, u32[]{:S(2)}, u32[]{:S(2)}) collective-permute-start(bf16[128,1152]{1,0:T(8,128)(2,1)S(1)} %get-tuple-element.100), channel_id=1, source_target_pairs={{0,4},{1,5},{2,6},{3,7},{4,0},{5,1},{6,2},{7,3},{8,12},{9,13},{10,... | collective-permute-start | bytes 884744 | tf_op jit(solution)/shard_map/ppermute | solution.py:28
  84.7 2.7 %collective-permute-start.22 = (bf16[128,1152]{1,0:T(8,128)(2,1)S(1)}, bf16[128,1152]{1,0:T(8,128)(2,1)S(1)}, u32[]{:S(2)}, u32[]{:S(2)}) collective-permute-start(bf16[128,1152]{1,0:T(8,128)(2,1)S(1)} %get-tuple-element.97), channel_id=1, source_target_pairs={{0,3},{1,0},{2,1},{3,2},{4,7},{5,4},{6,5},{7,6},{8,11},{9,8},{10,9... | collective-permute-start | bytes 884744 | tf_op jit(solution)/shard_map/ppermute | solution.py:28
  87.4 4.2 %collective-permute-done.23.arrived_ref = bf16[128,1152]{1,0:T(8,128)(2,1)S(1)} collective-permute-done((bf16[128,1152]{1,0:T(8,128)(2,1)S(1)}, bf16[128,1152]{1,0:T(8,128)(2,1)S(1)}, u32[]{:S(2)}, u32[]{:S(2)}) %collective-permute-start.23) | collective-permute-done | bytes 294944 | tf_op jit(solution)/shard_map/ppermute | solution.py:28
  91.5 0.1 shard_map.100
  91.7 3.0 %collective-permute-start.24 = (bf16[64,1152]{1,0:T(8,128)(2,1)S(1)}, bf16[64,1152]{1,0:T(8,128)(2,1)S(1)}, u32[]{:S(2)}, u32[]{:S(2)}) collective-permute-start(bf16[64,1152]{1,0:T(8,128)(2,1)S(1)} %get-tuple-element.101), channel_id=1, source_target_pairs={{0,2},{1,3},{2,0},{3,1},{4,6},{5,7},{6,4},{7,5},{8,10},{9,11},{10,... | collective-permute-start | bytes 442376 | tf_op jit(solution)/shard_map/ppermute | solution.py:28
  94.7 0.4 collective-permute-start.25
  95.1 0.1 shard_map.99
  95.2 2.5 %collective-permute-start.26 = (bf16[64,1152]{1,0:T(8,128)(2,1)S(1)}, bf16[64,1152]{1,0:T(8,128)(2,1)S(1)}, u32[]{:S(2)}, u32[]{:S(2)}) collective-permute-start(bf16[64,1152]{1,0:T(8,128)(2,1)S(1)} %get-tuple-element.103), channel_id=1, source_target_pairs={{0,4},{1,5},{2,6},{3,7},{4,0},{5,1},{6,2},{7,3},{8,12},{9,13},{10,... | collective-permute-start | bytes 442376 | tf_op jit(solution)/shard_map/ppermute | solution.py:28
  97.8 2.5 %collective-permute-start.21 = (bf16[8,4,192]{2,1,0:T(4,128)(2,1)S(1)}, bf16[8,4,192]{2,1,0:T(4,128)(2,1)S(1)}, u32[]{:S(2)}, u32[]{:S(2)}) collective-permute-start(bf16[8,4,192]{2,1,0:T(4,128)(2,1)S(1)} %get-tuple-element.106), channel_id=1, source_target_pairs={{0,8},{8,0},{16,24},{24,16},{32,40},{40,32},{48,56},{56,48},{64,72... | collective-permute-start | bytes 36872 | tf_op jit(solution)/shard_map/ppermute | solution.py:28
  100.3 0.8 collective-permute-done.21
  101.1 0.6 copy.10
  101.8 0.0 collective-permute-done.25.refs_1_
  101.8 0.8 shard_map.101
  (31 shorter events, 0.2 us)
Async XLA Ops:
  1.4 0.8 copy-start.1
  2.1 0.7 copy-start.2
  2.9 0.7 copy-start.3
  4.1 4.1 %collective-permute-start = (bf16[32,384]{1,0:T(8,128)(2,1)S(1)}, bf16[32,384]{1,0:T(8,128)(2,1)S(1)}, u32[]{:S(2)}, u32[]{:S(2)}) collective-permute-start(bf16[32,384]{1,0:T(8,128)(2,1)S(1)} %get-tuple-element.54), channel_id=1, source_target_pairs={{0,8},{8,0},{16,24},{24,16},{32,40},{40,32},{48,56},{56,48},{64,72... | collective-permute-start | bytes 73736 | tf_op jit(solution)/shard_map/ppermute | solution.py:28
  8.3 2.9 %collective-permute-start.1 = (bf16[64,384]{1,0:T(8,128)(2,1)S(1)}, bf16[64,384]{1,0:T(8,128)(2,1)S(1)}, u32[]{:S(2)}, u32[]{:S(2)}) collective-permute-start(bf16[64,384]{1,0:T(8,128)(2,1)S(1)} %pad_maximum_fusion), channel_id=1, source_target_pairs={{0,16},{8,24},{16,0},{24,8},{32,48},{40,56},{48,32},{56,40},{64,80... | collective-permute-start | bytes 147464 | tf_op jit(solution)/shard_map/ppermute | solution.py:28
  11.3 13.9 %collective-permute-start.9 = (bf16[1024,576]{0,1:T(8,128)(2,1)}, bf16[1024,576]{0,1:T(8,128)(2,1)S(1)}, u32[]{:S(2)}, u32[]{:S(2)}) collective-permute-start(bf16[1024,576]{0,1:T(8,128)(2,1)} %param.10), channel_id=1, source_target_pairs={{0,8},{8,0},{16,24},{24,16},{32,40},{40,32},{48,56},{56,48},{64,72... | collective-permute-start | bytes 3538952 | tf_op jit(solution)/shard_map/ppermute | solution.py:28
  12.8 7.5 %collective-permute-start.3 = (bf16[128,384]{1,0:T(8,128)(2,1)S(1)}, bf16[128,384]{1,0:T(8,128)(2,1)S(1)}, u32[]{:S(2)}, u32[]{:S(2)}) collective-permute-start(bf16[128,384]{1,0:T(8,128)(2,1)S(1)} %maximum_select_fusion.refs_0_), channel_id=1, source_target_pairs={{0,192},{8,200},{16,208},{24,216},{32,224},{40,232},{48,240},{56,2... | collective-permute-start | bytes 294920 | tf_op jit(solution)/shard_map/ppermute | solution.py:28
  17.1 8.0 %collective-permute-start.5 = (bf16[128,384]{1,0:T(8,128)(2,1)S(1)}, bf16[128,384]{1,0:T(8,128)(2,1)S(1)}, u32[]{:S(2)}, u32[]{:S(2)}) collective-permute-start(bf16[128,384]{1,0:T(8,128)(2,1)S(1)} %maximum_select_fusion.refs_0_), channel_id=1, source_target_pairs={{0,64},{8,72},{16,80},{24,88},{32,96},{40,104},{48,112},{56,120},{... | collective-permute-start | bytes 294920 | tf_op jit(solution)/shard_map/ppermute | solution.py:28
  17.1 11.0 %collective-permute-start.2 = (bf16[128,384]{1,0:T(8,128)(2,1)S(1)}, bf16[128,384]{1,0:T(8,128)(2,1)S(1)}, u32[]{:S(2)}, u32[]{:S(2)}) collective-permute-start(bf16[128,384]{1,0:T(8,128)(2,1)S(1)} %maximum_select_fusion.refs_0_), channel_id=1, source_target_pairs={{0,224},{8,232},{16,240},{24,248},{32,0},{40,8},{48,16},{56,24},{6... | collective-permute-start | bytes 294920 | tf_op jit(solution)/shard_map/ppermute | solution.py:28
  20.3 7.9 %collective-permute-start.8 = (bf16[128,384]{1,0:T(8,128)(2,1)S(1)}, bf16[128,384]{1,0:T(8,128)(2,1)S(1)}, u32[]{:S(2)}, u32[]{:S(2)}) collective-permute-start(bf16[128,384]{1,0:T(8,128)(2,1)S(1)} %maximum_select_fusion.refs_0_), channel_id=1, source_target_pairs={{0,32},{8,40},{16,48},{24,56},{32,64},{40,72},{48,80},{56,88},{64,... | collective-permute-start | bytes 294920 | tf_op jit(solution)/shard_map/ppermute | solution.py:28
  20.3 7.8 %collective-permute-start.4 = (bf16[128,384]{1,0:T(8,128)(2,1)S(1)}, bf16[128,384]{1,0:T(8,128)(2,1)S(1)}, u32[]{:S(2)}, u32[]{:S(2)}) collective-permute-start(bf16[128,384]{1,0:T(8,128)(2,1)S(1)} %collective-permute-done.3.refs_2_), channel_id=1, source_target_pairs={{0,224},{8,232},{16,240},{24,248},{32,0},{40,8},{48,16},{56,24},{6... | collective-permute-start | bytes 294920 | tf_op jit(solution)/shard_map/ppermute | solution.py:28
  25.2 6.1 %collective-permute-start.6 = (bf16[128,384]{1,0:T(8,128)(2,1)S(1)}, bf16[128,384]{1,0:T(8,128)(2,1)S(1)}, u32[]{:S(2)}, u32[]{:S(2)}) collective-permute-start(bf16[128,384]{1,0:T(8,128)(2,1)S(1)} %collective-permute-done.5.refs_6_), channel_id=1, source_target_pairs={{0,64},{8,72},{16,80},{24,88},{32,96},{40,104},{48,112},{56,120},{... | collective-permute-start | bytes 294920 | tf_op jit(solution)/shard_map/ppermute | solution.py:28
  25.2 9.0 %collective-permute-start.7 = (bf16[128,384]{1,0:T(8,128)(2,1)S(1)}, bf16[128,384]{1,0:T(8,128)(2,1)S(1)}, u32[]{:S(2)}, u32[]{:S(2)}) collective-permute-start(bf16[128,384]{1,0:T(8,128)(2,1)S(1)} %collective-permute-done.5.refs_6_), channel_id=1, source_target_pairs={{0,32},{8,40},{16,48},{24,56},{32,64},{40,72},{48,80},{56,88},{64,... | collective-permute-start | bytes 294920 | tf_op jit(solution)/shard_map/ppermute | solution.py:28
  25.9 1.3 %copy-start = (bf16[1024,576]{0,1:T(8,128)(2,1)S(1)}, bf16[1024,576]{0,1:T(8,128)(2,1)}, u32[]{:S(2)}) copy-start(bf16[1024,576]{0,1:T(8,128)(2,1)} %param.10) | copy-start | bytes 3538948
  27.2 7.0 %copy-start.5 = (bf16[16,512,256]{2,1,0:T(8,128)(2,1)S(1)}, bf16[16,512,256]{2,1,0:T(8,128)(2,1)}, u32[]{:S(2)}) copy-start(bf16[16,512,256]{2,1,0:T(8,128)(2,1)} %refs_8_.1) | copy-start | bytes 12582916
  45.0 5.3 %collective-permute-start.10 = (f32[3,1024]{1,0:T(4,128)S(1)}, f32[3,1024]{1,0:T(4,128)S(1)}, u32[]{:S(2)}, u32[]{:S(2)}) collective-permute-start(f32[3,1024]{1,0:T(4,128)S(1)} %get-tuple-element.60.refs_0_.refs_4_), channel_id=1, source_target_pairs={{0,16},{8,24},{16,0},{24,8},{32,48},{40,56},{48,32},{56,40},{64,80... | collective-permute-start | bytes 36872 | tf_op jit(solution)/shard_map/ppermute | solution.py:28
  45.1 5.2 %collective-permute-start.11 = (f32[3,1024]{1,0:T(4,128)S(1)}, f32[3,1024]{1,0:T(4,128)S(1)}, u32[]{:S(2)}, u32[]{:S(2)}) collective-permute-start(f32[3,1024]{1,0:T(4,128)S(1)} %get-tuple-element.60.refs_0_.refs_4_), channel_id=1, source_target_pairs={{0,32},{8,40},{16,48},{24,56},{32,0},{40,8},{48,16},{56,24},{64,96... | collective-permute-start | bytes 36872 | tf_op jit(solution)/shard_map/ppermute | solution.py:28
  45.2 5.2 %collective-permute-start.12 = (f32[3,1024]{1,0:T(4,128)S(1)}, f32[3,1024]{1,0:T(4,128)S(1)}, u32[]{:S(2)}, u32[]{:S(2)}) collective-permute-start(f32[3,1024]{1,0:T(4,128)S(1)} %get-tuple-element.60.refs_0_.refs_4_), channel_id=1, source_target_pairs={{0,48},{8,56},{16,32},{24,40},{32,16},{40,24},{48,0},{56,8},{64,11... | collective-permute-start | bytes 36872 | tf_op jit(solution)/shard_map/ppermute | solution.py:28
  50.4 8.4 %copy-start.4 = (s32[4]{0:T(128)S(1)}, s32[4]{0:T(128)}, u32[]{:S(2)}) copy-start(s32[4]{0:T(128)} %lens_ref.1) | copy-start | bytes 52
  50.4 8.3 %collective-permute-start.13 = (f32[3,1024]{1,0:T(4,128)S(1)}, f32[3,1024]{1,0:T(4,128)S(1)}, u32[]{:S(2)}, u32[]{:S(2)}) collective-permute-start(f32[3,1024]{1,0:T(4,128)S(1)} %shard_map.91.refs_0_), channel_id=1, source_target_pairs={{0,64},{8,72},{16,80},{24,88},{32,96},{40,104},{48,112},{56,120},{... | collective-permute-start | bytes 36872 | tf_op jit(solution)/shard_map/ppermute | solution.py:28
  50.5 8.3 %collective-permute-start.14 = (f32[3,1024]{1,0:T(4,128)S(1)}, f32[3,1024]{1,0:T(4,128)S(1)}, u32[]{:S(2)}, u32[]{:S(2)}) collective-permute-start(f32[3,1024]{1,0:T(4,128)S(1)} %shard_map.91.refs_0_), channel_id=1, source_target_pairs={{0,128},{8,136},{16,144},{24,152},{32,160},{40,168},{48,176},{56,1... | collective-permute-start | bytes 36872 | tf_op jit(solution)/shard_map/ppermute | solution.py:28
  52.7 6.1 %collective-permute-start.15 = (f32[3,1024]{1,0:T(4,128)S(1)}, f32[3,1024]{1,0:T(4,128)S(1)}, u32[]{:S(2)}, u32[]{:S(2)}) collective-permute-start(f32[3,1024]{1,0:T(4,128)S(1)} %shard_map.91.refs_0_), channel_id=1, source_target_pairs={{0,192},{8,200},{16,208},{24,216},{32,224},{40,232},{48,240},{56,2... | collective-permute-start | bytes 36872 | tf_op jit(solution)/shard_map/ppermute | solution.py:28
  61.9 10.5 %collective-permute-start.20 = (bf16[8,4,16,192]{3,2,1,0:T(8,128)(2,1)S(1)}, bf16[8,4,16,192]{3,2,1,0:T(8,128)(2,1)S(1)}, u32[]{:S(2)}, u32[]{:S(2)}) collective-permute-start(bf16[8,4,16,192]{3,2,1,0:T(8,128)(2,1)S(1)} %get-tuple-element.94), channel_id=1, source_target_pairs={{0,16},{8,24},{16,0},{24,8},{32,48},{40,56},{48,32},{56,40},{64,80... | collective-permute-start | bytes 589832 | tf_op jit(solution)/shard_map/ppermute | solution.py:28
  64.5 8.7 %collective-permute-start.16 = (bf16[128,1152]{1,0:T(8,128)(2,1)S(1)}, bf16[128,1152]{1,0:T(8,128)(2,1)S(1)}, u32[]{:S(2)}, u32[]{:S(2)}) collective-permute-start(bf16[128,1152]{1,0:T(8,128)(2,1)S(1)} %get-tuple-element.79), channel_id=1, source_target_pairs={{0,8},{8,0},{16,24},{24,16},{32,40},{40,32},{48,56},{56,48},{64,72... | collective-permute-start | bytes 884744 | tf_op jit(solution)/shard_map/ppermute | solution.py:28
  69.2 3.9 %collective-permute-start.17 = (bf16[128,1152]{1,0:T(8,128)(2,1)S(1)}, bf16[128,1152]{1,0:T(8,128)(2,1)S(1)}, u32[]{:S(2)}, u32[]{:S(2)}) collective-permute-start(bf16[128,1152]{1,0:T(8,128)(2,1)S(1)} %get-tuple-element.80), channel_id=1, source_target_pairs={{0,8},{8,0},{16,24},{24,16},{32,40},{40,32},{48,56},{56,48},{64,72... | collective-permute-start | bytes 884744 | tf_op jit(solution)/shard_map/ppermute | solution.py:28
  71.8 3.8 %collective-permute-start.18 = (bf16[128,1152]{1,0:T(8,128)(2,1)S(1)}, bf16[128,1152]{1,0:T(8,128)(2,1)S(1)}, u32[]{:S(2)}, u32[]{:S(2)}) collective-permute-start(bf16[128,1152]{1,0:T(8,128)(2,1)S(1)} %get-tuple-element.84), channel_id=1, source_target_pairs={{0,8},{8,0},{16,24},{24,16},{32,40},{40,32},{48,56},{56,48},{64,72... | collective-permute-start | bytes 884744 | tf_op jit(solution)/shard_map/ppermute | solution.py:28
  72.3 3.3 %collective-permute-start.19 = (bf16[128,1152]{1,0:T(8,128)(2,1)S(1)}, bf16[128,1152]{1,0:T(8,128)(2,1)S(1)}, u32[]{:S(2)}, u32[]{:S(2)}) collective-permute-start(bf16[128,1152]{1,0:T(8,128)(2,1)S(1)} %get-tuple-element.85), channel_id=1, source_target_pairs={{0,8},{8,0},{16,24},{24,16},{32,40},{40,32},{48,56},{56,48},{64,72... | collective-permute-start | bytes 884744 | tf_op jit(solution)/shard_map/ppermute | solution.py:28
  78.0 19.7 %all-to-all-start = ((bf16[8,4,16,192]{3,2,1,0:T(8,128)(2,1)}), bf16[8,4,16,192]{3,2,1,0:T(8,128)(2,1)S(1)}, u32[]{:S(2)}, u32[]{:S(2)}) async-start(bf16[8,4,16,192]{3,2,1,0:T(8,128)(2,1)} %add_convert_fusion), calls=%async_computation | async-start | bytes 524288 | tf_op jit(solution)/shard_map/all_to_all | solution.py:585
  82.2 9.4 %collective-permute-start.23 = (bf16[128,1152]{1,0:T(8,128)(2,1)S(1)}, bf16[128,1152]{1,0:T(8,128)(2,1)S(1)}, u32[]{:S(2)}, u32[]{:S(2)}) collective-permute-start(bf16[128,1152]{1,0:T(8,128)(2,1)S(1)} %get-tuple-element.100), channel_id=1, source_target_pairs={{0,4},{1,5},{2,6},{3,7},{4,0},{5,1},{6,2},{7,3},{8,12},{9,13},{10,... | collective-permute-start | bytes 884744 | tf_op jit(solution)/shard_map/ppermute | solution.py:28
  84.7 10.4 %collective-permute-start.22 = (bf16[128,1152]{1,0:T(8,128)(2,1)S(1)}, bf16[128,1152]{1,0:T(8,128)(2,1)S(1)}, u32[]{:S(2)}, u32[]{:S(2)}) collective-permute-start(bf16[128,1152]{1,0:T(8,128)(2,1)S(1)} %get-tuple-element.97), channel_id=1, source_target_pairs={{0,3},{1,0},{2,1},{3,2},{4,7},{5,4},{6,5},{7,6},{8,11},{9,8},{10,9... | collective-permute-start | bytes 884744 | tf_op jit(solution)/shard_map/ppermute | solution.py:28
  91.7 10.1 %collective-permute-start.24 = (bf16[64,1152]{1,0:T(8,128)(2,1)S(1)}, bf16[64,1152]{1,0:T(8,128)(2,1)S(1)}, u32[]{:S(2)}, u32[]{:S(2)}) collective-permute-start(bf16[64,1152]{1,0:T(8,128)(2,1)S(1)} %get-tuple-element.101), channel_id=1, source_target_pairs={{0,2},{1,3},{2,0},{3,1},{4,6},{5,7},{6,4},{7,5},{8,10},{9,11},{10,... | collective-permute-start | bytes 442376 | tf_op jit(solution)/shard_map/ppermute | solution.py:28
  94.7 7.1 %collective-permute-start.25 = (bf16[64,1152]{1,0:T(8,128)(2,1)S(1)}, bf16[64,1152]{1,0:T(8,128)(2,1)S(1)}, u32[]{:S(2)}, u32[]{:S(2)}) collective-permute-start(bf16[64,1152]{1,0:T(8,128)(2,1)S(1)} %get-tuple-element.102), channel_id=1, source_target_pairs={{0,1},{1,2},{2,3},{3,0},{4,5},{5,6},{6,7},{7,4},{8,9},{9,10},{10,1... | collective-permute-start | bytes 442376 | tf_op jit(solution)/shard_map/ppermute | solution.py:28
  95.2 6.6 %collective-permute-start.26 = (bf16[64,1152]{1,0:T(8,128)(2,1)S(1)}, bf16[64,1152]{1,0:T(8,128)(2,1)S(1)}, u32[]{:S(2)}, u32[]{:S(2)}) collective-permute-start(bf16[64,1152]{1,0:T(8,128)(2,1)S(1)} %get-tuple-element.103), channel_id=1, source_target_pairs={{0,4},{1,5},{2,6},{3,7},{4,0},{5,1},{6,2},{7,3},{8,12},{9,13},{10,... | collective-permute-start | bytes 442376 | tf_op jit(solution)/shard_map/ppermute | solution.py:28
  97.8 3.3 %collective-permute-start.21 = (bf16[8,4,192]{2,1,0:T(4,128)(2,1)S(1)}, bf16[8,4,192]{2,1,0:T(4,128)(2,1)S(1)}, u32[]{:S(2)}, u32[]{:S(2)}) collective-permute-start(bf16[8,4,192]{2,1,0:T(4,128)(2,1)S(1)} %get-tuple-element.106), channel_id=1, source_target_pairs={{0,8},{8,0},{16,24},{24,16},{32,40},{40,32},{48,56},{56,48},{64,72... | collective-permute-start | bytes 36872 | tf_op jit(solution)/shard_map/ppermute | solution.py:28

commit v3 on v2

--- a/solution.py
+++ b/solution.py
@@ -14,7 +14,7 @@
 FLOOR = -1e29
 F32 = jnp.float32
 BF16 = jnp.bfloat16
-CHUNK = 256
+CHUNK = 1024
 TOGETHER = 4
 PACKED = 384
 MIB = 1024 * 1024
@@ -507,12 +507,11 @@
     where = [core, ctx_index * p_dev, (ctx_index ^ 1) * p_dev, prompt_len[0]]
     where = where + [(z + k) & (nz - 1) for k in range(nz)] + [x_lo]
     where = jnp.stack(where).astype(jnp.int32)
+    own_t = latent_cache.T
+    other_t = permute(latent_cache, "ctx", other_core).T
     mine, theirs = pack(where, token_ratio, queries, out_grad)
     block = jnp.concatenate([mine, permute(theirs, "ctx", other_core)], 0)
     block = in_order(block, permute(block, "ctx", other_x_lo), x_lo == 1, 0)
-    block, latent_cache = lax.optimization_barrier((block, latent_cache))
-    own_t = latent_cache.T
-    other_t = permute(latent_cache, "ctx", other_core).T
     (own_keys,) = stage(own_t)
     cache_t, other_keys = stage(other_t, own_t)
     along_z = lambda x, k: permute(x, "ctx", lambda i: (i + 4 * k) % (4 * nz))

time: 104 us -> 102 us (0.981)
  waiting for transfers between devices: 15 us -> 13.1 us
    ppermute x27, waiting for transfers between devices: 15 us -> 13.1 us  [permute(): lax.ppermute(x, axis, [(i, to(i)) for i in range(lax.axis_size(axis))])]
    ppermute x27, starting transfers between devices: 45.4 us -> 46.8 us  [permute(): lax.ppermute(x, axis, [(i, to(i)) for i in range(lax.axis_size(axis))])]
  transfers between devices with their start and end apart: 28 -> 28, of which waited for: 7 -> 6; matrix products, arithmetic and copies ran while one was open for 2% -> 2% of each run, Pallas kernels for 13% -> 14%
where the time goes in v3:
time: 102 us; the launch traced here: 101 us
  starting transfers between devices  50.2 us (49%)
  Pallas kernels  30.9 us (30%)
  waiting for transfers between devices  13.1 us (13%)
  local copies, waits for them, and re-layouts  4.32 us (4%)
  between operations  1.52 us (1%)
    ppermute x27, starting transfers between devices, permute(): lax.ppermute(x, axis, [(i, to(i)) for i in range(lax.axis_size(axis))])  46.8 us
    ppermute x27, waiting for transfers between devices, permute(): lax.ppermute(x, axis, [(i, to(i)) for i in range(lax.axis_size(axis))])  13.1 us
    pallas_call x1, Pallas kernels, attend(): pl.pallas_call(functools.partial(attend_kernel, score_scale, blocks, toge...  10.4 us
    pallas_call x4, Pallas kernels, cache_terms(): pl.pallas_call(functools.partial(cache_kernel, part, d_lat), out_shape=[j...  9.65 us
    pallas_call x2, Pallas kernels, project(): pl.pallas_call(functools.partial(project_kernel, p), out_shape=(jax.Shape...  5.19 us
    unnamed x13, local copies, waits for them, and re-layouts  4.03 us
    all_to_all x1, starting transfers between devices, per_device(): dq = lax.all_to_all(dq, 'ctx', 0, 0, axis_index_groups=z_groups)  3.42 us
  transfers between devices with their start and end apart: 28, of which 6 were waited for; matrix products, arithmetic and copies ran while one was open for 2% of the time, Pallas kernels for 14%

profile of v3, /device:TPU:1, one launch (start us, length us, event | category | flops | bytes accessed | tf_op | source)
XLA Modules:
  0.0 101.0 jit_solution(8730902915443172939)
XLA Ops:
  0.6 3.3 %collective-permute-start.9 = (bf16[1024,576]{0,1:T(8,128)(2,1)}, bf16[1024,576]{0,1:T(8,128)(2,1)S(1)}, u32[]{:S(2)}, u32[]{:S(2)}) collective-permute-start(bf16[1024,576]{0,1:T(8,128)(2,1)} %param.10), channel_id=1, source_target_pairs={{0,8},{8,0},{16,24},{24,16},{32,40},{40,32},{48,56},{56,48},{64,72... | collective-permute-start | bytes 3538952 | tf_op jit(solution)/shard_map/ppermute | solution.py:28
  4.6 0.1 stack.93.where_ref
  4.7 0.0 copy-start.1
  4.7 0.8 copy-done.1
  5.5 0.7 copy-done.2
  6.2 0.7 copy-done.3
  6.8 0.6 shard_map.86
  7.5 0.1 collective-permute-start
  7.5 1.2 %collective-permute-done = bf16[32,384]{1,0:T(8,128)(2,1)S(1)} collective-permute-done((bf16[32,384]{1,0:T(8,128)(2,1)S(1)}, bf16[32,384]{1,0:T(8,128)(2,1)S(1)}, u32[]{:S(2)}, u32[]{:S(2)}) %collective-permute-start) | collective-permute-done | bytes 24608 | tf_op jit(solution)/shard_map/ppermute | solution.py:28
  8.7 2.9 %collective-permute-done.1 = bf16[64,384]{1,0:T(8,128)(2,1)S(1)} collective-permute-done((bf16[64,384]{1,0:T(8,128)(2,1)S(1)}, bf16[64,384]{1,0:T(8,128)(2,1)S(1)}, u32[]{:S(2)}, u32[]{:S(2)}) %collective-permute-start.1) | collective-permute-done | bytes 49184 | tf_op jit(solution)/shard_map/ppermute | solution.py:28
  11.7 4.4 %collective-permute-start.3 = (bf16[128,384]{1,0:T(8,128)(2,1)S(1)}, bf16[128,384]{1,0:T(8,128)(2,1)S(1)}, u32[]{:S(2)}, u32[]{:S(2)}) collective-permute-start(bf16[128,384]{1,0:T(8,128)(2,1)S(1)} %maximum_select_fusion.refs_0_), channel_id=1, source_target_pairs={{0,192},{8,200},{16,208},{24,216},{32,224},{40,232},{48,240},{56,2... | collective-permute-start | bytes 294920 | tf_op jit(solution)/shard_map/ppermute | solution.py:28
  16.0 0.0 collective-permute-start.5
  16.0 3.1 %collective-permute-start.2 = (bf16[128,384]{1,0:T(8,128)(2,1)S(1)}, bf16[128,384]{1,0:T(8,128)(2,1)S(1)}, u32[]{:S(2)}, u32[]{:S(2)}) collective-permute-start(bf16[128,384]{1,0:T(8,128)(2,1)S(1)} %maximum_select_fusion.refs_0_), channel_id=1, source_target_pairs={{0,224},{8,232},{16,240},{24,248},{32,0},{40,8},{48,16},{56,24},{6... | collective-permute-start | bytes 294920 | tf_op jit(solution)/shard_map/ppermute | solution.py:28
  19.2 0.0 collective-permute-start.8
  19.2 0.0 collective-permute-done.3.refs_2_
  19.2 4.2 %collective-permute-start.4 = (bf16[128,384]{1,0:T(8,128)(2,1)S(1)}, bf16[128,384]{1,0:T(8,128)(2,1)S(1)}, u32[]{:S(2)}, u32[]{:S(2)}) collective-permute-start(bf16[128,384]{1,0:T(8,128)(2,1)S(1)} %collective-permute-done.3.refs_2_), channel_id=1, source_target_pairs={{0,224},{8,232},{16,240},{24,248},{32,0},{40,8},{48,16},{56,24},{6... | collective-permute-start | bytes 294920 | tf_op jit(solution)/shard_map/ppermute | solution.py:28
  23.4 0.0 collective-permute-done.9
  23.4 0.4 collective-permute-start.7
  23.8 0.1 stack.80.order_ref
  23.9 0.1 stack.77.order_ref
  24.0 1.3 %copy-done = bf16[1024,576]{0,1:T(8,128)(2,1)S(1)} copy-done((bf16[1024,576]{0,1:T(8,128)(2,1)S(1)}, bf16[1024,576]{0,1:T(8,128)(2,1)}, u32[]{:S(2)}) %copy-start) | copy-done | bytes 1179672
  25.3 0.4 shard_map.87.refs_9_
  25.7 0.5 shard_map.88
  26.2 0.0 collective-permute-done.2.refs_1_
  26.2 0.0 collective-permute-done.8.refs_7_
  26.2 3.2 %collective-permute-done.6.refs_4_ = bf16[128,384]{1,0:T(8,128)(2,1)S(1)} collective-permute-done((bf16[128,384]{1,0:T(8,128)(2,1)S(1)}, bf16[128,384]{1,0:T(8,128)(2,1)S(1)}, u32[]{:S(2)}, u32[]{:S(2)}) %collective-permute-start.6) | collective-permute-done | bytes 98336 | tf_op jit(solution)/shard_map/ppermute | solution.py:28
  29.4 0.4 collective-permute-done.7.refs_5_
  29.8 10.4 %shard_map.89 = (bf16[1024,576]{1,0:T(8,128)(2,1)S(1)}, bf16[1024,512]{1,0:T(8,128)(2,1)S(1)}, bf16[2048,1024]{1,0:T(8,128)(2,1)S(1)}, bf16[2048,1024]{1,0:T(8,1...) custom-call(s32[13]{0:T(128)S(1)} %stack.93.where_ref, ...), custom_call_target="tpu_custom_call" | custom-call | flops 4563402752 | bytes 8388608 | tf_op jit(solution)/shard_map/pallas_call | solution.py:211
  40.2 1.5 %collective-permute-start.10 = (f32[3,1024]{1,0:T(4,128)S(1)}, f32[3,1024]{1,0:T(4,128)S(1)}, u32[]{:S(2)}, u32[]{:S(2)}) collective-permute-start(f32[3,1024]{1,0:T(4,128)S(1)} %get-tuple-element.56.refs_0_.refs_4_), channel_id=1, source_target_pairs={{0,16},{8,24},{16,0},{24,8},{32,48},{40,56},{48,32},{56,40},{64,80... | collective-permute-start | bytes 36872 | tf_op jit(solution)/shard_map/ppermute | solution.py:28
  41.7 0.1 collective-permute-start.11
  41.8 1.3 %collective-permute-start.12 = (f32[3,1024]{1,0:T(4,128)S(1)}, f32[3,1024]{1,0:T(4,128)S(1)}, u32[]{:S(2)}, u32[]{:S(2)}) collective-permute-start(f32[3,1024]{1,0:T(4,128)S(1)} %get-tuple-element.56.refs_0_.refs_4_), channel_id=1, source_target_pairs={{0,48},{8,56},{16,32},{24,40},{32,16},{40,24},{48,0},{56,8},{64,11... | collective-permute-start | bytes 36872 | tf_op jit(solution)/shard_map/ppermute | solution.py:28
  43.1 2.6 %shard_map.90 = (f32[576,512]{1,0:T(8,128)S(1)}, f32[576,512]{1,0:T(8,128)S(1)}) custom-call(bf16[576,2048]{1,0:T(8,128)(2,1)S(1)} %get-tuple-element.57.cache_ref, bf16[2048,1024]{1,0:T(8,128)(2,1)S(1)} %get-tuple-element.54.spread_ref, bf16[2048,1024]{1,0:T(8,128)(2,1)S(1)} %get-tuple-element.55.expo_ref), custom_call_target="tpu_custom_call" | custom-call | flops 2415919104 | bytes 4194304 | tf_op jit(solution)/shard_map/pallas_call | solution.py:251
  45.7 0.0 collective-permute-done.10.refs_1_
  45.7 0.1 shard_map.91.refs_0_
  45.8 0.0 copy-start.4
  45.8 0.1 collective-permute-start.13
  45.9 3.0 %collective-permute-start.14 = (f32[3,1024]{1,0:T(4,128)S(1)}, f32[3,1024]{1,0:T(4,128)S(1)}, u32[]{:S(2)}, u32[]{:S(2)}) collective-permute-start(f32[3,1024]{1,0:T(4,128)S(1)} %shard_map.91.refs_0_), channel_id=1, source_target_pairs={{0,128},{8,136},{16,144},{24,152},{32,160},{40,168},{48,176},{56,1... | collective-permute-start | bytes 36872 | tf_op jit(solution)/shard_map/ppermute | solution.py:28
  48.9 2.6 %collective-permute-start.15 = (f32[3,1024]{1,0:T(4,128)S(1)}, f32[3,1024]{1,0:T(4,128)S(1)}, u32[]{:S(2)}, u32[]{:S(2)}) collective-permute-start(f32[3,1024]{1,0:T(4,128)S(1)} %shard_map.91.refs_0_), channel_id=1, source_target_pairs={{0,192},{8,200},{16,208},{24,216},{32,224},{40,232},{48,240},{56,2... | collective-permute-start | bytes 36872 | tf_op jit(solution)/shard_map/ppermute | solution.py:28
  51.6 2.6 %shard_map.92 = (f32[576,512]{1,0:T(8,128)S(1)}, f32[576,512]{1,0:T(8,128)S(1)}) custom-call(bf16[576,2048]{1,0:T(8,128)(2,1)S(1)} %get-tuple-element.57.cache_ref, bf16[2048,1024]{1,0:T(8,128)(2,1)S(1)} %get-tuple-element.54.spread_ref, bf16[2048,1024]{1,0:T(8,128)(2,1)S(1)} %get-tuple-element.55.expo_ref), custom_call_target="tpu_custom_call" | custom-call | flops 2415919104 | bytes 4194304 | tf_op jit(solution)/shard_map/pallas_call | solution.py:251
  54.2 1.7 %shard_map.93 = (bf16[1024,576]{1,0:T(8,128)(2,1)S(1)}, bf16[1024,576]{1,0:T(8,128)(2,1)S(1)}, f32[2,1024]{1,0:T(2,128)S(1)}) custom-call(s32[13]{0:T(128)S(1)} %stack.93.where_ref, s32[4]{0:T(128)S(1)} %copy-done.4, f32[3,1024]{1,0:T(4,128)S(1)} %shard_map.91.refs_0_, f32[3,1024]{1,0:T(4,128)S(1)} %collective-permute-done.13.refs_1_, ...), custom_call_target="tpu_custom_call" | custom-call | flops 5898240 | bytes 4718592 | tf_op jit(solution)/shard_map/pallas_call | solution.py:326
  55.9 1.4 %shard_map.98 = (bf16[8,4,16,192]{3,2,1,0:T(8,128)(2,1)S(1)}, bf16[8,4,16,192]{3,2,1,0:T(8,128)(2,1)S(1)}) custom-call(s32[13]{0:T(128)S(1)} %stack.93.where_ref, f32[2,1024]{1,0:T(2,128)S(1)} %get-tuple-element.83.factors_ref, bf16[8,512,128]{2,1,0:T(8,128)(2,1)S(1)} %get-tuple-element.84.key_ref, f32[576,512]{1,0:T(8,128)S(1)} %get-tuple-element.85.refs_0_, ...), custom_call_target="tpu_custom_call" | custom-call | flops 268435456 | bytes 4194304 | tf_op jit(solution)/shard_map/pallas_call | solution.py:378
  57.3 1.3 %collective-permute-start.20 = (bf16[8,4,16,192]{3,2,1,0:T(8,128)(2,1)S(1)}, bf16[8,4,16,192]{3,2,1,0:T(8,128)(2,1)S(1)}, u32[]{:S(2)}, u32[]{:S(2)}) collective-permute-start(bf16[8,4,16,192]{3,2,1,0:T(8,128)(2,1)S(1)} %get-tuple-element.90), channel_id=1, source_target_pairs={{0,16},{8,24},{16,0},{24,8},{32,48},{40,56},{48,32},{56,40},{64,80... | collective-permute-start | bytes 589832 | tf_op jit(solution)/shard_map/ppermute | solution.py:28
  58.6 2.4 %shard_map.94 = (bf16[128,1152]{1,0:T(8,128)(2,1)S(1)}, bf16[128,1152]{1,0:T(8,128)(2,1)S(1)}) custom-call(s32[8]{0:T(128)S(1)} %stack.80.order_ref, bf16[2,2,4,128,1024]{4,3,2,1,0:T(8,128)(2,1)S(1)} %bitcast.35, bf16[2,2,4,128,1024]{4,3,2,1,0:T(8,128)(2,1)S(1)} %bitcast.31, bf16[1024,576]{1,0:T(8,128)(2,1)S(1)} %get-tuple-element.71.with_spread_ref, ...), custom_call_target="tpu_custom_call" | custom-call | flops 1207959552 | bytes 2097152 | tf_op jit(solution)/shard_map/pallas_call | solution.py:418
  61.0 7.2 %collective-permute-start.16 = (bf16[128,1152]{1,0:T(8,128)(2,1)S(1)}, bf16[128,1152]{1,0:T(8,128)(2,1)S(1)}, u32[]{:S(2)}, u32[]{:S(2)}) collective-permute-start(bf16[128,1152]{1,0:T(8,128)(2,1)S(1)} %get-tuple-element.75), channel_id=1, source_target_pairs={{0,8},{8,0},{16,24},{24,16},{32,40},{40,32},{48,56},{56,48},{64,72... | collective-permute-start | bytes 884744 | tf_op jit(solution)/shard_map/ppermute | solution.py:28
  68.2 0.1 collective-permute-start.17
  68.3 2.4 %shard_map.96 = (bf16[128,1152]{1,0:T(8,128)(2,1)S(1)}, bf16[128,1152]{1,0:T(8,128)(2,1)S(1)}) custom-call(s32[8]{0:T(128)S(1)} %stack.77.order_ref, bf16[2,2,4,128,1024]{4,3,2,1,0:T(8,128)(2,1)S(1)} %bitcast.36, bf16[2,2,4,128,1024]{4,3,2,1,0:T(8,128)(2,1)S(1)} %bitcast.32, bf16[1024,576]{1,0:T(8,128)(2,1)S(1)} %get-tuple-element.71.with_spread_ref, ...), custom_call_target="tpu_custom_call" | custom-call | flops 1207959552 | bytes 2097152 | tf_op jit(solution)/shard_map/pallas_call | solution.py:418
  70.7 0.7 collective-permute-start.18
  71.4 0.1 collective-permute-start.19
  71.5 0.8 add_convert_fusion
  72.3 2.4 %shard_map.95 = (bf16[128,1152]{1,0:T(8,128)(2,1)S(1)}, f32[128,1152]{1,0:T(8,128)S(1)}) custom-call(s32[8]{0:T(128)S(1)} %stack.80.order_ref, bf16[2,2,4,128,1024]{4,3,2,1,0:T(8,128)(2,1)S(1)} %bitcast.37, bf16[2,2,4,128,1024]{4,3,2,1,0:T(8,128)(2,1)S(1)} %bitcast.33, bf16[1024,576]{1,0:T(8,128)(2,1)S(1)} %get-tuple-element.71.with_spread_ref, ...), custom_call_target="tpu_custom_call" | custom-call | flops 1207959552 | bytes 2097152 | tf_op jit(solution)/shard_map/pallas_call | solution.py:418
  74.8 2.4 %shard_map.97 = (bf16[128,1152]{1,0:T(8,128)(2,1)S(1)}, f32[128,1152]{1,0:T(8,128)S(1)}) custom-call(s32[8]{0:T(128)S(1)} %stack.77.order_ref, bf16[2,2,4,128,1024]{4,3,2,1,0:T(8,128)(2,1)S(1)} %bitcast.38, bf16[2,2,4,128,1024]{4,3,2,1,0:T(8,128)(2,1)S(1)} %bitcast.34, bf16[1024,576]{1,0:T(8,128)(2,1)S(1)} %get-tuple-element.71.with_spread_ref, ...), custom_call_target="tpu_custom_call" | custom-call | flops 1207959552 | bytes 2097152 | tf_op jit(solution)/shard_map/pallas_call | solution.py:418
  77.2 3.4 %all-to-all-start = ((bf16[8,4,16,192]{3,2,1,0:T(8,128)(2,1)}), bf16[8,4,16,192]{3,2,1,0:T(8,128)(2,1)S(1)}, u32[]{:S(2)}, u32[]{:S(2)}) async-start(bf16[8,4,16,192]{3,2,1,0:T(8,128)(2,1)} %add_convert_fusion), calls=%async_computation | async-start | bytes 524288 | tf_op jit(solution)/shard_map/all_to_all | solution.py:584
  80.6 2.5 %collective-permute-start.23 = (bf16[128,1152]{1,0:T(8,128)(2,1)S(1)}, bf16[128,1152]{1,0:T(8,128)(2,1)S(1)}, u32[]{:S(2)}, u32[]{:S(2)}) collective-permute-start(bf16[128,1152]{1,0:T(8,128)(2,1)S(1)} %get-tuple-element.96), channel_id=1, source_target_pairs={{0,4},{1,5},{2,6},{3,7},{4,0},{5,1},{6,2},{7,3},{8,12},{9,13},{10,... | collective-permute-start | bytes 884744 | tf_op jit(solution)/shard_map/ppermute | solution.py:28
  83.1 2.7 %collective-permute-start.22 = (bf16[128,1152]{1,0:T(8,128)(2,1)S(1)}, bf16[128,1152]{1,0:T(8,128)(2,1)S(1)}, u32[]{:S(2)}, u32[]{:S(2)}) collective-permute-start(bf16[128,1152]{1,0:T(8,128)(2,1)S(1)} %get-tuple-element.93), channel_id=1, source_target_pairs={{0,3},{1,0},{2,1},{3,2},{4,7},{5,4},{6,5},{7,6},{8,11},{9,8},{10,9... | collective-permute-start | bytes 884744 | tf_op jit(solution)/shard_map/ppermute | solution.py:28
  85.8 4.5 %collective-permute-done.23.arrived_ref = bf16[128,1152]{1,0:T(8,128)(2,1)S(1)} collective-permute-done((bf16[128,1152]{1,0:T(8,128)(2,1)S(1)}, bf16[128,1152]{1,0:T(8,128)(2,1)S(1)}, u32[]{:S(2)}, u32[]{:S(2)}) %collective-permute-start.23) | collective-permute-done | bytes 294944 | tf_op jit(solution)/shard_map/ppermute | solution.py:28
  90.4 0.1 shard_map.100
  90.5 2.4 %collective-permute-start.24 = (bf16[64,1152]{1,0:T(8,128)(2,1)S(1)}, bf16[64,1152]{1,0:T(8,128)(2,1)S(1)}, u32[]{:S(2)}, u32[]{:S(2)}) collective-permute-start(bf16[64,1152]{1,0:T(8,128)(2,1)S(1)} %get-tuple-element.97), channel_id=1, source_target_pairs={{0,2},{1,3},{2,0},{3,1},{4,6},{5,7},{6,4},{7,5},{8,10},{9,11},{10,... | collective-permute-start | bytes 442376 | tf_op jit(solution)/shard_map/ppermute | solution.py:28
  92.9 0.4 collective-permute-start.25
  93.3 0.1 shard_map.99
  93.4 3.0 %collective-permute-start.26 = (bf16[64,1152]{1,0:T(8,128)(2,1)S(1)}, bf16[64,1152]{1,0:T(8,128)(2,1)S(1)}, u32[]{:S(2)}, u32[]{:S(2)}) collective-permute-start(bf16[64,1152]{1,0:T(8,128)(2,1)S(1)} %get-tuple-element.99), channel_id=1, source_target_pairs={{0,4},{1,5},{2,6},{3,7},{4,0},{5,1},{6,2},{7,3},{8,12},{9,13},{10,... | collective-permute-start | bytes 442376 | tf_op jit(solution)/shard_map/ppermute | solution.py:28
  96.5 2.2 %collective-permute-start.21 = (bf16[8,4,192]{2,1,0:T(4,128)(2,1)S(1)}, bf16[8,4,192]{2,1,0:T(4,128)(2,1)S(1)}, u32[]{:S(2)}, u32[]{:S(2)}) collective-permute-start(bf16[8,4,192]{2,1,0:T(4,128)(2,1)S(1)} %get-tuple-element.102), channel_id=1, source_target_pairs={{0,8},{8,0},{16,24},{24,16},{32,40},{40,32},{48,56},{56,48},{64,72... | collective-permute-start | bytes 36872 | tf_op jit(solution)/shard_map/ppermute | solution.py:28
  98.7 0.8 collective-permute-done.21
  99.6 0.6 copy.10
  100.2 0.8 shard_map.101
  (31 shorter events, 0.2 us)
Async XLA Ops:
  0.6 22.8 %collective-permute-start.9 = (bf16[1024,576]{0,1:T(8,128)(2,1)}, bf16[1024,576]{0,1:T(8,128)(2,1)S(1)}, u32[]{:S(2)}, u32[]{:S(2)}) collective-permute-start(bf16[1024,576]{0,1:T(8,128)(2,1)} %param.10), channel_id=1, source_target_pairs={{0,8},{8,0},{16,24},{24,16},{32,40},{40,32},{48,56},{56,48},{64,72... | collective-permute-start | bytes 3538952 | tf_op jit(solution)/shard_map/ppermute | solution.py:28
  4.7 0.8 copy-start.1
  5.5 0.7 copy-start.2
  6.2 0.7 copy-start.3
  7.5 1.2 %collective-permute-start = (bf16[32,384]{1,0:T(8,128)(2,1)S(1)}, bf16[32,384]{1,0:T(8,128)(2,1)S(1)}, u32[]{:S(2)}, u32[]{:S(2)}) collective-permute-start(bf16[32,384]{1,0:T(8,128)(2,1)S(1)} %get-tuple-element.52), channel_id=1, source_target_pairs={{0,8},{8,0},{16,24},{24,16},{32,40},{40,32},{48,56},{56,48},{64,72... | collective-permute-start | bytes 73736 | tf_op jit(solution)/shard_map/ppermute | solution.py:28
  8.7 2.9 %collective-permute-start.1 = (bf16[64,384]{1,0:T(8,128)(2,1)S(1)}, bf16[64,384]{1,0:T(8,128)(2,1)S(1)}, u32[]{:S(2)}, u32[]{:S(2)}) collective-permute-start(bf16[64,384]{1,0:T(8,128)(2,1)S(1)} %pad_maximum_fusion), channel_id=1, source_target_pairs={{0,16},{8,24},{16,0},{24,8},{32,48},{40,56},{48,32},{56,40},{64,80... | collective-permute-start | bytes 147464 | tf_op jit(solution)/shard_map/ppermute | solution.py:28
  11.7 7.5 %collective-permute-start.3 = (bf16[128,384]{1,0:T(8,128)(2,1)S(1)}, bf16[128,384]{1,0:T(8,128)(2,1)S(1)}, u32[]{:S(2)}, u32[]{:S(2)}) collective-permute-start(bf16[128,384]{1,0:T(8,128)(2,1)S(1)} %maximum_select_fusion.refs_0_), channel_id=1, source_target_pairs={{0,192},{8,200},{16,208},{24,216},{32,224},{40,232},{48,240},{56,2... | collective-permute-start | bytes 294920 | tf_op jit(solution)/shard_map/ppermute | solution.py:28
  16.0 7.4 %collective-permute-start.5 = (bf16[128,384]{1,0:T(8,128)(2,1)S(1)}, bf16[128,384]{1,0:T(8,128)(2,1)S(1)}, u32[]{:S(2)}, u32[]{:S(2)}) collective-permute-start(bf16[128,384]{1,0:T(8,128)(2,1)S(1)} %maximum_select_fusion.refs_0_), channel_id=1, source_target_pairs={{0,64},{8,72},{16,80},{24,88},{32,96},{40,104},{48,112},{56,120},{... | collective-permute-start | bytes 294920 | tf_op jit(solution)/shard_map/ppermute | solution.py:28
  16.0 10.1 %collective-permute-start.2 = (bf16[128,384]{1,0:T(8,128)(2,1)S(1)}, bf16[128,384]{1,0:T(8,128)(2,1)S(1)}, u32[]{:S(2)}, u32[]{:S(2)}) collective-permute-start(bf16[128,384]{1,0:T(8,128)(2,1)S(1)} %maximum_select_fusion.refs_0_), channel_id=1, source_target_pairs={{0,224},{8,232},{16,240},{24,248},{32,0},{40,8},{48,16},{56,24},{6... | collective-permute-start | bytes 294920 | tf_op jit(solution)/shard_map/ppermute | solution.py:28
  19.2 7.0 %collective-permute-start.8 = (bf16[128,384]{1,0:T(8,128)(2,1)S(1)}, bf16[128,384]{1,0:T(8,128)(2,1)S(1)}, u32[]{:S(2)}, u32[]{:S(2)}) collective-permute-start(bf16[128,384]{1,0:T(8,128)(2,1)S(1)} %maximum_select_fusion.refs_0_), channel_id=1, source_target_pairs={{0,32},{8,40},{16,48},{24,56},{32,64},{40,72},{48,80},{56,88},{64,... | collective-permute-start | bytes 294920 | tf_op jit(solution)/shard_map/ppermute | solution.py:28
  19.2 7.0 %collective-permute-start.4 = (bf16[128,384]{1,0:T(8,128)(2,1)S(1)}, bf16[128,384]{1,0:T(8,128)(2,1)S(1)}, u32[]{:S(2)}, u32[]{:S(2)}) collective-permute-start(bf16[128,384]{1,0:T(8,128)(2,1)S(1)} %collective-permute-done.3.refs_2_), channel_id=1, source_target_pairs={{0,224},{8,232},{16,240},{24,248},{32,0},{40,8},{48,16},{56,24},{6... | collective-permute-start | bytes 294920 | tf_op jit(solution)/shard_map/ppermute | solution.py:28
  23.4 6.0 %collective-permute-start.6 = (bf16[128,384]{1,0:T(8,128)(2,1)S(1)}, bf16[128,384]{1,0:T(8,128)(2,1)S(1)}, u32[]{:S(2)}, u32[]{:S(2)}) collective-permute-start(bf16[128,384]{1,0:T(8,128)(2,1)S(1)} %collective-permute-done.5.refs_6_), channel_id=1, source_target_pairs={{0,64},{8,72},{16,80},{24,88},{32,96},{40,104},{48,112},{56,120},{... | collective-permute-start | bytes 294920 | tf_op jit(solution)/shard_map/ppermute | solution.py:28
  23.4 6.4 %collective-permute-start.7 = (bf16[128,384]{1,0:T(8,128)(2,1)S(1)}, bf16[128,384]{1,0:T(8,128)(2,1)S(1)}, u32[]{:S(2)}, u32[]{:S(2)}) collective-permute-start(bf16[128,384]{1,0:T(8,128)(2,1)S(1)} %collective-permute-done.5.refs_6_), channel_id=1, source_target_pairs={{0,32},{8,40},{16,48},{24,56},{32,64},{40,72},{48,80},{56,88},{64,... | collective-permute-start | bytes 294920 | tf_op jit(solution)/shard_map/ppermute | solution.py:28
  24.0 1.3 %copy-start = (bf16[1024,576]{0,1:T(8,128)(2,1)S(1)}, bf16[1024,576]{0,1:T(8,128)(2,1)}, u32[]{:S(2)}) copy-start(bf16[1024,576]{0,1:T(8,128)(2,1)} %param.10) | copy-start | bytes 3538948
  25.3 4.5 %copy-start.5 = (bf16[16,512,256]{2,1,0:T(8,128)(2,1)S(1)}, bf16[16,512,256]{2,1,0:T(8,128)(2,1)}, u32[]{:S(2)}) copy-start(bf16[16,512,256]{2,1,0:T(8,128)(2,1)} %refs_8_.1) | copy-start | bytes 12582916
  40.2 5.5 %collective-permute-start.10 = (f32[3,1024]{1,0:T(4,128)S(1)}, f32[3,1024]{1,0:T(4,128)S(1)}, u32[]{:S(2)}, u32[]{:S(2)}) collective-permute-start(f32[3,1024]{1,0:T(4,128)S(1)} %get-tuple-element.56.refs_0_.refs_4_), channel_id=1, source_target_pairs={{0,16},{8,24},{16,0},{24,8},{32,48},{40,56},{48,32},{56,40},{64,80... | collective-permute-start | bytes 36872 | tf_op jit(solution)/shard_map/ppermute | solution.py:28
  41.7 4.1 %collective-permute-start.11 = (f32[3,1024]{1,0:T(4,128)S(1)}, f32[3,1024]{1,0:T(4,128)S(1)}, u32[]{:S(2)}, u32[]{:S(2)}) collective-permute-start(f32[3,1024]{1,0:T(4,128)S(1)} %get-tuple-element.56.refs_0_.refs_4_), channel_id=1, source_target_pairs={{0,32},{8,40},{16,48},{24,56},{32,0},{40,8},{48,16},{56,24},{64,96... | collective-permute-start | bytes 36872 | tf_op jit(solution)/shard_map/ppermute | solution.py:28
  41.8 3.9 %collective-permute-start.12 = (f32[3,1024]{1,0:T(4,128)S(1)}, f32[3,1024]{1,0:T(4,128)S(1)}, u32[]{:S(2)}, u32[]{:S(2)}) collective-permute-start(f32[3,1024]{1,0:T(4,128)S(1)} %get-tuple-element.56.refs_0_.refs_4_), channel_id=1, source_target_pairs={{0,48},{8,56},{16,32},{24,40},{32,16},{40,24},{48,0},{56,8},{64,11... | collective-permute-start | bytes 36872 | tf_op jit(solution)/shard_map/ppermute | solution.py:28
  45.8 8.4 %copy-start.4 = (s32[4]{0:T(128)S(1)}, s32[4]{0:T(128)}, u32[]{:S(2)}) copy-start(s32[4]{0:T(128)} %lens_ref.1) | copy-start | bytes 52
  45.8 8.3 %collective-permute-start.13 = (f32[3,1024]{1,0:T(4,128)S(1)}, f32[3,1024]{1,0:T(4,128)S(1)}, u32[]{:S(2)}, u32[]{:S(2)}) collective-permute-start(f32[3,1024]{1,0:T(4,128)S(1)} %shard_map.91.refs_0_), channel_id=1, source_target_pairs={{0,64},{8,72},{16,80},{24,88},{32,96},{40,104},{48,112},{56,120},{... | collective-permute-start | bytes 36872 | tf_op jit(solution)/shard_map/ppermute | solution.py:28
  45.9 8.3 %collective-permute-start.14 = (f32[3,1024]{1,0:T(4,128)S(1)}, f32[3,1024]{1,0:T(4,128)S(1)}, u32[]{:S(2)}, u32[]{:S(2)}) collective-permute-start(f32[3,1024]{1,0:T(4,128)S(1)} %shard_map.91.refs_0_), channel_id=1, source_target_pairs={{0,128},{8,136},{16,144},{24,152},{32,160},{40,168},{48,176},{56,1... | collective-permute-start | bytes 36872 | tf_op jit(solution)/shard_map/ppermute | solution.py:28
  48.9 5.2 %collective-permute-start.15 = (f32[3,1024]{1,0:T(4,128)S(1)}, f32[3,1024]{1,0:T(4,128)S(1)}, u32[]{:S(2)}, u32[]{:S(2)}) collective-permute-start(f32[3,1024]{1,0:T(4,128)S(1)} %shard_map.91.refs_0_), channel_id=1, source_target_pairs={{0,192},{8,200},{16,208},{24,216},{32,224},{40,232},{48,240},{56,2... | collective-permute-start | bytes 36872 | tf_op jit(solution)/shard_map/ppermute | solution.py:28
  57.3 14.2 %collective-permute-start.20 = (bf16[8,4,16,192]{3,2,1,0:T(8,128)(2,1)S(1)}, bf16[8,4,16,192]{3,2,1,0:T(8,128)(2,1)S(1)}, u32[]{:S(2)}, u32[]{:S(2)}) collective-permute-start(bf16[8,4,16,192]{3,2,1,0:T(8,128)(2,1)S(1)} %get-tuple-element.90), channel_id=1, source_target_pairs={{0,16},{8,24},{16,0},{24,8},{32,48},{40,56},{48,32},{56,40},{64,80... | collective-permute-start | bytes 589832 | tf_op jit(solution)/shard_map/ppermute | solution.py:28
  61.0 11.3 %collective-permute-start.16 = (bf16[128,1152]{1,0:T(8,128)(2,1)S(1)}, bf16[128,1152]{1,0:T(8,128)(2,1)S(1)}, u32[]{:S(2)}, u32[]{:S(2)}) collective-permute-start(bf16[128,1152]{1,0:T(8,128)(2,1)S(1)} %get-tuple-element.75), channel_id=1, source_target_pairs={{0,8},{8,0},{16,24},{24,16},{32,40},{40,32},{48,56},{56,48},{64,72... | collective-permute-start | bytes 884744 | tf_op jit(solution)/shard_map/ppermute | solution.py:28
  68.2 4.1 %collective-permute-start.17 = (bf16[128,1152]{1,0:T(8,128)(2,1)S(1)}, bf16[128,1152]{1,0:T(8,128)(2,1)S(1)}, u32[]{:S(2)}, u32[]{:S(2)}) collective-permute-start(bf16[128,1152]{1,0:T(8,128)(2,1)S(1)} %get-tuple-element.76), channel_id=1, source_target_pairs={{0,8},{8,0},{16,24},{24,16},{32,40},{40,32},{48,56},{56,48},{64,72... | collective-permute-start | bytes 884744 | tf_op jit(solution)/shard_map/ppermute | solution.py:28
  70.7 4.0 %collective-permute-start.18 = (bf16[128,1152]{1,0:T(8,128)(2,1)S(1)}, bf16[128,1152]{1,0:T(8,128)(2,1)S(1)}, u32[]{:S(2)}, u32[]{:S(2)}) collective-permute-start(bf16[128,1152]{1,0:T(8,128)(2,1)S(1)} %get-tuple-element.80), channel_id=1, source_target_pairs={{0,8},{8,0},{16,24},{24,16},{32,40},{40,32},{48,56},{56,48},{64,72... | collective-permute-start | bytes 884744 | tf_op jit(solution)/shard_map/ppermute | solution.py:28
  71.4 3.3 %collective-permute-start.19 = (bf16[128,1152]{1,0:T(8,128)(2,1)S(1)}, bf16[128,1152]{1,0:T(8,128)(2,1)S(1)}, u32[]{:S(2)}, u32[]{:S(2)}) collective-permute-start(bf16[128,1152]{1,0:T(8,128)(2,1)S(1)} %get-tuple-element.81), channel_id=1, source_target_pairs={{0,8},{8,0},{16,24},{24,16},{32,40},{40,32},{48,56},{56,48},{64,72... | collective-permute-start | bytes 884744 | tf_op jit(solution)/shard_map/ppermute | solution.py:28
  77.2 19.2 %all-to-all-start = ((bf16[8,4,16,192]{3,2,1,0:T(8,128)(2,1)}), bf16[8,4,16,192]{3,2,1,0:T(8,128)(2,1)S(1)}, u32[]{:S(2)}, u32[]{:S(2)}) async-start(bf16[8,4,16,192]{3,2,1,0:T(8,128)(2,1)} %add_convert_fusion), calls=%async_computation | async-start | bytes 524288 | tf_op jit(solution)/shard_map/all_to_all | solution.py:584
  80.6 9.7 %collective-permute-start.23 = (bf16[128,1152]{1,0:T(8,128)(2,1)S(1)}, bf16[128,1152]{1,0:T(8,128)(2,1)S(1)}, u32[]{:S(2)}, u32[]{:S(2)}) collective-permute-start(bf16[128,1152]{1,0:T(8,128)(2,1)S(1)} %get-tuple-element.96), channel_id=1, source_target_pairs={{0,4},{1,5},{2,6},{3,7},{4,0},{5,1},{6,2},{7,3},{8,12},{9,13},{10,... | collective-permute-start | bytes 884744 | tf_op jit(solution)/shard_map/ppermute | solution.py:28
  83.1 10.2 %collective-permute-start.22 = (bf16[128,1152]{1,0:T(8,128)(2,1)S(1)}, bf16[128,1152]{1,0:T(8,128)(2,1)S(1)}, u32[]{:S(2)}, u32[]{:S(2)}) collective-permute-start(bf16[128,1152]{1,0:T(8,128)(2,1)S(1)} %get-tuple-element.93), channel_id=1, source_target_pairs={{0,3},{1,0},{2,1},{3,2},{4,7},{5,4},{6,5},{7,6},{8,11},{9,8},{10,9... | collective-permute-start | bytes 884744 | tf_op jit(solution)/shard_map/ppermute | solution.py:28
  90.5 9.7 %collective-permute-start.24 = (bf16[64,1152]{1,0:T(8,128)(2,1)S(1)}, bf16[64,1152]{1,0:T(8,128)(2,1)S(1)}, u32[]{:S(2)}, u32[]{:S(2)}) collective-permute-start(bf16[64,1152]{1,0:T(8,128)(2,1)S(1)} %get-tuple-element.97), channel_id=1, source_target_pairs={{0,2},{1,3},{2,0},{3,1},{4,6},{5,7},{6,4},{7,5},{8,10},{9,11},{10,... | collective-permute-start | bytes 442376 | tf_op jit(solution)/shard_map/ppermute | solution.py:28
  92.9 7.3 %collective-permute-start.25 = (bf16[64,1152]{1,0:T(8,128)(2,1)S(1)}, bf16[64,1152]{1,0:T(8,128)(2,1)S(1)}, u32[]{:S(2)}, u32[]{:S(2)}) collective-permute-start(bf16[64,1152]{1,0:T(8,128)(2,1)S(1)} %get-tuple-element.98), channel_id=1, source_target_pairs={{0,1},{1,2},{2,3},{3,0},{4,5},{5,6},{6,7},{7,4},{8,9},{9,10},{10,1... | collective-permute-start | bytes 442376 | tf_op jit(solution)/shard_map/ppermute | solution.py:28
  93.4 6.8 %collective-permute-start.26 = (bf16[64,1152]{1,0:T(8,128)(2,1)S(1)}, bf16[64,1152]{1,0:T(8,128)(2,1)S(1)}, u32[]{:S(2)}, u32[]{:S(2)}) collective-permute-start(bf16[64,1152]{1,0:T(8,128)(2,1)S(1)} %get-tuple-element.99), channel_id=1, source_target_pairs={{0,4},{1,5},{2,6},{3,7},{4,0},{5,1},{6,2},{7,3},{8,12},{9,13},{10,... | collective-permute-start | bytes 442376 | tf_op jit(solution)/shard_map/ppermute | solution.py:28
  96.5 3.1 %collective-permute-start.21 = (bf16[8,4,192]{2,1,0:T(4,128)(2,1)S(1)}, bf16[8,4,192]{2,1,0:T(4,128)(2,1)S(1)}, u32[]{:S(2)}, u32[]{:S(2)}) collective-permute-start(bf16[8,4,192]{2,1,0:T(4,128)(2,1)S(1)} %get-tuple-element.102), channel_id=1, source_target_pairs={{0,8},{8,0},{16,24},{24,16},{32,40},{40,32},{48,56},{56,48},{64,72... | collective-permute-start | bytes 36872 | tf_op jit(solution)/shard_map/ppermute | solution.py:28

commit v4 on v3

--- a/solution.py
+++ b/solution.py
@@ -15,8 +15,7 @@
 F32 = jnp.float32
 BF16 = jnp.bfloat16
 CHUNK = 1024
-TOGETHER = 4
-PACKED = 384
+PAIR_LANES = 640
 MIB = 1024 * 1024
 ATTEND_MIB = 24
 PROJECT_MIB = 10
@@ -39,7 +38,8 @@
 def join_stats(first, second):
     top = jnp.maximum(first[0:1], second[0:1])
     both = jnp.exp2(first[0:1] - top) * first + jnp.exp2(second[0:1] - top) * second
-    return jnp.where(lax.broadcasted_iota(jnp.int32, both.shape, 0) == 0, top, both)
+    row = lax.broadcasted_iota(jnp.int32, both.shape, 0)
+    return jnp.where(row == 0, top, jnp.where(row == 3, first + second, both))
 
 
 def join_kernel(*refs):
@@ -61,95 +61,120 @@
     return lax.dot_general(x, y, (((1,), (1,)), ((), ())), preferred_element_type=F32)
 
 
-def pack_kernel(where_ref, ratio_ref, queries_ref, out_grad_ref, mine_ref, theirs_ref):
+def pack_kernel(where_ref, queries_ref, out_grad_ref, mine_ref, theirs_ref, wide, rows):
     q_dev, heads, q_width = queries_ref.shape
     d_nope = out_grad_ref.shape[2]
-    half = heads // 2
     d_rope = q_width - d_nope
-    lane = lax.broadcasted_iota(jnp.int32, (heads, PACKED - 2 * d_nope - d_rope), 1)
-    second = where_ref[0] == 1
-    mine, theirs = [], []
+    pairs = heads // 4
     for j in range(q_dev):
-        query = queries_ref[j].astype(F32)
-        ratio = jnp.full(lane.shape, ratio_ref[j], F32)
-        high = ratio.astype(BF16).astype(F32)
-        middle = (ratio - high).astype(BF16).astype(F32)
-        terms = jnp.where(lane == 0, high, jnp.where(lane == 1, middle, ratio - high - middle))
-        terms = jnp.where(lane < 3, terms, 0.0)
-        row = [query[:, :d_nope], out_grad_ref[j].astype(F32), query[:, d_nope:], terms]
-        row = jnp.concatenate(row, axis=1)
-        mine.append(jnp.where(second, row[half:], row[:half]))
-        theirs.append(jnp.where(second, row[:half], row[half:]))
-    mine_ref[...] = jnp.concatenate(mine, axis=0).astype(BF16)
-    theirs_ref[...] = jnp.concatenate(theirs, axis=0).astype(BF16)
-
-
-def pack(where, token_ratio, queries, out_grad):
-    q_dev, heads = queries.shape[:2]
+        wide[j, :, :q_width] = queries_ref[j].astype(F32)
+        wide[j, :, 2 * d_nope :] = out_grad_ref[j].astype(F32)
+        for half in range(2):
+            for second in range(2):
+                first = (2 * half + second) * pairs
+                of = slice(first, first + pairs)
+                to = slice(j * pairs, (j + 1) * pairs)
+                lane = 2 * d_nope * second
+                rows[half, to, lane : lane + d_nope] = wide[j, of, :d_nope]
+                rows[half, to, lane + d_nope : lane + 2 * d_nope] = wide[j, of, 2 * d_nope :]
+                lane = 4 * d_nope + d_rope * second
+                rows[half, to, lane : lane + d_rope] = wide[j, of, d_nope:q_width]
+    other = where_ref[0] == 1
+    mine_ref[...] = jnp.where(other, rows[1], rows[0]).astype(BF16)
+    theirs_ref[...] = jnp.where(other, rows[0], rows[1]).astype(BF16)
+
+
+def pack(where, queries, out_grad):
+    q_dev, heads, d_nope = out_grad.shape
     smem = pl.BlockSpec(memory_space=pltpu.SMEM)
     vmem = pl.BlockSpec(memory_space=pltpu.VMEM)
-    packed = jax.ShapeDtypeStruct((q_dev * heads // 2, PACKED), BF16)
+    size = q_dev * heads // 4
+    packed = jax.ShapeDtypeStruct((size, PAIR_LANES), BF16)
     return pl.pallas_call(
         pack_kernel,
         out_shape=(packed, packed),
-        in_specs=[smem, smem, vmem, vmem],
+        in_specs=[smem, vmem, vmem],
         out_specs=[vmem, vmem],
+        scratch_shapes=[
+            pltpu.VMEM((q_dev, heads, 3 * d_nope), F32),
+            pltpu.VMEM((2, size, PAIR_LANES), F32),
+        ],
         compiler_params=pltpu.CompilerParams(vmem_limit_bytes=2 * MIB),
         cost_estimate=pl.CostEstimate(flops=0, bytes_accessed=32 * MIB, transcendentals=0),
-    )(where, token_ratio, queries, out_grad)
-
-
-def stage_kernel(cache_ref, *refs):
-    refs[-1][...] = cache_ref[...].T
-    if len(refs) == 3:
-        own_ref, both_ref = refs[:2]
-        keys = own_ref.shape[1]
-        both_ref[:, :keys] = own_ref[...]
-        both_ref[:, keys:] = cache_ref[...]
-
-
-def stage(cache_t, own_t=None):
+    )(where, queries, out_grad)
+
+
+def stage_kernel(cache_ref, out_ref):
+    out_ref[...] = cache_ref[...].T
+
+
+def stage_all_kernel(where_ref, cache_ref, own_ref, kv_ref, out_ref, both_ref, key_ref):
+    keys = own_ref.shape[1]
+    half, _, d_nope = key_ref.shape
+    out_ref[...] = cache_ref[...].T
+    both_ref[:, :keys] = own_ref[...]
+    both_ref[:, keys:] = cache_ref[...]
+    for h in range(half):
+        key_ref[h] = kv_ref[where_ref[0] * half + h, :, :d_nope]
+
+
+def stage(cache_t):
     c_width, keys = cache_t.shape
     vmem = pl.BlockSpec(memory_space=pltpu.VMEM)
-    turned = jax.ShapeDtypeStruct((keys, c_width), BF16)
-    both = jax.ShapeDtypeStruct((c_width, 2 * keys), BF16)
-    operands, outs = ((cache_t,), (turned,)) if own_t is None else ((cache_t, own_t), (both, turned))
     return pl.pallas_call(
         stage_kernel,
-        out_shape=outs,
-        in_specs=[vmem] * len(operands),
-        out_specs=[vmem] * len(outs),
-        compiler_params=pltpu.CompilerParams(vmem_limit_bytes=10 * MIB),
+        out_shape=jax.ShapeDtypeStruct((keys, c_width), BF16),
+        in_specs=[vmem],
+        out_specs=vmem,
+        compiler_params=pltpu.CompilerParams(vmem_limit_bytes=6 * MIB),
         cost_estimate=pl.CostEstimate(
             flops=keys * c_width, bytes_accessed=4 * keys * c_width, transcendentals=0
         ),
-    )(*operands)
+    )(cache_t)
+
+
+def stage_all(where, cache_t, own_t, kv_up):
+    c_width, keys = cache_t.shape
+    heads, d_lat, width = kv_up.shape
+    smem = pl.BlockSpec(memory_space=pltpu.SMEM)
+    vmem = pl.BlockSpec(memory_space=pltpu.VMEM)
+    return pl.pallas_call(
+        stage_all_kernel,
+        out_shape=(
+            jax.ShapeDtypeStruct((keys, c_width), BF16),
+            jax.ShapeDtypeStruct((c_width, 2 * keys), BF16),
+            jax.ShapeDtypeStruct((heads // 2, d_lat, width // 2), BF16),
+        ),
+        in_specs=[smem] + [vmem] * 3,
+        out_specs=[vmem] * 3,
+        compiler_params=pltpu.CompilerParams(vmem_limit_bytes=16 * MIB),
+        cost_estimate=pl.CostEstimate(
+            flops=keys * c_width, bytes_accessed=8 * keys * c_width, transcendentals=0
+        ),
+    )(where, cache_t, own_t, kv_up)
 
 
 def attend_kernel(score_scale, blocks, together, where_ref, *refs):
     ring_refs, refs = refs[:blocks], refs[blocks:]
-    kv_ref, own_ref, other_ref, query_ref, grad_ref, expo_ref, spread_ref, stats_ref = refs[:8]
-    ratio_ref, key_ref, raw, expo, dprod = refs[8:]
+    kv_ref, key_ref, own_ref, other_ref, ratio_ref = refs[:5]
+    query_ref, grad_ref, expo_ref, spread_ref, stats_ref, raw, expo, dprod = refs[5:]
     size = ring_refs[0].shape[0]
     half, d_lat, d_nope = kv_ref.shape[0] // 2, kv_ref.shape[1], kv_ref.shape[2] // 2
-    rows = size * blocks // half
+    pairs = half // 2
+    rows = size * blocks // pairs
     first_head = where_ref[0] * half
     d_rope = query_ref.shape[1] - d_lat
     keys = own_ref.shape[0]
     width = together * rows
     for k in range(blocks):
         first = pl.multiple_of(where_ref[4 + k] * size, size)
-        for part in range(PACKED // 128):
+        for part in range(PAIR_LANES // 128):
             lanes = slice(part * 128, (part + 1) * 128)
             raw[part, pl.ds(first, size), :] = ring_refs[k][:, lanes].astype(F32)
-
-    def of_head(h, part):
-        return raw[part, pl.ds(h, rows, stride=half), :]
-
-    terms = of_head(0, 2)
-    lane = lax.broadcasted_iota(jnp.int32, terms.shape, 1)
-    terms = jnp.where((lane >= d_rope) & (lane < d_rope + 3), terms, 0.0)
-    ratio_ref[...] = jnp.broadcast_to(jnp.sum(terms, axis=1, keepdims=True), ratio_ref.shape)
+    stats_ref[3:4] = ratio_ref[...]
+
+    def of_pair(j, part):
+        return raw[part, pl.ds(j, rows, stride=pairs), :]
 
     def fold(x, join):
         return join(join(x.reshape(CHUNK // 8, 8, width), axis=0), axis=0, keepdims=True)
@@ -158,12 +183,12 @@
         for j in range(together):
             h = p * together + j
             at = pl.ds(pl.multiple_of(h * rows, rows), rows)
-            key_ref[h] = kv_ref[first_head + h, :, :d_nope]
-            lat = against(of_head(h, 0).astype(BF16), key_ref[h])
+            lat = against(of_pair(j, 2 * p).astype(BF16), key_ref[h])
             query_ref[at, :d_lat] = lat.astype(BF16)
-            rope = of_head(h, 2)[:, :d_rope]
+            rope = of_pair(j, 4)
+            rope = jnp.where(p == 0, rope[:, :d_rope], rope[:, d_rope:])
             query_ref[at, d_lat:] = rope.astype(BF16)
-            lat = against(of_head(h, 1).astype(BF16), kv_ref[first_head + h, :, d_nope:])
+            lat = against(of_pair(j, 2 * p + 1).astype(BF16), kv_ref[first_head + h, :, d_nope:])
             grad_ref[at, :] = lat.astype(BF16)
         columns = pl.ds(pl.multiple_of(p * width, width), width)
         tops, masses, dsums = [], [], []
@@ -200,11 +225,12 @@
     lax.fori_loop(0, half // together, group, 0)
 
 
-def attend(where, ring, kv_up, own, other, score_scale, together=TOGETHER):
-    blocks, (size, packed) = len(ring), ring[0].shape
+def attend(where, ring, kv_up, w_key, own, other, ratio, score_scale):
+    blocks, size = len(ring), ring[0].shape[0]
     half, d_lat = kv_up.shape[0] // 2, kv_up.shape[1]
-    total = blocks * size
-    rows = total // half
+    together = half // 2
+    rows = blocks * size // together
+    total = half * rows
     keys, c_width = own.shape
     smem = pl.BlockSpec(memory_space=pltpu.SMEM)
     vmem = pl.BlockSpec(memory_space=pltpu.VMEM)
@@ -215,14 +241,12 @@
             jax.ShapeDtypeStruct((total, d_lat), BF16),
             jax.ShapeDtypeStruct((2 * keys, total), BF16),
             jax.ShapeDtypeStruct((2 * keys, total), BF16),
-            jax.ShapeDtypeStruct((3, total), F32),
-            jax.ShapeDtypeStruct((rows, 128), F32),
-            jax.ShapeDtypeStruct((half, d_lat, kv_up.shape[2] // 2), BF16),
-        ),
-        in_specs=[smem] + [vmem] * (blocks + 3),
-        out_specs=[vmem] * 7,
+            jax.ShapeDtypeStruct((4, total), F32),
+        ),
+        in_specs=[smem] + [vmem] * (blocks + 5),
+        out_specs=[vmem] * 5,
         scratch_shapes=[
-            pltpu.VMEM((packed // 128, total, 128), F32),
+            pltpu.VMEM((PAIR_LANES // 128, blocks * size, 128), F32),
             pltpu.VMEM((2 * keys, together * rows), F32),
             pltpu.VMEM((2 * keys, together * rows), F32),
         ],
@@ -232,7 +256,7 @@
             bytes_accessed=8 * keys * total,
             transcendentals=2 * keys * total,
         ),
-    )(where, *ring, kv_up, own, other)
+    )(where, *ring, kv_up, w_key, own, other, ratio)
 
 
 def project_kernel(p, cache_ref, spread_ref, expo_ref, *out_refs):
@@ -260,13 +284,11 @@
     )(cache_t, spread, expo)
 
 
-def row_gains(where_ref, lens_ref, ratio_ref, rows_of_core):
-    rows = ratio_ref.shape[0]
-    place = lax.broadcasted_iota(jnp.int32, (rows, 1), 0)
+def row_gains(where_ref, lens_ref, ratio, rows_of_core):
+    place = lax.broadcasted_iota(jnp.int32, ratio.shape, 1)
     turn = place % (2 * rows_of_core) >= rows_of_core
     swapped = jnp.where(turn, place - rows_of_core, place + rows_of_core)
     place = jnp.where(where_ref[0] == 1, swapped, place)
-    ratio = ratio_ref[:, 0:1]
     segments = lens_ref.shape[0]
     members = []
     first = jnp.int32(0)
@@ -274,8 +296,8 @@
         last = first + lens_ref[k]
         members.append((place >= first) & (place < last))
         first = last
-    sums = [jnp.sum(jnp.where(m, ratio, 0.0), axis=0, keepdims=True) for m in members]
-    gains = jnp.zeros((rows, 1), F32)
+    sums = [jnp.sum(jnp.where(m, ratio, 0.0), axis=1, keepdims=True) for m in members]
+    gains = jnp.zeros(ratio.shape, F32)
     for p in range(segments // 2):
         margin = BETA * (sums[2 * p] - sums[2 * p + 1])
         weight = LOSS_SCALE * BETA / (1.0 + jnp.exp(margin))
@@ -288,18 +310,17 @@
     joined = functools.reduce(join_stats, [ref[...] for ref in joined_refs])
     centre = own_ref[2:3] / jnp.maximum(own_ref[1:2], 1e-30)
     factor = jnp.exp2(own_ref[0:1] - joined[0:1]) / joined[1:2]
-    return factor, joined[2:3] / joined[1:2] - centre
-
-
-def weigh_kernel(scale, rows_of_core, where_ref, lens_ref, *refs):
-    joined_refs, (own_ref, ratio_ref, query_ref, grad_ref) = refs[:4], refs[4:8]
-    with_spread_ref, with_expo_ref, factors_ref = refs[8:]
+    return joined[3:4], factor, joined[2:3] / joined[1:2] - centre
+
+
+def weigh_kernel(scale, rows, rows_of_core, where_ref, lens_ref, *refs):
+    joined_refs, (own_ref, query_ref, grad_ref) = refs[:4], refs[4:7]
+    with_spread_ref, with_expo_ref, factors_ref = refs[7:]
     total = query_ref.shape[0]
     d_lat = grad_ref.shape[1]
-    rows = ratio_ref.shape[0]
-    gains = row_gains(where_ref, lens_ref, ratio_ref, rows_of_core)
-    factor, shift = row_factors(joined_refs, own_ref)
-    gains_row = jnp.broadcast_to(gains, (rows, 128)).T[0:1]
+    ratio, factor, shift = row_factors(joined_refs, own_ref)
+    gains_row = row_gains(where_ref, lens_ref, ratio[:, :rows], rows_of_core)
+    gains = jnp.broadcast_to(gains_row, (8, rows)).T[:, 0:1]
     gains_row = jnp.concatenate([gains_row] * (total // rows), axis=1)
     factors_ref[0:1] = scale * gains_row * factor
     factors_ref[1:2] = shift
@@ -317,14 +338,14 @@
         with_expo_ref[at, d_lat:] = (-moved[:, d_lat:]).astype(BF16)
 
 
-def weigh(where, lens, joined, stats, ratio, query, grad, scale, q_dev):
+def weigh(where, lens, joined, stats, query, grad, scale, rows, q_dev):
     total, c_width = query.shape
     smem = pl.BlockSpec(memory_space=pltpu.SMEM)
     vmem = pl.BlockSpec(memory_space=pltpu.VMEM)
     weight = jax.ShapeDtypeStruct((total, c_width), BF16)
-    inputs = (*joined, stats, ratio, query, grad)
-    return pl.pallas_call(
-        functools.partial(weigh_kernel, scale, q_dev),
+    inputs = (*joined, stats, query, grad)
+    return pl.pallas_call(
+        functools.partial(weigh_kernel, scale, rows, q_dev),
         out_shape=(weight, weight, jax.ShapeDtypeStruct((2, total), F32)),
         in_specs=[smem, smem] + [vmem] * len(inputs),
         out_specs=[vmem] * 3,
@@ -509,11 +530,15 @@
     where = jnp.stack(where).astype(jnp.int32)
     own_t = latent_cache.T
     other_t = permute(latent_cache, "ctx", other_core).T
-    mine, theirs = pack(where, token_ratio, queries, out_grad)
+    rows = 4 * nz * q_dev
+    ratio = jnp.concatenate([token_ratio, permute(token_ratio, "ctx", other_core)])
+    chip = jnp.arange(half * rows, dtype=jnp.int32)[None, :] // (2 * q_dev) == ctx_index // 2
+    ratio = jnp.where(chip, jnp.tile(ratio, half * rows // (2 * q_dev))[None, :], 0.0)
+    mine, theirs = pack(where, queries, out_grad)
     block = jnp.concatenate([mine, permute(theirs, "ctx", other_core)], 0)
     block = in_order(block, permute(block, "ctx", other_x_lo), x_lo == 1, 0)
-    (own_keys,) = stage(own_t)
-    cache_t, other_keys = stage(other_t, own_t)
+    own_keys = stage(own_t)
+    other_keys, cache_t, w_key = stage_all(where, other_t, own_t, kv_up)
     along_z = lambda x, k: permute(x, "ctx", lambda i: (i + 4 * k) % (4 * nz))
     ring = [block] + [None] * (nz - 1)
     ring[nz - 2], ring[2] = along_z(block, 2), along_z(block, -2)
@@ -521,8 +546,8 @@
     ring[nz - 4] = along_z(ring[nz - 2], 2)
     ring[nz - 3], ring[3] = along_z(ring[nz - 2], 1), along_z(ring[2], -1)
 
-    query, grad, expo, spread, stats, ratio, w_key = attend(
-        where, ring, kv_up, own_keys, other_keys, scale * LOG2E
+    query, grad, expo, spread, stats = attend(
+        where, ring, kv_up, w_key, own_keys, other_keys, ratio, scale * LOG2E
     )
 
     joined = [stats]
@@ -536,7 +561,7 @@
         projected += joined[len(partners) :]
         joined = (mine, *joined[: len(partners)])
     with_spread, with_expo, factors = weigh(
-        where, pair_lens, joined, stats, ratio, query, grad, scale, q_dev
+        where, pair_lens, joined, stats, query, grad, scale, rows, q_dev
     )
     dq_keep, dq_send = query_terms(where, factors, w_key, projected, nz, q_width)
     dq_pair = permute(dq_send, "ctx", other_x_lo)

time: 102 us -> 101 us (level)
  waiting for transfers between devices: 13.1 us -> 9.92 us
  local copies, waits for them, and re-layouts: 4.32 us -> 6.34 us
  Pallas kernels: 30.9 us -> 32.4 us
    ppermute x27 -> x28, waiting for transfers between devices: 13.1 us -> 9.91 us  [permute(): lax.ppermute(x, axis, [(i, to(i)) for i in range(lax.axis_size(axis))])]
    unnamed x13 -> x17, local copies, waits for them, and re-layouts: 4.03 us -> 5.94 us
    pallas_call x4, Pallas kernels: 3.22 us -> 4.89 us  [the longest x1 2.1 us: stage_all(): pl.pallas_call(stage_all_kernel, out_shape=(jax.ShapeDtypeStruct((keys, c...]
    ppermute x27 -> x28, starting transfers between devices: 46.8 us -> 45.9 us  [permute(): lax.ppermute(x, axis, [(i, to(i)) for i in range(lax.axis_size(axis))])]
  transfers between devices with their start and end apart: 28 -> 29, of which waited for: 6 -> 6; matrix products, arithmetic and copies ran while one was open for 2% -> 2% of each run, Pallas kernels for 14% -> 16%
where the time goes in v4:
time: 101 us; the launch traced here: 100 us
  starting transfers between devices  49.3 us (49%)
  Pallas kernels  32.4 us (32%)
  waiting for transfers between devices  9.92 us (10%)
  local copies, waits for them, and re-layouts  6.34 us (6%)
  between operations  1.56 us (2%)
    ppermute x28, starting transfers between devices, permute(): lax.ppermute(x, axis, [(i, to(i)) for i in range(lax.axis_size(axis))])  45.9 us
    pallas_call x1, Pallas kernels, attend(): pl.pallas_call(functools.partial(attend_kernel, score_scale, blocks, toge...  10.1 us
    ppermute x28, waiting for transfers between devices, permute(): lax.ppermute(x, axis, [(i, to(i)) for i in range(lax.axis_size(axis))])  9.91 us
    pallas_call x4, Pallas kernels, cache_terms(): pl.pallas_call(functools.partial(cache_kernel, part, d_lat), out_shape=[j...  9.69 us
    unnamed x17, local copies, waits for them, and re-layouts  5.94 us
    pallas_call x2, Pallas kernels, project(): pl.pallas_call(functools.partial(project_kernel, p), out_shape=(jax.Shape...  5.19 us
    all_to_all x1, starting transfers between devices, per_device(): dq = lax.all_to_all(dq, 'ctx', 0, 0, axis_index_groups=z_groups)  3.42 us
    pallas_call x1, Pallas kernels, stage_all(): pl.pallas_call(stage_all_kernel, out_shape=(jax.ShapeDtypeStruct((keys, c...  2.1 us
  transfers between devices with their start and end apart: 29, of which 6 were waited for; matrix products, arithmetic and copies ran while one was open for 2% of the time, Pallas kernels for 16%

profile of v4, /device:TPU:1, one launch (start us, length us, event | category | flops | bytes accessed | tf_op | source)
XLA Modules:
  0.0 100.5 jit_solution(10578822978931247681)
XLA Ops:
  0.6 3.3 %collective-permute-start.9 = (bf16[1024,576]{0,1:T(8,128)(2,1)}, bf16[1024,576]{0,1:T(8,128)(2,1)}, u32[]{:S(2)}, u32[]{:S(2)}) collective-permute-start(bf16[1024,576]{0,1:T(8,128)(2,1)} %param.10), channel_id=1, source_target_pairs={{0,8},{8,0},{16,24},{24,16},{32,40},{40,32},{48,56},{56,48},{64,72... | collective-permute-start | bytes 3538952 | tf_op jit(solution)/shard_map/ppermute | solution.py:27
  4.6 0.1 stack.93.where_ref
  4.7 0.0 copy-start.4
  4.7 0.8 copy-done.4
  5.5 0.7 copy-done.5
  6.2 0.6 shard_map.86
  6.8 0.1 collective-permute-start
  6.9 1.2 %collective-permute-done = bf16[16,640]{1,0:T(8,128)(2,1)S(1)} collective-permute-done((bf16[16,640]{1,0:T(8,128)(2,1)S(1)}, bf16[16,640]{1,0:T(8,128)(2,1)S(1)}, u32[]{:S(2)}, u32[]{:S(2)}) %collective-permute-start) | collective-permute-done | bytes 20512 | tf_op jit(solution)/shard_map/ppermute | solution.py:27
  8.1 0.0 collective-permute-start.1
  8.1 0.2 collective-permute-start.10
  8.3 0.1 stack.80.order_ref
  8.4 0.1 stack.77.order_ref
  8.5 1.3 %copy-done = bf16[1024,576]{0,1:T(8,128)(2,1)S(1)} copy-done((bf16[1024,576]{0,1:T(8,128)(2,1)S(1)}, bf16[1024,576]{0,1:T(8,128)(2,1)}, u32[]{:S(2)}) %copy-start) | copy-done | bytes 1179672
  9.8 0.4 shard_map.88.refs_10_
  10.2 0.8 collective-permute-done.1
  11.0 5.0 %collective-permute-start.3 = (bf16[64,640]{1,0:T(8,128)(2,1)S(1)}, bf16[64,640]{1,0:T(8,128)(2,1)S(1)}, u32[]{:S(2)}, u32[]{:S(2)}) collective-permute-start(bf16[64,640]{1,0:T(8,128)(2,1)S(1)} %maximum_select_fusion.refs_0_), channel_id=1, source_target_pairs={{0,192},{8,200},{16,208},{24,216},{32,224},{40,232},{48,240},{56,2... | collective-permute-start | bytes 245768 | tf_op jit(solution)/shard_map/ppermute | solution.py:27
  16.0 0.1 pad_maximum_fusion.1
  16.1 0.1 broadcast_in_dim_tile.3
  16.2 3.2 %collective-permute-start.2 = (bf16[64,640]{1,0:T(8,128)(2,1)S(1)}, bf16[64,640]{1,0:T(8,128)(2,1)S(1)}, u32[]{:S(2)}, u32[]{:S(2)}) collective-permute-start(bf16[64,640]{1,0:T(8,128)(2,1)S(1)} %maximum_select_fusion.refs_0_), channel_id=1, source_target_pairs={{0,224},{8,232},{16,240},{24,248},{32,0},{40,8},{48,16},{56,24},{6... | collective-permute-start | bytes 245768 | tf_op jit(solution)/shard_map/ppermute | solution.py:27
  19.4 0.0 collective-permute-start.8
  19.4 2.4 %collective-permute-done.5.refs_6_ = bf16[64,640]{1,0:T(8,128)(2,1)S(1)} collective-permute-done((bf16[64,640]{1,0:T(8,128)(2,1)S(1)}, bf16[64,640]{1,0:T(8,128)(2,1)S(1)}, u32[]{:S(2)}, u32[]{:S(2)}) %collective-permute-start.5) | collective-permute-done | bytes 81952 | tf_op jit(solution)/shard_map/ppermute | solution.py:27
  21.8 1.7 %collective-permute-start.7 = (bf16[64,640]{1,0:T(8,128)(2,1)S(1)}, bf16[64,640]{1,0:T(8,128)(2,1)S(1)}, u32[]{:S(2)}, u32[]{:S(2)}) collective-permute-start(bf16[64,640]{1,0:T(8,128)(2,1)S(1)} %collective-permute-done.5.refs_6_), channel_id=1, source_target_pairs={{0,32},{8,40},{16,48},{24,56},{32,64},{40,72},{48,80},{56,88},{64,... | collective-permute-start | bytes 245768 | tf_op jit(solution)/shard_map/ppermute | solution.py:27
  23.5 2.7 %collective-permute-start.4 = (bf16[64,640]{1,0:T(8,128)(2,1)S(1)}, bf16[64,640]{1,0:T(8,128)(2,1)S(1)}, u32[]{:S(2)}, u32[]{:S(2)}) collective-permute-start(bf16[64,640]{1,0:T(8,128)(2,1)S(1)} %collective-permute-done.3.refs_2_), channel_id=1, source_target_pairs={{0,224},{8,232},{16,240},{24,248},{32,0},{40,8},{48,16},{56,24},{6... | collective-permute-start | bytes 245768 | tf_op jit(solution)/shard_map/ppermute | solution.py:27
  26.2 0.0 copy-start.2
  26.2 2.2 %copy-done.2 = bf16[16,512,256]{2,1,0:T(8,128)(2,1)S(1)} copy-done((bf16[16,512,256]{2,1,0:T(8,128)(2,1)S(1)}, bf16[16,512,256]{2,1,0:T(8,128)(2,1)}, u32[]{:S(2)}) %copy-start.2) | copy-done | bytes 4194328
  28.4 2.1 %shard_map.87 = (bf16[1024,576]{1,0:T(8,128)(2,1)S(1)}, bf16[576,2048]{1,0:T(8,128)(2,1)S(1)}, bf16[8,512,128]{2,1,0:T(8,128)(2,1)S(1)}) custom-call(s32[13]{0:T(128)S(1)} %stack.93.where_ref, bf16[576,1024]{1,0:T(8,128)(2,1)} %bitcast.18.cache_ref, bf16[576,1024]{1,0:T(8,128)(2,1)S(1)} %bitcast.40, bf16[16,512,256]{2,1,0:T(8,128)(2,1)S(1)} %copy-done.2), custom_call_target="tpu_custom_call" | custom-call | flops 589824 | bytes 4718592 | tf_op jit(solution)/shard_map/pallas_call | solution.py:141
  30.5 0.4 copy-done.3
  30.9 10.1 %shard_map.89 = (bf16[1024,576]{1,0:T(8,128)(2,1)S(1)}, bf16[1024,512]{1,0:T(8,128)(2,1)S(1)}, bf16[2048,1024]{1,0:T(8,128)(2,1)S(1)}, bf16[2048,1024]{1,0:T(8,128)(2,1)S(1)}, f32[4,1024]{1,0:T(4,128)S(1)}) custom-call(s32[13]{0:T(128)S(1)} %stack.93.where_ref, bf16[64,640]{1,0:T(8,128)(2,1)S(1)} %maximum_select_fusion.refs_0_, ...), custom_call_target="tpu_custom_call" | custom-call | flops 4563402752 | bytes 8388608 | tf_op jit(solution)/shard_map/pallas_call | solution.py:237
  41.0 0.2 collective-permute-start.11
  41.2 0.0 collective-permute-start.12
  41.2 2.5 %collective-permute-start.13 = (f32[4,1024]{1,0:T(4,128)S(1)}, f32[4,1024]{1,0:T(4,128)S(1)}, u32[]{:S(2)}, u32[]{:S(2)}) collective-permute-start(f32[4,1024]{1,0:T(4,128)S(1)} %get-tuple-element.56.refs_0_.refs_4_), channel_id=1, source_target_pairs={{0,48},{8,56},{16,32},{24,40},{32,16},{40,24},{48,0},{56,8},{64,11... | collective-permute-start | bytes 49160 | tf_op jit(solution)/shard_map/ppermute | solution.py:27
  43.7 2.6 %shard_map.90 = (f32[576,512]{1,0:T(8,128)S(1)}, f32[576,512]{1,0:T(8,128)S(1)}) custom-call(bf16[576,2048]{1,0:T(8,128)(2,1)S(1)} %get-tuple-element.57.cache_ref, bf16[2048,1024]{1,0:T(8,128)(2,1)S(1)} %get-tuple-element.54.spread_ref, bf16[2048,1024]{1,0:T(8,128)(2,1)S(1)} %get-tuple-element.55.expo_ref), custom_call_target="tpu_custom_call" | custom-call | flops 2415919104 | bytes 4194304 | tf_op jit(solution)/shard_map/pallas_call | solution.py:275
  46.4 0.1 shard_map.91.refs_0_
  46.4 0.0 copy-start.6
  46.4 0.1 collective-permute-start.14
  46.5 3.0 %collective-permute-start.15 = (f32[4,1024]{1,0:T(4,128)S(1)}, f32[4,1024]{1,0:T(4,128)S(1)}, u32[]{:S(2)}, u32[]{:S(2)}) collective-permute-start(f32[4,1024]{1,0:T(4,128)S(1)} %shard_map.91.refs_0_), channel_id=1, source_target_pairs={{0,128},{8,136},{16,144},{24,152},{32,160},{40,168},{48,176},{56,1... | collective-permute-start | bytes 49160 | tf_op jit(solution)/shard_map/ppermute | solution.py:27
  49.5 2.6 %collective-permute-start.16 = (f32[4,1024]{1,0:T(4,128)S(1)}, f32[4,1024]{1,0:T(4,128)S(1)}, u32[]{:S(2)}, u32[]{:S(2)}) collective-permute-start(f32[4,1024]{1,0:T(4,128)S(1)} %shard_map.91.refs_0_), channel_id=1, source_target_pairs={{0,192},{8,200},{16,208},{24,216},{32,224},{40,232},{48,240},{56,2... | collective-permute-start | bytes 49160 | tf_op jit(solution)/shard_map/ppermute | solution.py:27
  52.2 2.6 %shard_map.92 = (f32[576,512]{1,0:T(8,128)S(1)}, f32[576,512]{1,0:T(8,128)S(1)}) custom-call(bf16[576,2048]{1,0:T(8,128)(2,1)S(1)} %get-tuple-element.57.cache_ref, bf16[2048,1024]{1,0:T(8,128)(2,1)S(1)} %get-tuple-element.54.spread_ref, bf16[2048,1024]{1,0:T(8,128)(2,1)S(1)} %get-tuple-element.55.expo_ref), custom_call_target="tpu_custom_call" | custom-call | flops 2415919104 | bytes 4194304 | tf_op jit(solution)/shard_map/pallas_call | solution.py:275
  54.8 1.8 %shard_map.93 = (bf16[1024,576]{1,0:T(8,128)(2,1)S(1)}, bf16[1024,576]{1,0:T(8,128)(2,1)S(1)}, f32[2,1024]{1,0:T(2,128)S(1)}) custom-call(s32[13]{0:T(128)S(1)} %stack.93.where_ref, s32[4]{0:T(128)S(1)} %copy-done.6, f32[4,1024]{1,0:T(4,128)S(1)} %shard_map.91.refs_0_, f32[4,1024]{1,0:T(4,128)S(1)} %collective-permute-done.14.refs_1_, ...), custom_call_target="tpu_custom_call" | custom-call | flops 5898240 | bytes 4718592 | tf_op jit(solution)/shard_map/pallas_call | solution.py:347
  56.6 1.4 %shard_map.98 = (bf16[8,4,16,192]{3,2,1,0:T(8,128)(2,1)S(1)}, bf16[8,4,16,192]{3,2,1,0:T(8,128)(2,1)S(1)}) custom-call(s32[13]{0:T(128)S(1)} %stack.93.where_ref, f32[2,1024]{1,0:T(2,128)S(1)} %get-tuple-element.82.factors_ref, bf16[8,512,128]{2,1,0:T(8,128)(2,1)S(1)} %get-tuple-element.52.refs_9_.key_ref, f32[576,512]{1,0:T(8,128)S(1)} %get-tuple-element.83.refs_0_, ...), custom_call_target="tpu_custom_call" | custom-call | flops 268435456 | bytes 4194304 | tf_op jit(solution)/shard_map/pallas_call | solution.py:399
  58.0 0.6 collective-permute-start.21
  58.6 2.4 %shard_map.94 = (bf16[128,1152]{1,0:T(8,128)(2,1)S(1)}, bf16[128,1152]{1,0:T(8,128)(2,1)S(1)}) custom-call(s32[8]{0:T(128)S(1)} %stack.80.order_ref, bf16[2,2,4,128,1024]{4,3,2,1,0:T(8,128)(2,1)S(1)} %bitcast.35, bf16[2,2,4,128,1024]{4,3,2,1,0:T(8,128)(2,1)S(1)} %bitcast.31, bf16[1024,576]{1,0:T(8,128)(2,1)S(1)} %get-tuple-element.70.with_spread_ref, ...), custom_call_target="tpu_custom_call" | custom-call | flops 1207959552 | bytes 2097152 | tf_op jit(solution)/shard_map/pallas_call | solution.py:439
  61.1 6.5 %collective-permute-start.17 = (bf16[128,1152]{1,0:T(8,128)(2,1)S(1)}, bf16[128,1152]{1,0:T(8,128)(2,1)S(1)}, u32[]{:S(2)}, u32[]{:S(2)}) collective-permute-start(bf16[128,1152]{1,0:T(8,128)(2,1)S(1)} %get-tuple-element.74), channel_id=1, source_target_pairs={{0,8},{8,0},{16,24},{24,16},{32,40},{40,32},{48,56},{56,48},{64,72... | collective-permute-start | bytes 884744 | tf_op jit(solution)/shard_map/ppermute | solution.py:27
  67.5 0.1 collective-permute-start.18
  67.6 2.4 %shard_map.96 = (bf16[128,1152]{1,0:T(8,128)(2,1)S(1)}, bf16[128,1152]{1,0:T(8,128)(2,1)S(1)}) custom-call(s32[8]{0:T(128)S(1)} %stack.77.order_ref, bf16[2,2,4,128,1024]{4,3,2,1,0:T(8,128)(2,1)S(1)} %bitcast.36, bf16[2,2,4,128,1024]{4,3,2,1,0:T(8,128)(2,1)S(1)} %bitcast.32, bf16[1024,576]{1,0:T(8,128)(2,1)S(1)} %get-tuple-element.70.with_spread_ref, ...), custom_call_target="tpu_custom_call" | custom-call | flops 1207959552 | bytes 2097152 | tf_op jit(solution)/shard_map/pallas_call | solution.py:439
  70.1 0.5 collective-permute-start.19
  70.6 0.1 collective-permute-start.20
  70.7 0.8 add_convert_fusion
  71.5 2.4 %shard_map.95 = (bf16[128,1152]{1,0:T(8,128)(2,1)S(1)}, f32[128,1152]{1,0:T(8,128)S(1)}) custom-call(s32[8]{0:T(128)S(1)} %stack.80.order_ref, bf16[2,2,4,128,1024]{4,3,2,1,0:T(8,128)(2,1)S(1)} %bitcast.37, bf16[2,2,4,128,1024]{4,3,2,1,0:T(8,128)(2,1)S(1)} %bitcast.33, bf16[1024,576]{1,0:T(8,128)(2,1)S(1)} %get-tuple-element.70.with_spread_ref, ...), custom_call_target="tpu_custom_call" | custom-call | flops 1207959552 | bytes 2097152 | tf_op jit(solution)/shard_map/pallas_call | solution.py:439
  73.9 2.4 %shard_map.97 = (bf16[128,1152]{1,0:T(8,128)(2,1)S(1)}, f32[128,1152]{1,0:T(8,128)S(1)}) custom-call(s32[8]{0:T(128)S(1)} %stack.77.order_ref, bf16[2,2,4,128,1024]{4,3,2,1,0:T(8,128)(2,1)S(1)} %bitcast.38, bf16[2,2,4,128,1024]{4,3,2,1,0:T(8,128)(2,1)S(1)} %bitcast.34, bf16[1024,576]{1,0:T(8,128)(2,1)S(1)} %get-tuple-element.70.with_spread_ref, ...), custom_call_target="tpu_custom_call" | custom-call | flops 1207959552 | bytes 2097152 | tf_op jit(solution)/shard_map/pallas_call | solution.py:439
  76.3 3.4 %all-to-all-start = ((bf16[8,4,16,192]{3,2,1,0:T(8,128)(2,1)}), bf16[8,4,16,192]{3,2,1,0:T(8,128)(2,1)S(1)}, u32[]{:S(2)}, u32[]{:S(2)}) async-start(bf16[8,4,16,192]{3,2,1,0:T(8,128)(2,1)} %add_convert_fusion), calls=%async_computation | async-start | bytes 524288 | tf_op jit(solution)/shard_map/all_to_all | solution.py:609
  79.8 2.6 %collective-permute-start.24 = (bf16[128,1152]{1,0:T(8,128)(2,1)S(1)}, bf16[128,1152]{1,0:T(8,128)(2,1)S(1)}, u32[]{:S(2)}, u32[]{:S(2)}) collective-permute-start(bf16[128,1152]{1,0:T(8,128)(2,1)S(1)} %get-tuple-element.94), channel_id=1, source_target_pairs={{0,4},{1,5},{2,6},{3,7},{4,0},{5,1},{6,2},{7,3},{8,12},{9,13},{10,... | collective-permute-start | bytes 884744 | tf_op jit(solution)/shard_map/ppermute | solution.py:27
  82.3 2.7 %collective-permute-start.23 = (bf16[128,1152]{1,0:T(8,128)(2,1)S(1)}, bf16[128,1152]{1,0:T(8,128)(2,1)S(1)}, u32[]{:S(2)}, u32[]{:S(2)}) collective-permute-start(bf16[128,1152]{1,0:T(8,128)(2,1)S(1)} %get-tuple-element.91), channel_id=1, source_target_pairs={{0,3},{1,0},{2,1},{3,2},{4,7},{5,4},{6,5},{7,6},{8,11},{9,8},{10,9... | collective-permute-start | bytes 884744 | tf_op jit(solution)/shard_map/ppermute | solution.py:27
  85.1 4.5 %collective-permute-done.24.arrived_ref = bf16[128,1152]{1,0:T(8,128)(2,1)S(1)} collective-permute-done((bf16[128,1152]{1,0:T(8,128)(2,1)S(1)}, bf16[128,1152]{1,0:T(8,128)(2,1)S(1)}, u32[]{:S(2)}, u32[]{:S(2)}) %collective-permute-start.24) | collective-permute-done | bytes 294944 | tf_op jit(solution)/shard_map/ppermute | solution.py:27
  89.5 0.1 shard_map.100
  89.7 3.0 %collective-permute-start.25 = (bf16[64,1152]{1,0:T(8,128)(2,1)S(1)}, bf16[64,1152]{1,0:T(8,128)(2,1)S(1)}, u32[]{:S(2)}, u32[]{:S(2)}) collective-permute-start(bf16[64,1152]{1,0:T(8,128)(2,1)S(1)} %get-tuple-element.95), channel_id=1, source_target_pairs={{0,2},{1,3},{2,0},{3,1},{4,6},{5,7},{6,4},{7,5},{8,10},{9,11},{10,... | collective-permute-start | bytes 442376 | tf_op jit(solution)/shard_map/ppermute | solution.py:27
  92.6 0.4 collective-permute-start.26
  93.0 0.1 shard_map.99
  93.1 2.3 %collective-permute-start.27 = (bf16[64,1152]{1,0:T(8,128)(2,1)S(1)}, bf16[64,1152]{1,0:T(8,128)(2,1)S(1)}, u32[]{:S(2)}, u32[]{:S(2)}) collective-permute-start(bf16[64,1152]{1,0:T(8,128)(2,1)S(1)} %get-tuple-element.97), channel_id=1, source_target_pairs={{0,4},{1,5},{2,6},{3,7},{4,0},{5,1},{6,2},{7,3},{8,12},{9,13},{10,... | collective-permute-start | bytes 442376 | tf_op jit(solution)/shard_map/ppermute | solution.py:27
  95.5 2.5 %collective-permute-start.22 = (bf16[8,4,192]{2,1,0:T(4,128)(2,1)S(1)}, bf16[8,4,192]{2,1,0:T(4,128)(2,1)S(1)}, u32[]{:S(2)}, u32[]{:S(2)}) collective-permute-start(bf16[8,4,192]{2,1,0:T(4,128)(2,1)S(1)} %get-tuple-element.100), channel_id=1, source_target_pairs={{0,8},{8,0},{16,24},{24,16},{32,40},{40,32},{48,56},{56,48},{64,72... | collective-permute-start | bytes 36872 | tf_op jit(solution)/shard_map/ppermute | solution.py:27
  98.0 0.8 collective-permute-done.22
  98.8 0.6 copy.10
  99.5 0.2 collective-permute-done.26.refs_1_
  99.7 0.8 shard_map.101
  (41 shorter events, 0.2 us)
Async XLA Ops:
  0.6 22.9 %collective-permute-start.9 = (bf16[1024,576]{0,1:T(8,128)(2,1)}, bf16[1024,576]{0,1:T(8,128)(2,1)}, u32[]{:S(2)}, u32[]{:S(2)}) collective-permute-start(bf16[1024,576]{0,1:T(8,128)(2,1)} %param.10), channel_id=1, source_target_pairs={{0,8},{8,0},{16,24},{24,16},{32,40},{40,32},{48,56},{56,48},{64,72... | collective-permute-start | bytes 3538952 | tf_op jit(solution)/shard_map/ppermute | solution.py:27
  4.7 0.8 copy-start.4
  5.5 0.7 copy-start.5
  6.8 1.3 %collective-permute-start = (bf16[16,640]{1,0:T(8,128)(2,1)S(1)}, bf16[16,640]{1,0:T(8,128)(2,1)S(1)}, u32[]{:S(2)}, u32[]{:S(2)}) collective-permute-start(bf16[16,640]{1,0:T(8,128)(2,1)S(1)} %get-tuple-element.51), channel_id=1, source_target_pairs={{0,8},{8,0},{16,24},{24,16},{32,40},{40,32},{48,56},{56,48},{64,72... | collective-permute-start | bytes 61448 | tf_op jit(solution)/shard_map/ppermute | solution.py:27
  8.1 2.9 %collective-permute-start.1 = (bf16[32,640]{1,0:T(8,128)(2,1)S(1)}, bf16[32,640]{1,0:T(8,128)(2,1)S(1)}, u32[]{:S(2)}, u32[]{:S(2)}) collective-permute-start(bf16[32,640]{1,0:T(8,128)(2,1)S(1)} %pad_maximum_fusion), channel_id=1, source_target_pairs={{0,16},{8,24},{16,0},{24,8},{32,48},{40,56},{48,32},{56,40},{64,80... | collective-permute-start | bytes 122888 | tf_op jit(solution)/shard_map/ppermute | solution.py:27
  8.1 7.9 %collective-permute-start.10 = (f32[4]{0:T(128)}, f32[4]{0:T(128)S(1)}, u32[]{:S(2)}, u32[]{:S(2)}) collective-permute-start(f32[4]{0:T(128)} %param.11), channel_id=1, source_target_pairs={{0,8},{8,0},{16,24},{24,16},{32,40},{40,32},{48,56},{56,48},{64,72... | collective-permute-start | bytes 56 | tf_op jit(solution)/shard_map/ppermute | solution.py:27
  8.5 1.3 %copy-start = (bf16[1024,576]{0,1:T(8,128)(2,1)S(1)}, bf16[1024,576]{0,1:T(8,128)(2,1)}, u32[]{:S(2)}) copy-start(bf16[1024,576]{0,1:T(8,128)(2,1)} %param.10) | copy-start | bytes 3538948
  9.8 6.3 %copy-start.7 = (f32[4]{0:T(128)S(1)}, f32[4]{0:T(128)}, u32[]{:S(2)}) copy-start(f32[4]{0:T(128)} %param.11) | copy-start | bytes 52
  9.8 16.4 %copy-start.1 = (bf16[1024,576]{0,1:T(8,128)(2,1)S(1)}, bf16[1024,576]{0,1:T(8,128)(2,1)}, u32[]{:S(2)}) copy-start(bf16[1024,576]{0,1:T(8,128)(2,1)} %param.10) | copy-start | bytes 3538948
  11.0 10.8 %collective-permute-start.3 = (bf16[64,640]{1,0:T(8,128)(2,1)S(1)}, bf16[64,640]{1,0:T(8,128)(2,1)S(1)}, u32[]{:S(2)}, u32[]{:S(2)}) collective-permute-start(bf16[64,640]{1,0:T(8,128)(2,1)S(1)} %maximum_select_fusion.refs_0_), channel_id=1, source_target_pairs={{0,192},{8,200},{16,208},{24,216},{32,224},{40,232},{48,240},{56,2... | collective-permute-start | bytes 245768 | tf_op jit(solution)/shard_map/ppermute | solution.py:27
  16.0 5.8 %collective-permute-start.5 = (bf16[64,640]{1,0:T(8,128)(2,1)S(1)}, bf16[64,640]{1,0:T(8,128)(2,1)S(1)}, u32[]{:S(2)}, u32[]{:S(2)}) collective-permute-start(bf16[64,640]{1,0:T(8,128)(2,1)S(1)} %maximum_select_fusion.refs_0_), channel_id=1, source_target_pairs={{0,64},{8,72},{16,80},{24,88},{32,96},{40,104},{48,112},{56,120},{... | collective-permute-start | bytes 245768 | tf_op jit(solution)/shard_map/ppermute | solution.py:27
  16.2 14.3 %collective-permute-start.2 = (bf16[64,640]{1,0:T(8,128)(2,1)S(1)}, bf16[64,640]{1,0:T(8,128)(2,1)S(1)}, u32[]{:S(2)}, u32[]{:S(2)}) collective-permute-start(bf16[64,640]{1,0:T(8,128)(2,1)S(1)} %maximum_select_fusion.refs_0_), channel_id=1, source_target_pairs={{0,224},{8,232},{16,240},{24,248},{32,0},{40,8},{48,16},{56,24},{6... | collective-permute-start | bytes 245768 | tf_op jit(solution)/shard_map/ppermute | solution.py:27
  19.4 11.1 %collective-permute-start.8 = (bf16[64,640]{1,0:T(8,128)(2,1)S(1)}, bf16[64,640]{1,0:T(8,128)(2,1)S(1)}, u32[]{:S(2)}, u32[]{:S(2)}) collective-permute-start(bf16[64,640]{1,0:T(8,128)(2,1)S(1)} %maximum_select_fusion.refs_0_), channel_id=1, source_target_pairs={{0,32},{8,40},{16,48},{24,56},{32,64},{40,72},{48,80},{56,88},{64,... | collective-permute-start | bytes 245768 | tf_op jit(solution)/shard_map/ppermute | solution.py:27
  21.8 8.7 %collective-permute-start.6 = (bf16[64,640]{1,0:T(8,128)(2,1)S(1)}, bf16[64,640]{1,0:T(8,128)(2,1)S(1)}, u32[]{:S(2)}, u32[]{:S(2)}) collective-permute-start(bf16[64,640]{1,0:T(8,128)(2,1)S(1)} %collective-permute-done.5.refs_6_), channel_id=1, source_target_pairs={{0,64},{8,72},{16,80},{24,88},{32,96},{40,104},{48,112},{56,120},{... | collective-permute-start | bytes 245768 | tf_op jit(solution)/shard_map/ppermute | solution.py:27
  21.8 8.7 %collective-permute-start.7 = (bf16[64,640]{1,0:T(8,128)(2,1)S(1)}, bf16[64,640]{1,0:T(8,128)(2,1)S(1)}, u32[]{:S(2)}, u32[]{:S(2)}) collective-permute-start(bf16[64,640]{1,0:T(8,128)(2,1)S(1)} %collective-permute-done.5.refs_6_), channel_id=1, source_target_pairs={{0,32},{8,40},{16,48},{24,56},{32,64},{40,72},{48,80},{56,88},{64,... | collective-permute-start | bytes 245768 | tf_op jit(solution)/shard_map/ppermute | solution.py:27
  23.5 7.0 %collective-permute-start.4 = (bf16[64,640]{1,0:T(8,128)(2,1)S(1)}, bf16[64,640]{1,0:T(8,128)(2,1)S(1)}, u32[]{:S(2)}, u32[]{:S(2)}) collective-permute-start(bf16[64,640]{1,0:T(8,128)(2,1)S(1)} %collective-permute-done.3.refs_2_), channel_id=1, source_target_pairs={{0,224},{8,232},{16,240},{24,248},{32,0},{40,8},{48,16},{56,24},{6... | collective-permute-start | bytes 245768 | tf_op jit(solution)/shard_map/ppermute | solution.py:27
  26.2 2.2 %copy-start.2 = (bf16[16,512,256]{2,1,0:T(8,128)(2,1)S(1)}, bf16[16,512,256]{2,1,0:T(8,128)(2,1)}, u32[]{:S(2)}) copy-start(bf16[16,512,256]{2,1,0:T(8,128)(2,1)} %refs_8_.1) | copy-start | bytes 12582916
  28.4 2.5 %copy-start.3 = (bf16[16,512,256]{2,1,0:T(8,128)(2,1)S(1)}, bf16[16,512,256]{2,1,0:T(8,128)(2,1)}, u32[]{:S(2)}) copy-start(bf16[16,512,256]{2,1,0:T(8,128)(2,1)} %refs_8_.1) | copy-start | bytes 12582916
  41.0 5.3 %collective-permute-start.11 = (f32[4,1024]{1,0:T(4,128)S(1)}, f32[4,1024]{1,0:T(4,128)S(1)}, u32[]{:S(2)}, u32[]{:S(2)}) collective-permute-start(f32[4,1024]{1,0:T(4,128)S(1)} %get-tuple-element.56.refs_0_.refs_4_), channel_id=1, source_target_pairs={{0,16},{8,24},{16,0},{24,8},{32,48},{40,56},{48,32},{56,40},{64,80... | collective-permute-start | bytes 49160 | tf_op jit(solution)/shard_map/ppermute | solution.py:27
  41.2 5.2 %collective-permute-start.12 = (f32[4,1024]{1,0:T(4,128)S(1)}, f32[4,1024]{1,0:T(4,128)S(1)}, u32[]{:S(2)}, u32[]{:S(2)}) collective-permute-start(f32[4,1024]{1,0:T(4,128)S(1)} %get-tuple-element.56.refs_0_.refs_4_), channel_id=1, source_target_pairs={{0,32},{8,40},{16,48},{24,56},{32,0},{40,8},{48,16},{56,24},{64,96... | collective-permute-start | bytes 49160 | tf_op jit(solution)/shard_map/ppermute | solution.py:27
  41.2 5.2 %collective-permute-start.13 = (f32[4,1024]{1,0:T(4,128)S(1)}, f32[4,1024]{1,0:T(4,128)S(1)}, u32[]{:S(2)}, u32[]{:S(2)}) collective-permute-start(f32[4,1024]{1,0:T(4,128)S(1)} %get-tuple-element.56.refs_0_.refs_4_), channel_id=1, source_target_pairs={{0,48},{8,56},{16,32},{24,40},{32,16},{40,24},{48,0},{56,8},{64,11... | collective-permute-start | bytes 49160 | tf_op jit(solution)/shard_map/ppermute | solution.py:27
  46.4 8.4 %copy-start.6 = (s32[4]{0:T(128)S(1)}, s32[4]{0:T(128)}, u32[]{:S(2)}) copy-start(s32[4]{0:T(128)} %lens_ref.1) | copy-start | bytes 52
  46.4 8.3 %collective-permute-start.14 = (f32[4,1024]{1,0:T(4,128)S(1)}, f32[4,1024]{1,0:T(4,128)S(1)}, u32[]{:S(2)}, u32[]{:S(2)}) collective-permute-start(f32[4,1024]{1,0:T(4,128)S(1)} %shard_map.91.refs_0_), channel_id=1, source_target_pairs={{0,64},{8,72},{16,80},{24,88},{32,96},{40,104},{48,112},{56,120},{... | collective-permute-start | bytes 49160 | tf_op jit(solution)/shard_map/ppermute | solution.py:27
  46.5 8.3 %collective-permute-start.15 = (f32[4,1024]{1,0:T(4,128)S(1)}, f32[4,1024]{1,0:T(4,128)S(1)}, u32[]{:S(2)}, u32[]{:S(2)}) collective-permute-start(f32[4,1024]{1,0:T(4,128)S(1)} %shard_map.91.refs_0_), channel_id=1, source_target_pairs={{0,128},{8,136},{16,144},{24,152},{32,160},{40,168},{48,176},{56,1... | collective-permute-start | bytes 49160 | tf_op jit(solution)/shard_map/ppermute | solution.py:27
  49.5 5.3 %collective-permute-start.16 = (f32[4,1024]{1,0:T(4,128)S(1)}, f32[4,1024]{1,0:T(4,128)S(1)}, u32[]{:S(2)}, u32[]{:S(2)}) collective-permute-start(f32[4,1024]{1,0:T(4,128)S(1)} %shard_map.91.refs_0_), channel_id=1, source_target_pairs={{0,192},{8,200},{16,208},{24,216},{32,224},{40,232},{48,240},{56,2... | collective-permute-start | bytes 49160 | tf_op jit(solution)/shard_map/ppermute | solution.py:27
  58.0 12.7 %collective-permute-start.21 = (bf16[8,4,16,192]{3,2,1,0:T(8,128)(2,1)S(1)}, bf16[8,4,16,192]{3,2,1,0:T(8,128)(2,1)S(1)}, u32[]{:S(2)}, u32[]{:S(2)}) collective-permute-start(bf16[8,4,16,192]{3,2,1,0:T(8,128)(2,1)S(1)} %get-tuple-element.88), channel_id=1, source_target_pairs={{0,16},{8,24},{16,0},{24,8},{32,48},{40,56},{48,32},{56,40},{64,80... | collective-permute-start | bytes 589832 | tf_op jit(solution)/shard_map/ppermute | solution.py:27
  61.1 10.4 %collective-permute-start.17 = (bf16[128,1152]{1,0:T(8,128)(2,1)S(1)}, bf16[128,1152]{1,0:T(8,128)(2,1)S(1)}, u32[]{:S(2)}, u32[]{:S(2)}) collective-permute-start(bf16[128,1152]{1,0:T(8,128)(2,1)S(1)} %get-tuple-element.74), channel_id=1, source_target_pairs={{0,8},{8,0},{16,24},{24,16},{32,40},{40,32},{48,56},{56,48},{64,72... | collective-permute-start | bytes 884744 | tf_op jit(solution)/shard_map/ppermute | solution.py:27
  67.5 3.9 %collective-permute-start.18 = (bf16[128,1152]{1,0:T(8,128)(2,1)S(1)}, bf16[128,1152]{1,0:T(8,128)(2,1)S(1)}, u32[]{:S(2)}, u32[]{:S(2)}) collective-permute-start(bf16[128,1152]{1,0:T(8,128)(2,1)S(1)} %get-tuple-element.75), channel_id=1, source_target_pairs={{0,8},{8,0},{16,24},{24,16},{32,40},{40,32},{48,56},{56,48},{64,72... | collective-permute-start | bytes 884744 | tf_op jit(solution)/shard_map/ppermute | solution.py:27
  70.1 3.8 %collective-permute-start.19 = (bf16[128,1152]{1,0:T(8,128)(2,1)S(1)}, bf16[128,1152]{1,0:T(8,128)(2,1)S(1)}, u32[]{:S(2)}, u32[]{:S(2)}) collective-permute-start(bf16[128,1152]{1,0:T(8,128)(2,1)S(1)} %get-tuple-element.79), channel_id=1, source_target_pairs={{0,8},{8,0},{16,24},{24,16},{32,40},{40,32},{48,56},{56,48},{64,72... | collective-permute-start | bytes 884744 | tf_op jit(solution)/shard_map/ppermute | solution.py:27
  70.6 3.3 %collective-permute-start.20 = (bf16[128,1152]{1,0:T(8,128)(2,1)S(1)}, bf16[128,1152]{1,0:T(8,128)(2,1)S(1)}, u32[]{:S(2)}, u32[]{:S(2)}) collective-permute-start(bf16[128,1152]{1,0:T(8,128)(2,1)S(1)} %get-tuple-element.80), channel_id=1, source_target_pairs={{0,8},{8,0},{16,24},{24,16},{32,40},{40,32},{48,56},{56,48},{64,72... | collective-permute-start | bytes 884744 | tf_op jit(solution)/shard_map/ppermute | solution.py:27
  76.3 19.1 %all-to-all-start = ((bf16[8,4,16,192]{3,2,1,0:T(8,128)(2,1)}), bf16[8,4,16,192]{3,2,1,0:T(8,128)(2,1)S(1)}, u32[]{:S(2)}, u32[]{:S(2)}) async-start(bf16[8,4,16,192]{3,2,1,0:T(8,128)(2,1)} %add_convert_fusion), calls=%async_computation | async-start | bytes 524288 | tf_op jit(solution)/shard_map/all_to_all | solution.py:609
  79.8 9.8 %collective-permute-start.24 = (bf16[128,1152]{1,0:T(8,128)(2,1)S(1)}, bf16[128,1152]{1,0:T(8,128)(2,1)S(1)}, u32[]{:S(2)}, u32[]{:S(2)}) collective-permute-start(bf16[128,1152]{1,0:T(8,128)(2,1)S(1)} %get-tuple-element.94), channel_id=1, source_target_pairs={{0,4},{1,5},{2,6},{3,7},{4,0},{5,1},{6,2},{7,3},{8,12},{9,13},{10,... | collective-permute-start | bytes 884744 | tf_op jit(solution)/shard_map/ppermute | solution.py:27
  82.3 10.7 %collective-permute-start.23 = (bf16[128,1152]{1,0:T(8,128)(2,1)S(1)}, bf16[128,1152]{1,0:T(8,128)(2,1)S(1)}, u32[]{:S(2)}, u32[]{:S(2)}) collective-permute-start(bf16[128,1152]{1,0:T(8,128)(2,1)S(1)} %get-tuple-element.91), channel_id=1, source_target_pairs={{0,3},{1,0},{2,1},{3,2},{4,7},{5,4},{6,5},{7,6},{8,11},{9,8},{10,9... | collective-permute-start | bytes 884744 | tf_op jit(solution)/shard_map/ppermute | solution.py:27
  89.7 9.8 %collective-permute-start.25 = (bf16[64,1152]{1,0:T(8,128)(2,1)S(1)}, bf16[64,1152]{1,0:T(8,128)(2,1)S(1)}, u32[]{:S(2)}, u32[]{:S(2)}) collective-permute-start(bf16[64,1152]{1,0:T(8,128)(2,1)S(1)} %get-tuple-element.95), channel_id=1, source_target_pairs={{0,2},{1,3},{2,0},{3,1},{4,6},{5,7},{6,4},{7,5},{8,10},{9,11},{10,... | collective-permute-start | bytes 442376 | tf_op jit(solution)/shard_map/ppermute | solution.py:27
  92.6 7.0 %collective-permute-start.26 = (bf16[64,1152]{1,0:T(8,128)(2,1)S(1)}, bf16[64,1152]{1,0:T(8,128)(2,1)S(1)}, u32[]{:S(2)}, u32[]{:S(2)}) collective-permute-start(bf16[64,1152]{1,0:T(8,128)(2,1)S(1)} %get-tuple-element.96), channel_id=1, source_target_pairs={{0,1},{1,2},{2,3},{3,0},{4,5},{5,6},{6,7},{7,4},{8,9},{9,10},{10,1... | collective-permute-start | bytes 442376 | tf_op jit(solution)/shard_map/ppermute | solution.py:27
  93.1 6.5 %collective-permute-start.27 = (bf16[64,1152]{1,0:T(8,128)(2,1)S(1)}, bf16[64,1152]{1,0:T(8,128)(2,1)S(1)}, u32[]{:S(2)}, u32[]{:S(2)}) collective-permute-start(bf16[64,1152]{1,0:T(8,128)(2,1)S(1)} %get-tuple-element.97), channel_id=1, source_target_pairs={{0,4},{1,5},{2,6},{3,7},{4,0},{5,1},{6,2},{7,3},{8,12},{9,13},{10,... | collective-permute-start | bytes 442376 | tf_op jit(solution)/shard_map/ppermute | solution.py:27
  95.5 3.3 %collective-permute-start.22 = (bf16[8,4,192]{2,1,0:T(4,128)(2,1)S(1)}, bf16[8,4,192]{2,1,0:T(4,128)(2,1)S(1)}, u32[]{:S(2)}, u32[]{:S(2)}) collective-permute-start(bf16[8,4,192]{2,1,0:T(4,128)(2,1)S(1)} %get-tuple-element.100), channel_id=1, source_target_pairs={{0,8},{8,0},{16,24},{24,16},{32,40},{40,32},{48,56},{56,48},{64,72... | collective-permute-start | bytes 36872 | tf_op jit(solution)/shard_map/ppermute | solution.py:27

commit v5 on v4

--- a/solution.py
+++ b/solution.py
@@ -100,69 +100,69 @@
             pltpu.VMEM((2, size, PAIR_LANES), F32),
         ],
         compiler_params=pltpu.CompilerParams(vmem_limit_bytes=2 * MIB),
-        cost_estimate=pl.CostEstimate(flops=0, bytes_accessed=32 * MIB, transcendentals=0),
+        cost_estimate=pl.CostEstimate(flops=0, bytes_accessed=MIB, transcendentals=0),
     )(where, queries, out_grad)
 
 
-def stage_kernel(cache_ref, out_ref):
-    out_ref[...] = cache_ref[...].T
-
-
-def stage_all_kernel(where_ref, cache_ref, own_ref, kv_ref, out_ref, both_ref, key_ref):
-    keys = own_ref.shape[1]
+def stage_own_kernel(where_ref, cache_ref, kv_ref, out_ref, key_ref, value_ref):
     half, _, d_nope = key_ref.shape
     out_ref[...] = cache_ref[...].T
-    both_ref[:, :keys] = own_ref[...]
-    both_ref[:, keys:] = cache_ref[...]
     for h in range(half):
         key_ref[h] = kv_ref[where_ref[0] * half + h, :, :d_nope]
-
-
-def stage(cache_t):
-    c_width, keys = cache_t.shape
-    vmem = pl.BlockSpec(memory_space=pltpu.VMEM)
-    return pl.pallas_call(
-        stage_kernel,
-        out_shape=jax.ShapeDtypeStruct((keys, c_width), BF16),
-        in_specs=[vmem],
-        out_specs=vmem,
-        compiler_params=pltpu.CompilerParams(vmem_limit_bytes=6 * MIB),
-        cost_estimate=pl.CostEstimate(
-            flops=keys * c_width, bytes_accessed=4 * keys * c_width, transcendentals=0
-        ),
-    )(cache_t)
-
-
-def stage_all(where, cache_t, own_t, kv_up):
+        value_ref[h] = kv_ref[where_ref[0] * half + h, :, d_nope:]
+
+
+def stage_own(where, cache_t, kv_up):
     c_width, keys = cache_t.shape
     heads, d_lat, width = kv_up.shape
     smem = pl.BlockSpec(memory_space=pltpu.SMEM)
     vmem = pl.BlockSpec(memory_space=pltpu.VMEM)
-    return pl.pallas_call(
-        stage_all_kernel,
-        out_shape=(
-            jax.ShapeDtypeStruct((keys, c_width), BF16),
-            jax.ShapeDtypeStruct((c_width, 2 * keys), BF16),
-            jax.ShapeDtypeStruct((heads // 2, d_lat, width // 2), BF16),
-        ),
-        in_specs=[smem] + [vmem] * 3,
+    weight = jax.ShapeDtypeStruct((heads // 2, d_lat, width // 2), BF16)
+    return pl.pallas_call(
+        stage_own_kernel,
+        out_shape=(jax.ShapeDtypeStruct((keys, c_width), BF16), weight, weight),
+        in_specs=[smem, vmem, vmem],
         out_specs=[vmem] * 3,
         compiler_params=pltpu.CompilerParams(vmem_limit_bytes=16 * MIB),
         cost_estimate=pl.CostEstimate(
             flops=keys * c_width, bytes_accessed=8 * keys * c_width, transcendentals=0
         ),
-    )(where, cache_t, own_t, kv_up)
+    )(where, cache_t, kv_up)
+
+
+def stage_other_kernel(cache_ref, own_ref, out_ref, both_ref):
+    keys = own_ref.shape[1]
+    out_ref[...] = cache_ref[...].T
+    both_ref[:, :keys] = own_ref[...]
+    both_ref[:, keys:] = cache_ref[...]
+
+
+def stage_other(cache_t, own_t):
+    c_width, keys = cache_t.shape
+    vmem = pl.BlockSpec(memory_space=pltpu.VMEM)
+    return pl.pallas_call(
+        stage_other_kernel,
+        out_shape=(
+            jax.ShapeDtypeStruct((keys, c_width), BF16),
+            jax.ShapeDtypeStruct((c_width, 2 * keys), BF16),
+        ),
+        in_specs=[vmem] * 2,
+        out_specs=[vmem] * 2,
+        compiler_params=pltpu.CompilerParams(vmem_limit_bytes=10 * MIB),
+        cost_estimate=pl.CostEstimate(
+            flops=keys * c_width, bytes_accessed=4 * keys * c_width, transcendentals=0
+        ),
+    )(cache_t, own_t)
 
 
 def attend_kernel(score_scale, blocks, together, where_ref, *refs):
     ring_refs, refs = refs[:blocks], refs[blocks:]
-    kv_ref, key_ref, own_ref, other_ref, ratio_ref = refs[:5]
-    query_ref, grad_ref, expo_ref, spread_ref, stats_ref, raw, expo, dprod = refs[5:]
+    key_ref, value_ref, own_ref, other_ref, mine_ref, theirs_ref = refs[:6]
+    query_ref, grad_ref, expo_ref, spread_ref, stats_ref, raw, expo, dprod = refs[6:]
     size = ring_refs[0].shape[0]
-    half, d_lat, d_nope = kv_ref.shape[0] // 2, kv_ref.shape[1], kv_ref.shape[2] // 2
+    half, d_lat = key_ref.shape[:2]
     pairs = half // 2
     rows = size * blocks // pairs
-    first_head = where_ref[0] * half
     d_rope = query_ref.shape[1] - d_lat
     keys = own_ref.shape[0]
     width = together * rows
@@ -171,7 +171,14 @@
         for part in range(PAIR_LANES // 128):
             lanes = slice(part * 128, (part + 1) * 128)
             raw[part, pl.ds(first, size), :] = ring_refs[k][:, lanes].astype(F32)
-    stats_ref[3:4] = ratio_ref[...]
+    q_dev = mine_ref.shape[0]
+    lane = lax.broadcasted_iota(jnp.int32, (1, stats_ref.shape[1]), 1)
+    lane = lane - where_ref[5 + blocks] * (2 * q_dev)
+    ratio = jnp.zeros(lane.shape, F32)
+    for j in range(q_dev):
+        ratio = jnp.where(lane == j, mine_ref[j], ratio)
+        ratio = jnp.where(lane == q_dev + j, theirs_ref[j], ratio)
+    stats_ref[3:4] = ratio
 
     def of_pair(j, part):
         return raw[part, pl.ds(j, rows, stride=pairs), :]
@@ -188,7 +195,7 @@
             rope = of_pair(j, 4)
             rope = jnp.where(p == 0, rope[:, :d_rope], rope[:, d_rope:])
             query_ref[at, d_lat:] = rope.astype(BF16)
-            lat = against(of_pair(j, 2 * p + 1).astype(BF16), kv_ref[first_head + h, :, d_nope:])
+            lat = against(of_pair(j, 2 * p + 1).astype(BF16), value_ref[h])
             grad_ref[at, :] = lat.astype(BF16)
         columns = pl.ds(pl.multiple_of(p * width, width), width)
         tops, masses, dsums = [], [], []
@@ -225,9 +232,9 @@
     lax.fori_loop(0, half // together, group, 0)
 
 
-def attend(where, ring, kv_up, w_key, own, other, ratio, score_scale):
+def attend(where, ring, w_key, w_val, own, other, ratios, score_scale):
     blocks, size = len(ring), ring[0].shape[0]
-    half, d_lat = kv_up.shape[0] // 2, kv_up.shape[1]
+    half, d_lat = w_key.shape[:2]
     together = half // 2
     rows = blocks * size // together
     total = half * rows
@@ -243,7 +250,7 @@
             jax.ShapeDtypeStruct((2 * keys, total), BF16),
             jax.ShapeDtypeStruct((4, total), F32),
         ),
-        in_specs=[smem] + [vmem] * (blocks + 5),
+        in_specs=[smem] + [vmem] * (blocks + 4) + [smem] * 2,
         out_specs=[vmem] * 5,
         scratch_shapes=[
             pltpu.VMEM((PAIR_LANES // 128, blocks * size, 128), F32),
@@ -256,7 +263,7 @@
             bytes_accessed=8 * keys * total,
             transcendentals=2 * keys * total,
         ),
-    )(where, *ring, kv_up, w_key, own, other, ratio)
+    )(where, *ring, w_key, w_val, own, other, *ratios)
 
 
 def project_kernel(p, cache_ref, spread_ref, expo_ref, *out_refs):
@@ -408,12 +415,22 @@
     )(where, factors, w_key, *projected)
 
 
-def cache_kernel(part, d_lat, order_ref, spread_ref, expo_ref, with_spread_ref, with_expo_ref, *refs):
+def cache_kernel(
+    part, turn, d_lat, where_ref, spread_ref, expo_ref, with_spread_ref, with_expo_ref, *refs
+):
     adds, outs = refs[:-2], refs[-2:]
     keys = spread_ref.shape[3]
 
+    ny = spread_ref.shape[2]
+    y, here = where_ref[where_ref.shape[0] - 2], where_ref[where_ref.shape[0] - 1]
+    there = 1 - here
+    if turn == 0:
+        places = [(there, 2), (there, 1), (here, 2), (here, 1)]
+    else:
+        places = [(there, 3), (here, 3), (there, 0), (here, 0)]
+
     def gather(ref):
-        blocks = [ref[part, order_ref[i], order_ref[4 + i]] for i in range(4)]
+        blocks = [ref[part, x, (y + k) & (ny - 1)] for x, k in places]
         return jnp.concatenate(blocks, axis=0)
 
     out = jnp.dot(gather(spread_ref), with_spread_ref[...], preferred_element_type=F32)
@@ -431,13 +448,13 @@
             outs[i // 2][:, lanes] = value.astype(outs[i // 2].dtype)
 
 
-def cache_terms(part, order, d_lat, spread, expo, with_spread, with_expo, dtypes, adds=()):
+def cache_terms(part, turn, where, d_lat, spread, expo, with_spread, with_expo, dtypes, adds=()):
     total, c_width = with_spread.shape
     keys = spread.shape[3]
     smem = pl.BlockSpec(memory_space=pltpu.SMEM)
     vmem = pl.BlockSpec(memory_space=pltpu.VMEM)
     return pl.pallas_call(
-        functools.partial(cache_kernel, part, d_lat),
+        functools.partial(cache_kernel, part, turn, d_lat),
         out_shape=[jax.ShapeDtypeStruct((keys, 2 * c_width), dtype) for dtype in dtypes],
         in_specs=[smem] + [vmem] * (4 + len(adds)),
         out_specs=[vmem, vmem],
@@ -447,7 +464,7 @@
             bytes_accessed=16 * keys * total,
             transcendentals=0,
         ),
-    )(order, spread, expo, with_spread, with_expo, *adds)
+    )(where, spread, expo, with_spread, with_expo, *adds)
 
 
 def unfold(x, d_lat):
@@ -524,21 +541,24 @@
     d_nope = q_width - d_rope
     half = heads // 2
     scale = q_width ** (-0.5)
+    rows = 4 * nz * q_dev
 
     where = [core, ctx_index * p_dev, (ctx_index ^ 1) * p_dev, prompt_len[0]]
-    where = where + [(z + k) & (nz - 1) for k in range(nz)] + [x_lo]
+    where = where + [(z + k) & (nz - 1) for k in range(nz)]
+    where = where + [x_lo, ctx_index >> 1, y, x_hi]
     where = jnp.stack(where).astype(jnp.int32)
     own_t = latent_cache.T
     other_t = permute(latent_cache, "ctx", other_core).T
-    rows = 4 * nz * q_dev
-    ratio = jnp.concatenate([token_ratio, permute(token_ratio, "ctx", other_core)])
-    chip = jnp.arange(half * rows, dtype=jnp.int32)[None, :] // (2 * q_dev) == ctx_index // 2
-    ratio = jnp.where(chip, jnp.tile(ratio, half * rows // (2 * q_dev))[None, :], 0.0)
+    other_ratio = permute(token_ratio, "ctx", other_core)
     mine, theirs = pack(where, queries, out_grad)
     block = jnp.concatenate([mine, permute(theirs, "ctx", other_core)], 0)
-    block = in_order(block, permute(block, "ctx", other_x_lo), x_lo == 1, 0)
-    own_keys = stage(own_t)
-    other_keys, cache_t, w_key = stage_all(where, other_t, own_t, kv_up)
+    own_keys, w_key, w_val = stage_own(where, own_t, kv_up)
+    from_x_lo = permute(block, "ctx", other_x_lo)
+    from_x_lo, own_keys, w_key, w_val, other_ratio = lax.optimization_barrier(
+        (from_x_lo, own_keys, w_key, w_val, other_ratio)
+    )
+    block = in_order(block, from_x_lo, x_lo == 1, 0)
+    other_keys, cache_t = stage_other(other_t, own_t)
     along_z = lambda x, k: permute(x, "ctx", lambda i: (i + 4 * k) % (4 * nz))
     ring = [block] + [None] * (nz - 1)
     ring[nz - 2], ring[2] = along_z(block, 2), along_z(block, -2)
@@ -547,7 +567,7 @@
     ring[nz - 3], ring[3] = along_z(ring[nz - 2], 1), along_z(ring[2], -1)
 
     query, grad, expo, spread, stats = attend(
-        where, ring, kv_up, w_key, own_keys, other_keys, ratio, scale * LOG2E
+        where, ring, w_key, w_val, own_keys, other_keys, (token_ratio, other_ratio), scale * LOG2E
     )
 
     joined = [stats]
@@ -566,27 +586,20 @@
     dq_keep, dq_send = query_terms(where, factors, w_key, projected, nz, q_width)
     dq_pair = permute(dq_send, "ctx", other_x_lo)
     keys = p_dev // (2 * ny)
-    there, here = 1 - x_hi, x_hi
-    along = [(y + k) & (ny - 1) for k in (0, 1, 2, 3)]
-    orders = [
-        [there, there, here, here, along[2], along[1], along[2], along[1]],
-        [there, here, there, here, along[3], along[3], along[0], along[0]],
-    ]
-    orders = [jnp.stack(order).astype(jnp.int32) for order in orders]
     shape = (2, 2, ny, keys, spread.shape[1])
     operands = (d_lat, spread.reshape(shape), expo.reshape(shape), with_spread, with_expo)
     adds = []
-    sends = cache_terms(1, orders[0], *operands, (BF16, BF16))
-    later, *sends = lax.optimization_barrier((orders[1], *sends))
+    sends = cache_terms(1, 0, where, *operands, (BF16, BF16))
+    later, *sends = lax.optimization_barrier((where, *sends))
     adds.append([permute(x, "ctx", other_core) for x in sends])
-    sends = cache_terms(1, later, *operands, (BF16, BF16))
+    sends = cache_terms(1, 1, later, *operands, (BF16, BF16))
     adds.append([permute(x, "ctx", other_core) for x in sends])
     to_x_hi = lambda x: permute(x, "head", lambda i: (i + ny) % (2 * ny))
     to_y = lambda x, k: permute(x, "head", lambda i: (i // ny) * ny + (i + k) % ny)
-    send, keep = cache_terms(0, orders[0], *operands, (BF16, F32), adds[0])
-    later, send = lax.optimization_barrier((orders[1], send))
+    send, keep = cache_terms(0, 0, where, *operands, (BF16, F32), adds[0])
+    later, send = lax.optimization_barrier((where, send))
     from_x_hi = to_x_hi(send)
-    send, own = cache_terms(0, later, *operands, (BF16, F32), adds[1])
+    send, own = cache_terms(0, 1, later, *operands, (BF16, F32), adds[1])
     dq = (dq_keep.astype(F32) + dq_pair.astype(F32)).astype(BF16)
     send, dq = lax.optimization_barrier((send, dq))
     from_y = to_y(send, 3)

time: 101 us -> 101 us (level)
    all_to_all x1, starting transfers between devices: 3.42 us -> 4.81 us  [per_device(): dq = lax.all_to_all(dq, 'ctx', 0, 0, axis_index_groups=z_groups)]
    unnamed x17 -> x13, local copies, waits for them, and re-layouts: 5.94 us -> 5.56 us
  transfers between devices with their start and end apart: 29 -> 29, of which waited for: 6 -> 5; matrix products, arithmetic and copies ran while one was open for 2% -> 2% of each run, Pallas kernels for 16% -> 15%
where the time goes in v5:
time: 101 us; the launch traced here: 100 us
  starting transfers between devices  50.2 us (50%)
  Pallas kernels  31.7 us (31%)
  waiting for transfers between devices  10.3 us (10%)
  local copies, waits for them, and re-layouts  5.69 us (6%)
  between operations  1.53 us (2%)
    ppermute x28, starting transfers between devices, permute(): lax.ppermute(x, axis, [(i, to(i)) for i in range(lax.axis_size(axis))])  45.4 us
    ppermute x28, waiting for transfers between devices, permute(): lax.ppermute(x, axis, [(i, to(i)) for i in range(lax.axis_size(axis))])  10.3 us
    pallas_call x1, Pallas kernels, attend(): pl.pallas_call(functools.partial(attend_kernel, score_scale, blocks, toge...  10.2 us
    pallas_call x4, Pallas kernels, cache_terms(): pl.pallas_call(functools.partial(cache_kernel, part, turn, d_lat), out_sh...  9.64 us
    unnamed x13, local copies, waits for them, and re-layouts  5.56 us
    pallas_call x2, Pallas kernels, project(): pl.pallas_call(functools.partial(project_kernel, p), out_shape=(jax.Shape...  5.22 us
    all_to_all x1, starting transfers between devices, per_device(): dq = lax.all_to_all(dq, 'ctx', 0, 0, axis_index_groups=z_groups)  4.81 us
  transfers between devices with their start and end apart: 29, of which 5 were waited for; matrix products, arithmetic and copies ran while one was open for 2% of the time, Pallas kernels for 15%

profile of v5, /device:TPU:1, one launch (start us, length us, event | category | flops | bytes accessed | tf_op | source)
XLA Modules:
  0.0 100.3 jit_solution(2980076282693964653)
XLA Ops:
  0.6 3.3 %collective-permute-start.10 = (bf16[1024,576]{0,1:T(8,128)(2,1)}, bf16[1024,576]{0,1:T(8,128)(2,1)S(1)}, u32[]{:S(2)}, u32[]{:S(2)}) collective-permute-start(bf16[1024,576]{0,1:T(8,128)(2,1)} %param.10), channel_id=1, source_target_pairs={{0,8},{8,0},{16,24},{24,16},{32,40},{40,32},{48,56},{56,48},{64,72... | collective-permute-start | bytes 3538952 | tf_op jit(solution)/shard_map/ppermute | solution.py:27
  4.6 0.1 stack.67.where_ref
  4.7 0.0 copy-start.2
  4.7 0.8 copy-done.2
  5.5 0.7 copy-done.3
  6.2 0.6 shard_map.86
  6.8 0.1 collective-permute-start
  6.9 1.2 %collective-permute-done = bf16[16,640]{1,0:T(8,128)(2,1)S(1)} collective-permute-done((bf16[16,640]{1,0:T(8,128)(2,1)S(1)}, bf16[16,640]{1,0:T(8,128)(2,1)S(1)}, u32[]{:S(2)}, u32[]{:S(2)}) %collective-permute-start) | collective-permute-done | bytes 20512 | tf_op jit(solution)/shard_map/ppermute | solution.py:27
  8.1 0.0 collective-permute-start.1
  8.1 0.2 collective-permute-start.2
  8.3 1.3 %copy-done = bf16[1024,576]{0,1:T(8,128)(2,1)S(1)} copy-done((bf16[1024,576]{0,1:T(8,128)(2,1)S(1)}, bf16[1024,576]{0,1:T(8,128)(2,1)}, u32[]{:S(2)}) %copy-start) | copy-done | bytes 1179672
  9.6 2.2 %copy-done.1 = bf16[16,512,256]{2,1,0:T(8,128)(2,1)S(1)} copy-done((bf16[16,512,256]{2,1,0:T(8,128)(2,1)S(1)}, bf16[16,512,256]{2,1,0:T(8,128)(2,1)}, u32[]{:S(2)}) %copy-start.1) | copy-done | bytes 4194328
  11.8 1.2 %shard_map.87 = (bf16[1024,576]{1,0:T(8,128)(2,1)S(1)}, bf16[8,512,128]{2,1,0:T(8,128)(2,1)S(1)}, bf16[8,512,128]{2,1,0:T(8,128)(2,1)S(1)}) custom-call(s32[16]{0:T(128)S(1)} %stack.67.where_ref, bf16[576,1024]{1,0:T(8,128)(2,1)S(1)} %bitcast.36, bf16[16,512,256]{2,1,0:T(8,128)(2,1)S(1)} %copy-done.1), custom_call_target="tpu_custom_call" | custom-call | flops 589824 | bytes 4718592 | tf_op jit(solution)/shard_map/pallas_call | solution.py:121
  13.0 0.0 copy-start.5
  13.0 0.0 collective-permute-done.1
  13.1 2.8 %collective-permute-start.6 = (bf16[64,640]{1,0:T(8,128)(2,1)S(1)}, bf16[64,640]{1,0:T(8,128)(2,1)S(1)}, u32[]{:S(2)}, u32[]{:S(2)}) collective-permute-start(bf16[64,640]{1,0:T(8,128)(2,1)S(1)} %maximum_select_fusion.refs_0_), channel_id=1, source_target_pairs={{0,64},{8,72},{16,80},{24,88},{32,96},{40,104},{48,112},{56,120},{... | collective-permute-start | bytes 245768 | tf_op jit(solution)/shard_map/ppermute | solution.py:27
  15.9 3.1 %collective-permute-start.4 = (bf16[64,640]{1,0:T(8,128)(2,1)S(1)}, bf16[64,640]{1,0:T(8,128)(2,1)S(1)}, u32[]{:S(2)}, u32[]{:S(2)}) collective-permute-start(bf16[64,640]{1,0:T(8,128)(2,1)S(1)} %maximum_select_fusion.refs_0_), channel_id=1, source_target_pairs={{0,192},{8,200},{16,208},{24,216},{32,224},{40,232},{48,240},{56,2... | collective-permute-start | bytes 245768 | tf_op jit(solution)/shard_map/ppermute | solution.py:27
  19.0 0.7 collective-permute-start.9
  19.7 1.9 %collective-permute-start.3 = (bf16[64,640]{1,0:T(8,128)(2,1)S(1)}, bf16[64,640]{1,0:T(8,128)(2,1)S(1)}, u32[]{:S(2)}, u32[]{:S(2)}) collective-permute-start(bf16[64,640]{1,0:T(8,128)(2,1)S(1)} %maximum_select_fusion.refs_0_), channel_id=1, source_target_pairs={{0,224},{8,232},{16,240},{24,248},{32,0},{40,8},{48,16},{56,24},{6... | collective-permute-start | bytes 245768 | tf_op jit(solution)/shard_map/ppermute | solution.py:27
  21.6 0.0 collective-permute-done.6.refs_6_
  21.7 2.4 %collective-permute-start.8 = (bf16[64,640]{1,0:T(8,128)(2,1)S(1)}, bf16[64,640]{1,0:T(8,128)(2,1)S(1)}, u32[]{:S(2)}, u32[]{:S(2)}) collective-permute-start(bf16[64,640]{1,0:T(8,128)(2,1)S(1)} %collective-permute-done.6.refs_6_), channel_id=1, source_target_pairs={{0,32},{8,40},{16,48},{24,56},{32,64},{40,72},{48,80},{56,88},{64,... | collective-permute-start | bytes 245768 | tf_op jit(solution)/shard_map/ppermute | solution.py:27
  24.1 0.2 collective-permute-done.4.refs_2_
  24.4 2.6 %collective-permute-start.7 = (bf16[64,640]{1,0:T(8,128)(2,1)S(1)}, bf16[64,640]{1,0:T(8,128)(2,1)S(1)}, u32[]{:S(2)}, u32[]{:S(2)}) collective-permute-start(bf16[64,640]{1,0:T(8,128)(2,1)S(1)} %collective-permute-done.6.refs_6_), channel_id=1, source_target_pairs={{0,64},{8,72},{16,80},{24,88},{32,96},{40,104},{48,112},{56,120},{... | collective-permute-start | bytes 245768 | tf_op jit(solution)/shard_map/ppermute | solution.py:27
  27.0 0.0 collective-permute-done.10
  27.0 0.0 collective-permute-start.5
  27.0 0.5 shard_map.88
  27.6 3.8 %collective-permute-done.7.refs_4_ = bf16[64,640]{1,0:T(8,128)(2,1)S(1)} collective-permute-done((bf16[64,640]{1,0:T(8,128)(2,1)S(1)}, bf16[64,640]{1,0:T(8,128)(2,1)S(1)}, u32[]{:S(2)}, u32[]{:S(2)}) %collective-permute-start.7) | collective-permute-done | bytes 81952 | tf_op jit(solution)/shard_map/ppermute | solution.py:27
  31.4 10.2 %shard_map.89 = (bf16[1024,576]{1,0:T(8,128)(2,1)S(1)}, bf16[1024,512]{1,0:T(8,128)(2,1)S(1)}, bf16[2048,1024]{1,0:T(8,128)(2,1)S(1)}, bf16[2048,1024]{1,0:T(8,128)(2,1)S(1)}, f32[4,1024]{1,0:T(4,128)S(1)}) custom-call(s32[16]{0:T(128)S(1)} %stack.67.where_ref, bf16[64,640]{1,0:T(8,128)(2,1)S(1)} %maximum_select_fusion.refs_0_, ...), custom_call_target="tpu_custom_call" | custom-call | flops 4563402752 | bytes 8388608 | tf_op jit(solution)/shard_map/pallas_call | solution.py:244
  41.6 0.5 collective-permute-start.13
  42.1 1.0 collective-permute-start.12
  43.1 1.2 %collective-permute-start.11 = (f32[4,1024]{1,0:T(4,128)S(1)}, f32[4,1024]{1,0:T(4,128)S(1)}, u32[]{:S(2)}, u32[]{:S(2)}) collective-permute-start(f32[4,1024]{1,0:T(4,128)S(1)} %get-tuple-element.70.refs_0_.refs_4_), channel_id=1, source_target_pairs={{0,16},{8,24},{16,0},{24,8},{32,48},{40,56},{48,32},{56,40},{64,80... | collective-permute-start | bytes 49160 | tf_op jit(solution)/shard_map/ppermute | solution.py:27
  44.3 2.6 %shard_map.90 = (f32[576,512]{1,0:T(8,128)S(1)}, f32[576,512]{1,0:T(8,128)S(1)}) custom-call(bf16[576,2048]{1,0:T(8,128)(2,1)S(1)} %get-tuple-element.71.cache_ref, bf16[2048,1024]{1,0:T(8,128)(2,1)S(1)} %get-tuple-element.68.spread_ref, bf16[2048,1024]{1,0:T(8,128)(2,1)S(1)} %get-tuple-element.69.expo_ref), custom_call_target="tpu_custom_call" | custom-call | flops 2415919104 | bytes 4194304 | tf_op jit(solution)/shard_map/pallas_call | solution.py:282
  47.0 0.1 shard_map.91.refs_0_
  47.1 0.0 copy-start.4
  47.1 0.4 collective-permute-start.16
  47.4 3.7 %collective-permute-start.15 = (f32[4,1024]{1,0:T(4,128)S(1)}, f32[4,1024]{1,0:T(4,128)S(1)}, u32[]{:S(2)}, u32[]{:S(2)}) collective-permute-start(f32[4,1024]{1,0:T(4,128)S(1)} %shard_map.91.refs_0_), channel_id=1, source_target_pairs={{0,128},{8,136},{16,144},{24,152},{32,160},{40,168},{48,176},{56,1... | collective-permute-start | bytes 49160 | tf_op jit(solution)/shard_map/ppermute | solution.py:27
  51.1 1.7 %collective-permute-start.14 = (f32[4,1024]{1,0:T(4,128)S(1)}, f32[4,1024]{1,0:T(4,128)S(1)}, u32[]{:S(2)}, u32[]{:S(2)}) collective-permute-start(f32[4,1024]{1,0:T(4,128)S(1)} %shard_map.91.refs_0_), channel_id=1, source_target_pairs={{0,64},{8,72},{16,80},{24,88},{32,96},{40,104},{48,112},{56,120},{... | collective-permute-start | bytes 49160 | tf_op jit(solution)/shard_map/ppermute | solution.py:27
  52.8 2.6 %shard_map.92 = (f32[576,512]{1,0:T(8,128)S(1)}, f32[576,512]{1,0:T(8,128)S(1)}) custom-call(bf16[576,2048]{1,0:T(8,128)(2,1)S(1)} %get-tuple-element.71.cache_ref, bf16[2048,1024]{1,0:T(8,128)(2,1)S(1)} %get-tuple-element.68.spread_ref, bf16[2048,1024]{1,0:T(8,128)(2,1)S(1)} %get-tuple-element.69.expo_ref), custom_call_target="tpu_custom_call" | custom-call | flops 2415919104 | bytes 4194304 | tf_op jit(solution)/shard_map/pallas_call | solution.py:282
  55.5 1.8 %shard_map.93 = (bf16[1024,576]{1,0:T(8,128)(2,1)S(1)}, bf16[1024,576]{1,0:T(8,128)(2,1)S(1)}, f32[2,1024]{1,0:T(2,128)S(1)}) custom-call(s32[16]{0:T(128)S(1)} %stack.67.where_ref, s32[4]{0:T(128)S(1)} %copy-done.4, f32[4,1024]{1,0:T(4,128)S(1)} %shard_map.91.refs_0_, f32[4,1024]{1,0:T(4,128)S(1)} %collective-permute-done.14.refs_1_, ...), custom_call_target="tpu_custom_call" | custom-call | flops 5898240 | bytes 4718592 | tf_op jit(solution)/shard_map/pallas_call | solution.py:354
  57.2 1.4 %shard_map.98 = (bf16[8,4,16,192]{3,2,1,0:T(8,128)(2,1)S(1)}, bf16[8,4,16,192]{3,2,1,0:T(8,128)(2,1)S(1)}) custom-call(s32[16]{0:T(128)S(1)} %stack.67.where_ref, f32[2,1024]{1,0:T(2,128)S(1)} %get-tuple-element.96.factors_ref, bf16[8,512,128]{2,1,0:T(8,128)(2,1)S(1)} %get-tuple-element.63.refs_8_.key_ref, f32[576,512]{1,0:T(8,128)S(1)} %get-tuple-element.97.refs_0_, ...), custom_call_target="tpu_custom_call" | custom-call | flops 268435456 | bytes 4194304 | tf_op jit(solution)/shard_map/pallas_call | solution.py:406
  58.6 0.3 collective-permute-start.21
  59.0 2.4 %shard_map.94 = (bf16[128,1152]{1,0:T(8,128)(2,1)S(1)}, bf16[128,1152]{1,0:T(8,128)(2,1)S(1)}) custom-call(s32[16]{0:T(128)S(1)} %stack.67.where_ref, bf16[2,2,4,128,1024]{4,3,2,1,0:T(8,128)(2,1)S(1)} %bitcast.32, bf16[2,2,4,128,1024]{4,3,2,1,0:T(8,128)(2,1)S(1)} %bitcast.28, bf16[1024,576]{1,0:T(8,128)(2,1)S(1)} %get-tuple-element.84.with_spread_ref, ...), custom_call_target="tpu_custom_call" | custom-call | flops 1207959552 | bytes 2097152 | tf_op jit(solution)/shard_map/pallas_call | solution.py:456
  61.4 5.0 %collective-permute-start.17 = (bf16[128,1152]{1,0:T(8,128)(2,1)S(1)}, bf16[128,1152]{1,0:T(8,128)(2,1)S(1)}, u32[]{:S(2)}, u32[]{:S(2)}) collective-permute-start(bf16[128,1152]{1,0:T(8,128)(2,1)S(1)} %get-tuple-element.88), channel_id=1, source_target_pairs={{0,8},{8,0},{16,24},{24,16},{32,40},{40,32},{48,56},{56,48},{64,72... | collective-permute-start | bytes 884744 | tf_op jit(solution)/shard_map/ppermute | solution.py:27
  66.4 0.1 collective-permute-start.18
  66.5 2.4 %shard_map.96 = (bf16[128,1152]{1,0:T(8,128)(2,1)S(1)}, bf16[128,1152]{1,0:T(8,128)(2,1)S(1)}) custom-call(s32[16]{0:T(128)S(1)} %stack.67.where_ref, bf16[2,2,4,128,1024]{4,3,2,1,0:T(8,128)(2,1)S(1)} %bitcast.33, bf16[2,2,4,128,1024]{4,3,2,1,0:T(8,128)(2,1)S(1)} %bitcast.29, bf16[1024,576]{1,0:T(8,128)(2,1)S(1)} %get-tuple-element.84.with_spread_ref, ...), custom_call_target="tpu_custom_call" | custom-call | flops 1207959552 | bytes 2097152 | tf_op jit(solution)/shard_map/pallas_call | solution.py:456
  68.9 0.5 collective-permute-start.19
  69.4 0.1 collective-permute-start.20
  69.5 0.8 add_convert_fusion
  70.3 2.4 %shard_map.95 = (bf16[128,1152]{1,0:T(8,128)(2,1)S(1)}, f32[128,1152]{1,0:T(8,128)S(1)}) custom-call(s32[16]{0:T(128)S(1)} %stack.67.where_ref, bf16[2,2,4,128,1024]{4,3,2,1,0:T(8,128)(2,1)S(1)} %bitcast.34, bf16[2,2,4,128,1024]{4,3,2,1,0:T(8,128)(2,1)S(1)} %bitcast.30, bf16[1024,576]{1,0:T(8,128)(2,1)S(1)} %get-tuple-element.84.with_spread_ref, ...), custom_call_target="tpu_custom_call" | custom-call | flops 1207959552 | bytes 2097152 | tf_op jit(solution)/shard_map/pallas_call | solution.py:456
  72.7 2.4 %shard_map.97 = (bf16[128,1152]{1,0:T(8,128)(2,1)S(1)}, f32[128,1152]{1,0:T(8,128)S(1)}) custom-call(s32[16]{0:T(128)S(1)} %stack.67.where_ref, bf16[2,2,4,128,1024]{4,3,2,1,0:T(8,128)(2,1)S(1)} %bitcast.35, bf16[2,2,4,128,1024]{4,3,2,1,0:T(8,128)(2,1)S(1)} %bitcast.31, bf16[1024,576]{1,0:T(8,128)(2,1)S(1)} %get-tuple-element.84.with_spread_ref, ...), custom_call_target="tpu_custom_call" | custom-call | flops 1207959552 | bytes 2097152 | tf_op jit(solution)/shard_map/pallas_call | solution.py:456
  75.1 4.8 %all-to-all-start = ((bf16[8,4,16,192]{3,2,1,0:T(8,128)(2,1)}), bf16[8,4,16,192]{3,2,1,0:T(8,128)(2,1)S(1)}, u32[]{:S(2)}, u32[]{:S(2)}) async-start(bf16[8,4,16,192]{3,2,1,0:T(8,128)(2,1)} %add_convert_fusion), calls=%async_computation | async-start | bytes 524288 | tf_op jit(solution)/shard_map/all_to_all | solution.py:622
  79.9 2.5 %collective-permute-start.24 = (bf16[128,1152]{1,0:T(8,128)(2,1)S(1)}, bf16[128,1152]{1,0:T(8,128)(2,1)S(1)}, u32[]{:S(2)}, u32[]{:S(2)}) collective-permute-start(bf16[128,1152]{1,0:T(8,128)(2,1)S(1)} %get-tuple-element.108), channel_id=1, source_target_pairs={{0,4},{1,5},{2,6},{3,7},{4,0},{5,1},{6,2},{7,3},{8,12},{9,13},{10,... | collective-permute-start | bytes 884744 | tf_op jit(solution)/shard_map/ppermute | solution.py:27
  82.4 2.7 %collective-permute-start.23 = (bf16[128,1152]{1,0:T(8,128)(2,1)S(1)}, bf16[128,1152]{1,0:T(8,128)(2,1)S(1)}, u32[]{:S(2)}, u32[]{:S(2)}) collective-permute-start(bf16[128,1152]{1,0:T(8,128)(2,1)S(1)} %get-tuple-element.105), channel_id=1, source_target_pairs={{0,3},{1,0},{2,1},{3,2},{4,7},{5,4},{6,5},{7,6},{8,11},{9,8},{10,9... | collective-permute-start | bytes 884744 | tf_op jit(solution)/shard_map/ppermute | solution.py:27
  85.1 4.2 %collective-permute-done.24.arrived_ref = bf16[128,1152]{1,0:T(8,128)(2,1)S(1)} collective-permute-done((bf16[128,1152]{1,0:T(8,128)(2,1)S(1)}, bf16[128,1152]{1,0:T(8,128)(2,1)S(1)}, u32[]{:S(2)}, u32[]{:S(2)}) %collective-permute-start.24) | collective-permute-done | bytes 294944 | tf_op jit(solution)/shard_map/ppermute | solution.py:27
  89.3 0.1 shard_map.100
  89.4 3.0 %collective-permute-start.25 = (bf16[64,1152]{1,0:T(8,128)(2,1)S(1)}, bf16[64,1152]{1,0:T(8,128)(2,1)S(1)}, u32[]{:S(2)}, u32[]{:S(2)}) collective-permute-start(bf16[64,1152]{1,0:T(8,128)(2,1)S(1)} %get-tuple-element.109), channel_id=1, source_target_pairs={{0,2},{1,3},{2,0},{3,1},{4,6},{5,7},{6,4},{7,5},{8,10},{9,11},{10,... | collective-permute-start | bytes 442376 | tf_op jit(solution)/shard_map/ppermute | solution.py:27
  92.4 0.4 collective-permute-start.26
  92.8 0.1 shard_map.99
  92.9 2.5 %collective-permute-start.27 = (bf16[64,1152]{1,0:T(8,128)(2,1)S(1)}, bf16[64,1152]{1,0:T(8,128)(2,1)S(1)}, u32[]{:S(2)}, u32[]{:S(2)}) collective-permute-start(bf16[64,1152]{1,0:T(8,128)(2,1)S(1)} %get-tuple-element.111), channel_id=1, source_target_pairs={{0,4},{1,5},{2,6},{3,7},{4,0},{5,1},{6,2},{7,3},{8,12},{9,13},{10,... | collective-permute-start | bytes 442376 | tf_op jit(solution)/shard_map/ppermute | solution.py:27
  95.5 2.5 %collective-permute-start.22 = (bf16[8,4,192]{2,1,0:T(4,128)(2,1)S(1)}, bf16[8,4,192]{2,1,0:T(4,128)(2,1)S(1)}, u32[]{:S(2)}, u32[]{:S(2)}) collective-permute-start(bf16[8,4,192]{2,1,0:T(4,128)(2,1)S(1)} %get-tuple-element.114), channel_id=1, source_target_pairs={{0,8},{8,0},{16,24},{24,16},{32,40},{40,32},{48,56},{56,48},{64,72... | collective-permute-start | bytes 36872 | tf_op jit(solution)/shard_map/ppermute | solution.py:27
  98.0 0.8 collective-permute-done.22
  98.9 0.6 copy.10
  99.5 0.0 collective-permute-done.26.refs_1_
  99.5 0.8 shard_map.101
  (31 shorter events, 0.2 us)
Async XLA Ops:
  0.6 26.4 %collective-permute-start.10 = (bf16[1024,576]{0,1:T(8,128)(2,1)}, bf16[1024,576]{0,1:T(8,128)(2,1)S(1)}, u32[]{:S(2)}, u32[]{:S(2)}) collective-permute-start(bf16[1024,576]{0,1:T(8,128)(2,1)} %param.10), channel_id=1, source_target_pairs={{0,8},{8,0},{16,24},{24,16},{32,40},{40,32},{48,56},{56,48},{64,72... | collective-permute-start | bytes 3538952 | tf_op jit(solution)/shard_map/ppermute | solution.py:27
  4.7 0.8 copy-start.2
  5.5 0.7 copy-start.3
  6.8 1.3 %collective-permute-start = (bf16[16,640]{1,0:T(8,128)(2,1)S(1)}, bf16[16,640]{1,0:T(8,128)(2,1)S(1)}, u32[]{:S(2)}, u32[]{:S(2)}) collective-permute-start(bf16[16,640]{1,0:T(8,128)(2,1)S(1)} %get-tuple-element.58), channel_id=1, source_target_pairs={{0,8},{8,0},{16,24},{24,16},{32,40},{40,32},{48,56},{56,48},{64,72... | collective-permute-start | bytes 61448 | tf_op jit(solution)/shard_map/ppermute | solution.py:27
  8.1 4.9 %collective-permute-start.1 = (bf16[32,640]{1,0:T(8,128)(2,1)S(1)}, bf16[32,640]{1,0:T(8,128)(2,1)S(1)}, u32[]{:S(2)}, u32[]{:S(2)}) collective-permute-start(bf16[32,640]{1,0:T(8,128)(2,1)S(1)} %pad_maximum_fusion), channel_id=1, source_target_pairs={{0,16},{8,24},{16,0},{24,8},{32,48},{40,56},{48,32},{56,40},{64,80... | collective-permute-start | bytes 122888 | tf_op jit(solution)/shard_map/ppermute | solution.py:27
  8.1 4.9 %collective-permute-start.2 = (f32[4]{0:T(128)}, f32[4]{0:T(128)S(1)}, u32[]{:S(2)}, u32[]{:S(2)}) collective-permute-start(f32[4]{0:T(128)} %refs_12_.1), channel_id=1, source_target_pairs={{0,8},{8,0},{16,24},{24,16},{32,40},{40,32},{48,56},{56,48},{64,72... | collective-permute-start | bytes 56 | tf_op jit(solution)/shard_map/ppermute | solution.py:27
  8.3 1.3 %copy-start = (bf16[1024,576]{0,1:T(8,128)(2,1)S(1)}, bf16[1024,576]{0,1:T(8,128)(2,1)}, u32[]{:S(2)}) copy-start(bf16[1024,576]{0,1:T(8,128)(2,1)} %param.10) | copy-start | bytes 3538948
  9.6 2.2 %copy-start.1 = (bf16[16,512,256]{2,1,0:T(8,128)(2,1)S(1)}, bf16[16,512,256]{2,1,0:T(8,128)(2,1)}, u32[]{:S(2)}) copy-start(bf16[16,512,256]{2,1,0:T(8,128)(2,1)} %kv_ref.1) | copy-start | bytes 12582916
  13.0 18.4 %copy-start.5 = (f32[4]{0:T(128)S(1)}, f32[4]{0:T(128)}, u32[]{:S(2)}) copy-start(f32[4]{0:T(128)} %refs_12_.1) | copy-start | bytes 52
  13.1 8.6 %collective-permute-start.6 = (bf16[64,640]{1,0:T(8,128)(2,1)S(1)}, bf16[64,640]{1,0:T(8,128)(2,1)S(1)}, u32[]{:S(2)}, u32[]{:S(2)}) collective-permute-start(bf16[64,640]{1,0:T(8,128)(2,1)S(1)} %maximum_select_fusion.refs_0_), channel_id=1, source_target_pairs={{0,64},{8,72},{16,80},{24,88},{32,96},{40,104},{48,112},{56,120},{... | collective-permute-start | bytes 245768 | tf_op jit(solution)/shard_map/ppermute | solution.py:27
  15.9 8.5 %collective-permute-start.4 = (bf16[64,640]{1,0:T(8,128)(2,1)S(1)}, bf16[64,640]{1,0:T(8,128)(2,1)S(1)}, u32[]{:S(2)}, u32[]{:S(2)}) collective-permute-start(bf16[64,640]{1,0:T(8,128)(2,1)S(1)} %maximum_select_fusion.refs_0_), channel_id=1, source_target_pairs={{0,192},{8,200},{16,208},{24,216},{32,224},{40,232},{48,240},{56,2... | collective-permute-start | bytes 245768 | tf_op jit(solution)/shard_map/ppermute | solution.py:27
  19.0 8.6 %collective-permute-start.9 = (bf16[64,640]{1,0:T(8,128)(2,1)S(1)}, bf16[64,640]{1,0:T(8,128)(2,1)S(1)}, u32[]{:S(2)}, u32[]{:S(2)}) collective-permute-start(bf16[64,640]{1,0:T(8,128)(2,1)S(1)} %maximum_select_fusion.refs_0_), channel_id=1, source_target_pairs={{0,32},{8,40},{16,48},{24,56},{32,64},{40,72},{48,80},{56,88},{64,... | collective-permute-start | bytes 245768 | tf_op jit(solution)/shard_map/ppermute | solution.py:27
  19.7 7.8 %collective-permute-start.3 = (bf16[64,640]{1,0:T(8,128)(2,1)S(1)}, bf16[64,640]{1,0:T(8,128)(2,1)S(1)}, u32[]{:S(2)}, u32[]{:S(2)}) collective-permute-start(bf16[64,640]{1,0:T(8,128)(2,1)S(1)} %maximum_select_fusion.refs_0_), channel_id=1, source_target_pairs={{0,224},{8,232},{16,240},{24,248},{32,0},{40,8},{48,16},{56,24},{6... | collective-permute-start | bytes 245768 | tf_op jit(solution)/shard_map/ppermute | solution.py:27
  21.7 5.9 %collective-permute-start.8 = (bf16[64,640]{1,0:T(8,128)(2,1)S(1)}, bf16[64,640]{1,0:T(8,128)(2,1)S(1)}, u32[]{:S(2)}, u32[]{:S(2)}) collective-permute-start(bf16[64,640]{1,0:T(8,128)(2,1)S(1)} %collective-permute-done.6.refs_6_), channel_id=1, source_target_pairs={{0,32},{8,40},{16,48},{24,56},{32,64},{40,72},{48,80},{56,88},{64,... | collective-permute-start | bytes 245768 | tf_op jit(solution)/shard_map/ppermute | solution.py:27
  24.4 7.0 %collective-permute-start.7 = (bf16[64,640]{1,0:T(8,128)(2,1)S(1)}, bf16[64,640]{1,0:T(8,128)(2,1)S(1)}, u32[]{:S(2)}, u32[]{:S(2)}) collective-permute-start(bf16[64,640]{1,0:T(8,128)(2,1)S(1)} %collective-permute-done.6.refs_6_), channel_id=1, source_target_pairs={{0,64},{8,72},{16,80},{24,88},{32,96},{40,104},{48,112},{56,120},{... | collective-permute-start | bytes 245768 | tf_op jit(solution)/shard_map/ppermute | solution.py:27
  27.0 4.4 %collective-permute-start.5 = (bf16[64,640]{1,0:T(8,128)(2,1)S(1)}, bf16[64,640]{1,0:T(8,128)(2,1)S(1)}, u32[]{:S(2)}, u32[]{:S(2)}) collective-permute-start(bf16[64,640]{1,0:T(8,128)(2,1)S(1)} %collective-permute-done.4.refs_2_), channel_id=1, source_target_pairs={{0,224},{8,232},{16,240},{24,248},{32,0},{40,8},{48,16},{56,24},{6... | collective-permute-start | bytes 245768 | tf_op jit(solution)/shard_map/ppermute | solution.py:27
  41.6 5.4 %collective-permute-start.13 = (f32[4,1024]{1,0:T(4,128)S(1)}, f32[4,1024]{1,0:T(4,128)S(1)}, u32[]{:S(2)}, u32[]{:S(2)}) collective-permute-start(f32[4,1024]{1,0:T(4,128)S(1)} %get-tuple-element.70.refs_0_.refs_4_), channel_id=1, source_target_pairs={{0,48},{8,56},{16,32},{24,40},{32,16},{40,24},{48,0},{56,8},{64,11... | collective-permute-start | bytes 49160 | tf_op jit(solution)/shard_map/ppermute | solution.py:27
  42.1 4.8 %collective-permute-start.12 = (f32[4,1024]{1,0:T(4,128)S(1)}, f32[4,1024]{1,0:T(4,128)S(1)}, u32[]{:S(2)}, u32[]{:S(2)}) collective-permute-start(f32[4,1024]{1,0:T(4,128)S(1)} %get-tuple-element.70.refs_0_.refs_4_), channel_id=1, source_target_pairs={{0,32},{8,40},{16,48},{24,56},{32,0},{40,8},{48,16},{56,24},{64,96... | collective-permute-start | bytes 49160 | tf_op jit(solution)/shard_map/ppermute | solution.py:27
  43.1 3.8 %collective-permute-start.11 = (f32[4,1024]{1,0:T(4,128)S(1)}, f32[4,1024]{1,0:T(4,128)S(1)}, u32[]{:S(2)}, u32[]{:S(2)}) collective-permute-start(f32[4,1024]{1,0:T(4,128)S(1)} %get-tuple-element.70.refs_0_.refs_4_), channel_id=1, source_target_pairs={{0,16},{8,24},{16,0},{24,8},{32,48},{40,56},{48,32},{56,40},{64,80... | collective-permute-start | bytes 49160 | tf_op jit(solution)/shard_map/ppermute | solution.py:27
  47.1 8.4 %copy-start.4 = (s32[4]{0:T(128)S(1)}, s32[4]{0:T(128)}, u32[]{:S(2)}) copy-start(s32[4]{0:T(128)} %lens_ref.1) | copy-start | bytes 52
  47.1 8.4 %collective-permute-start.16 = (f32[4,1024]{1,0:T(4,128)S(1)}, f32[4,1024]{1,0:T(4,128)S(1)}, u32[]{:S(2)}, u32[]{:S(2)}) collective-permute-start(f32[4,1024]{1,0:T(4,128)S(1)} %shard_map.91.refs_0_), channel_id=1, source_target_pairs={{0,192},{8,200},{16,208},{24,216},{32,224},{40,232},{48,240},{56,2... | collective-permute-start | bytes 49160 | tf_op jit(solution)/shard_map/ppermute | solution.py:27
  47.4 8.0 %collective-permute-start.15 = (f32[4,1024]{1,0:T(4,128)S(1)}, f32[4,1024]{1,0:T(4,128)S(1)}, u32[]{:S(2)}, u32[]{:S(2)}) collective-permute-start(f32[4,1024]{1,0:T(4,128)S(1)} %shard_map.91.refs_0_), channel_id=1, source_target_pairs={{0,128},{8,136},{16,144},{24,152},{32,160},{40,168},{48,176},{56,1... | collective-permute-start | bytes 49160 | tf_op jit(solution)/shard_map/ppermute | solution.py:27
  51.1 4.3 %collective-permute-start.14 = (f32[4,1024]{1,0:T(4,128)S(1)}, f32[4,1024]{1,0:T(4,128)S(1)}, u32[]{:S(2)}, u32[]{:S(2)}) collective-permute-start(f32[4,1024]{1,0:T(4,128)S(1)} %shard_map.91.refs_0_), channel_id=1, source_target_pairs={{0,64},{8,72},{16,80},{24,88},{32,96},{40,104},{48,112},{56,120},{... | collective-permute-start | bytes 49160 | tf_op jit(solution)/shard_map/ppermute | solution.py:27
  58.6 10.8 %collective-permute-start.21 = (bf16[8,4,16,192]{3,2,1,0:T(8,128)(2,1)S(1)}, bf16[8,4,16,192]{3,2,1,0:T(8,128)(2,1)S(1)}, u32[]{:S(2)}, u32[]{:S(2)}) collective-permute-start(bf16[8,4,16,192]{3,2,1,0:T(8,128)(2,1)S(1)} %get-tuple-element.102), channel_id=1, source_target_pairs={{0,16},{8,24},{16,0},{24,8},{32,48},{40,56},{48,32},{56,40},{64,80... | collective-permute-start | bytes 589832 | tf_op jit(solution)/shard_map/ppermute | solution.py:27
  61.4 8.9 %collective-permute-start.17 = (bf16[128,1152]{1,0:T(8,128)(2,1)S(1)}, bf16[128,1152]{1,0:T(8,128)(2,1)S(1)}, u32[]{:S(2)}, u32[]{:S(2)}) collective-permute-start(bf16[128,1152]{1,0:T(8,128)(2,1)S(1)} %get-tuple-element.88), channel_id=1, source_target_pairs={{0,8},{8,0},{16,24},{24,16},{32,40},{40,32},{48,56},{56,48},{64,72... | collective-permute-start | bytes 884744 | tf_op jit(solution)/shard_map/ppermute | solution.py:27
  66.4 3.9 %collective-permute-start.18 = (bf16[128,1152]{1,0:T(8,128)(2,1)S(1)}, bf16[128,1152]{1,0:T(8,128)(2,1)S(1)}, u32[]{:S(2)}, u32[]{:S(2)}) collective-permute-start(bf16[128,1152]{1,0:T(8,128)(2,1)S(1)} %get-tuple-element.89), channel_id=1, source_target_pairs={{0,8},{8,0},{16,24},{24,16},{32,40},{40,32},{48,56},{56,48},{64,72... | collective-permute-start | bytes 884744 | tf_op jit(solution)/shard_map/ppermute | solution.py:27
  68.9 3.8 %collective-permute-start.19 = (bf16[128,1152]{1,0:T(8,128)(2,1)S(1)}, bf16[128,1152]{1,0:T(8,128)(2,1)S(1)}, u32[]{:S(2)}, u32[]{:S(2)}) collective-permute-start(bf16[128,1152]{1,0:T(8,128)(2,1)S(1)} %get-tuple-element.93), channel_id=1, source_target_pairs={{0,8},{8,0},{16,24},{24,16},{32,40},{40,32},{48,56},{56,48},{64,72... | collective-permute-start | bytes 884744 | tf_op jit(solution)/shard_map/ppermute | solution.py:27
  69.4 3.3 %collective-permute-start.20 = (bf16[128,1152]{1,0:T(8,128)(2,1)S(1)}, bf16[128,1152]{1,0:T(8,128)(2,1)S(1)}, u32[]{:S(2)}, u32[]{:S(2)}) collective-permute-start(bf16[128,1152]{1,0:T(8,128)(2,1)S(1)} %get-tuple-element.94), channel_id=1, source_target_pairs={{0,8},{8,0},{16,24},{24,16},{32,40},{40,32},{48,56},{56,48},{64,72... | collective-permute-start | bytes 884744 | tf_op jit(solution)/shard_map/ppermute | solution.py:27
  75.1 20.3 %all-to-all-start = ((bf16[8,4,16,192]{3,2,1,0:T(8,128)(2,1)}), bf16[8,4,16,192]{3,2,1,0:T(8,128)(2,1)S(1)}, u32[]{:S(2)}, u32[]{:S(2)}) async-start(bf16[8,4,16,192]{3,2,1,0:T(8,128)(2,1)} %add_convert_fusion), calls=%async_computation | async-start | bytes 524288 | tf_op jit(solution)/shard_map/all_to_all | solution.py:622
  79.9 9.4 %collective-permute-start.24 = (bf16[128,1152]{1,0:T(8,128)(2,1)S(1)}, bf16[128,1152]{1,0:T(8,128)(2,1)S(1)}, u32[]{:S(2)}, u32[]{:S(2)}) collective-permute-start(bf16[128,1152]{1,0:T(8,128)(2,1)S(1)} %get-tuple-element.108), channel_id=1, source_target_pairs={{0,4},{1,5},{2,6},{3,7},{4,0},{5,1},{6,2},{7,3},{8,12},{9,13},{10,... | collective-permute-start | bytes 884744 | tf_op jit(solution)/shard_map/ppermute | solution.py:27
  82.4 10.4 %collective-permute-start.23 = (bf16[128,1152]{1,0:T(8,128)(2,1)S(1)}, bf16[128,1152]{1,0:T(8,128)(2,1)S(1)}, u32[]{:S(2)}, u32[]{:S(2)}) collective-permute-start(bf16[128,1152]{1,0:T(8,128)(2,1)S(1)} %get-tuple-element.105), channel_id=1, source_target_pairs={{0,3},{1,0},{2,1},{3,2},{4,7},{5,4},{6,5},{7,6},{8,11},{9,8},{10,9... | collective-permute-start | bytes 884744 | tf_op jit(solution)/shard_map/ppermute | solution.py:27
  89.4 10.1 %collective-permute-start.25 = (bf16[64,1152]{1,0:T(8,128)(2,1)S(1)}, bf16[64,1152]{1,0:T(8,128)(2,1)S(1)}, u32[]{:S(2)}, u32[]{:S(2)}) collective-permute-start(bf16[64,1152]{1,0:T(8,128)(2,1)S(1)} %get-tuple-element.109), channel_id=1, source_target_pairs={{0,2},{1,3},{2,0},{3,1},{4,6},{5,7},{6,4},{7,5},{8,10},{9,11},{10,... | collective-permute-start | bytes 442376 | tf_op jit(solution)/shard_map/ppermute | solution.py:27
  92.4 7.1 %collective-permute-start.26 = (bf16[64,1152]{1,0:T(8,128)(2,1)S(1)}, bf16[64,1152]{1,0:T(8,128)(2,1)S(1)}, u32[]{:S(2)}, u32[]{:S(2)}) collective-permute-start(bf16[64,1152]{1,0:T(8,128)(2,1)S(1)} %get-tuple-element.110), channel_id=1, source_target_pairs={{0,1},{1,2},{2,3},{3,0},{4,5},{5,6},{6,7},{7,4},{8,9},{9,10},{10,1... | collective-permute-start | bytes 442376 | tf_op jit(solution)/shard_map/ppermute | solution.py:27
  92.9 6.6 %collective-permute-start.27 = (bf16[64,1152]{1,0:T(8,128)(2,1)S(1)}, bf16[64,1152]{1,0:T(8,128)(2,1)S(1)}, u32[]{:S(2)}, u32[]{:S(2)}) collective-permute-start(bf16[64,1152]{1,0:T(8,128)(2,1)S(1)} %get-tuple-element.111), channel_id=1, source_target_pairs={{0,4},{1,5},{2,6},{3,7},{4,0},{5,1},{6,2},{7,3},{8,12},{9,13},{10,... | collective-permute-start | bytes 442376 | tf_op jit(solution)/shard_map/ppermute | solution.py:27
  95.5 3.3 %collective-permute-start.22 = (bf16[8,4,192]{2,1,0:T(4,128)(2,1)S(1)}, bf16[8,4,192]{2,1,0:T(4,128)(2,1)S(1)}, u32[]{:S(2)}, u32[]{:S(2)}) collective-permute-start(bf16[8,4,192]{2,1,0:T(4,128)(2,1)S(1)} %get-tuple-element.114), channel_id=1, source_target_pairs={{0,8},{8,0},{16,24},{24,16},{32,40},{40,32},{48,56},{56,48},{64,72... | collective-permute-start | bytes 36872 | tf_op jit(solution)/shard_map/ppermute | solution.py:27

commit v6 on v5

--- a/solution.py
+++ b/solution.py
@@ -104,55 +104,59 @@
     )(where, queries, out_grad)
 
 
-def stage_own_kernel(where_ref, cache_ref, kv_ref, out_ref, key_ref, value_ref):
+def stage_own_kernel(cache_ref, out_ref):
+    out_ref[...] = cache_ref[...].T
+
+
+def stage_own(cache_t):
+    c_width, keys = cache_t.shape
+    vmem = pl.BlockSpec(memory_space=pltpu.VMEM)
+    return pl.pallas_call(
+        stage_own_kernel,
+        out_shape=jax.ShapeDtypeStruct((keys, c_width), BF16),
+        in_specs=[vmem],
+        out_specs=vmem,
+        compiler_params=pltpu.CompilerParams(vmem_limit_bytes=6 * MIB),
+        cost_estimate=pl.CostEstimate(
+            flops=keys * c_width, bytes_accessed=4 * keys * c_width, transcendentals=0
+        ),
+    )(cache_t)
+
+
+def stage_other_kernel(
+    where_ref, cache_ref, own_ref, kv_ref, out_ref, both_ref, key_ref, value_ref
+):
+    keys = own_ref.shape[1]
     half, _, d_nope = key_ref.shape
     out_ref[...] = cache_ref[...].T
+    both_ref[:, :keys] = own_ref[...]
+    both_ref[:, keys:] = cache_ref[...]
     for h in range(half):
         key_ref[h] = kv_ref[where_ref[0] * half + h, :, :d_nope]
         value_ref[h] = kv_ref[where_ref[0] * half + h, :, d_nope:]
 
 
-def stage_own(where, cache_t, kv_up):
+def stage_other(where, cache_t, own_t, kv_up):
     c_width, keys = cache_t.shape
     heads, d_lat, width = kv_up.shape
     smem = pl.BlockSpec(memory_space=pltpu.SMEM)
     vmem = pl.BlockSpec(memory_space=pltpu.VMEM)
     weight = jax.ShapeDtypeStruct((heads // 2, d_lat, width // 2), BF16)
-    return pl.pallas_call(
-        stage_own_kernel,
-        out_shape=(jax.ShapeDtypeStruct((keys, c_width), BF16), weight, weight),
-        in_specs=[smem, vmem, vmem],
-        out_specs=[vmem] * 3,
-        compiler_params=pltpu.CompilerParams(vmem_limit_bytes=16 * MIB),
-        cost_estimate=pl.CostEstimate(
-            flops=keys * c_width, bytes_accessed=8 * keys * c_width, transcendentals=0
-        ),
-    )(where, cache_t, kv_up)
-
-
-def stage_other_kernel(cache_ref, own_ref, out_ref, both_ref):
-    keys = own_ref.shape[1]
-    out_ref[...] = cache_ref[...].T
-    both_ref[:, :keys] = own_ref[...]
-    both_ref[:, keys:] = cache_ref[...]
-
-
-def stage_other(cache_t, own_t):
-    c_width, keys = cache_t.shape
-    vmem = pl.BlockSpec(memory_space=pltpu.VMEM)
     return pl.pallas_call(
         stage_other_kernel,
         out_shape=(
             jax.ShapeDtypeStruct((keys, c_width), BF16),
             jax.ShapeDtypeStruct((c_width, 2 * keys), BF16),
-        ),
-        in_specs=[vmem] * 2,
-        out_specs=[vmem] * 2,
-        compiler_params=pltpu.CompilerParams(vmem_limit_bytes=10 * MIB),
+            weight,
+            weight,
+        ),
+        in_specs=[smem] + [vmem] * 3,
+        out_specs=[vmem] * 4,
+        compiler_params=pltpu.CompilerParams(vmem_limit_bytes=18 * MIB),
         cost_estimate=pl.CostEstimate(
-            flops=keys * c_width, bytes_accessed=4 * keys * c_width, transcendentals=0
-        ),
-    )(cache_t, own_t)
+            flops=keys * c_width, bytes_accessed=8 * keys * c_width, transcendentals=0
+        ),
+    )(where, cache_t, own_t, kv_up)
 
 
 def attend_kernel(score_scale, blocks, together, where_ref, *refs):
@@ -552,13 +556,13 @@
     other_ratio = permute(token_ratio, "ctx", other_core)
     mine, theirs = pack(where, queries, out_grad)
     block = jnp.concatenate([mine, permute(theirs, "ctx", other_core)], 0)
-    own_keys, w_key, w_val = stage_own(where, own_t, kv_up)
+    own_keys = stage_own(own_t)
     from_x_lo = permute(block, "ctx", other_x_lo)
-    from_x_lo, own_keys, w_key, w_val, other_ratio = lax.optimization_barrier(
-        (from_x_lo, own_keys, w_key, w_val, other_ratio)
+    from_x_lo, own_keys, other_ratio = lax.optimization_barrier(
+        (from_x_lo, own_keys, other_ratio)
     )
     block = in_order(block, from_x_lo, x_lo == 1, 0)
-    other_keys, cache_t = stage_other(other_t, own_t)
+    other_keys, cache_t, w_key, w_val = stage_other(where, other_t, own_t, kv_up)
     along_z = lambda x, k: permute(x, "ctx", lambda i: (i + 4 * k) % (4 * nz))
     ring = [block] + [None] * (nz - 1)
     ring[nz - 2], ring[2] = along_z(block, 2), along_z(block, -2)

time: 101 us -> 98.4 us (0.974)
  starting transfers between devices: 50.2 us -> 48.6 us
  waiting for transfers between devices: 10.3 us -> 9.01 us
    ppermute x28, waiting for transfers between devices: 10.3 us -> 9.01 us  [permute(): lax.ppermute(x, axis, [(i, to(i)) for i in range(lax.axis_size(axis))])]
    unnamed x13 -> x15, local copies, waits for them, and re-layouts: 5.56 us -> 5.56 us
  transfers between devices with their start and end apart: 29 -> 29, of which waited for: 5 -> 7; matrix products, arithmetic and copies ran while one was open for 2% -> 2% of each run, Pallas kernels for 15% -> 16%
where the time goes in v6:
time: 98.4 us; the launch traced here: 97.4 us
  starting transfers between devices  48.6 us (49%)
  Pallas kernels  31.8 us (32%)
  waiting for transfers between devices  9.01 us (9%)
  local copies, waits for them, and re-layouts  5.69 us (6%)
  between operations  1.49 us (2%)
    ppermute x28, starting transfers between devices, permute(): lax.ppermute(x, axis, [(i, to(i)) for i in range(lax.axis_size(axis))])  44.6 us
    pallas_call x1, Pallas kernels, attend(): pl.pallas_call(functools.partial(attend_kernel, score_scale, blocks, toge...  10.2 us
    pallas_call x4, Pallas kernels, cache_terms(): pl.pallas_call(functools.partial(cache_kernel, part, turn, d_lat), out_sh...  9.64 us
    ppermute x28, waiting for transfers between devices, permute(): lax.ppermute(x, axis, [(i, to(i)) for i in range(lax.axis_size(axis))])  9.01 us
    unnamed x15, local copies, waits for them, and re-layouts  5.56 us
    pallas_call x2, Pallas kernels, project(): pl.pallas_call(functools.partial(project_kernel, p), out_shape=(jax.Shape...  5.22 us
    all_to_all x1, starting transfers between devices, per_device(): dq = lax.all_to_all(dq, 'ctx', 0, 0, axis_index_groups=z_groups)  4.03 us
  transfers between devices with their start and end apart: 29, of which 7 were waited for; matrix products, arithmetic and copies ran while one was open for 2% of the time, Pallas kernels for 16%

profile of v6, /device:TPU:1, one launch (start us, length us, event | category | flops | bytes accessed | tf_op | source)
XLA Modules:
  0.0 97.4 jit_solution(16612293944596630399)
XLA Ops:
  0.6 3.3 %collective-permute-start.10 = (bf16[1024,576]{0,1:T(8,128)(2,1)}, bf16[1024,576]{0,1:T(8,128)(2,1)S(1)}, u32[]{:S(2)}, u32[]{:S(2)}) collective-permute-start(bf16[1024,576]{0,1:T(8,128)(2,1)} %param.10), channel_id=1, source_target_pairs={{0,8},{8,0},{16,24},{24,16},{32,40},{40,32},{48,56},{56,48},{64,72... | collective-permute-start | bytes 3538952 | tf_op jit(solution)/shard_map/ppermute | solution.py:27
  4.6 0.1 stack.67.where_ref
  4.7 0.0 copy-start.3
  4.7 0.8 copy-done.3
  5.5 0.7 copy-done.4
  6.2 0.6 shard_map.86
  6.8 0.1 collective-permute-start
  6.9 1.2 %collective-permute-done = bf16[16,640]{1,0:T(8,128)(2,1)S(1)} collective-permute-done((bf16[16,640]{1,0:T(8,128)(2,1)S(1)}, bf16[16,640]{1,0:T(8,128)(2,1)S(1)}, u32[]{:S(2)}, u32[]{:S(2)}) %collective-permute-start) | collective-permute-done | bytes 20512 | tf_op jit(solution)/shard_map/ppermute | solution.py:27
  8.1 0.0 collective-permute-start.1
  8.1 0.2 collective-permute-start.2
  8.3 1.3 %copy-done = bf16[1024,576]{0,1:T(8,128)(2,1)S(1)} copy-done((bf16[1024,576]{0,1:T(8,128)(2,1)S(1)}, bf16[1024,576]{0,1:T(8,128)(2,1)}, u32[]{:S(2)}) %copy-start) | copy-done | bytes 1179672
  9.6 0.4 shard_map.87.refs_10_
  10.0 1.0 collective-permute-done.1
  11.0 1.8 %collective-permute-start.6 = (bf16[64,640]{1,0:T(8,128)(2,1)S(1)}, bf16[64,640]{1,0:T(8,128)(2,1)S(1)}, u32[]{:S(2)}, u32[]{:S(2)}) collective-permute-start(bf16[64,640]{1,0:T(8,128)(2,1)S(1)} %maximum_select_fusion.refs_0_), channel_id=1, source_target_pairs={{0,64},{8,72},{16,80},{24,88},{32,96},{40,104},{48,112},{56,120},{... | collective-permute-start | bytes 245768 | tf_op jit(solution)/shard_map/ppermute | solution.py:27
  12.8 3.1 %collective-permute-start.4 = (bf16[64,640]{1,0:T(8,128)(2,1)S(1)}, bf16[64,640]{1,0:T(8,128)(2,1)S(1)}, u32[]{:S(2)}, u32[]{:S(2)}) collective-permute-start(bf16[64,640]{1,0:T(8,128)(2,1)S(1)} %maximum_select_fusion.refs_0_), channel_id=1, source_target_pairs={{0,192},{8,200},{16,208},{24,216},{32,224},{40,232},{48,240},{56,2... | collective-permute-start | bytes 245768 | tf_op jit(solution)/shard_map/ppermute | solution.py:27
  15.9 0.7 collective-permute-start.9
  16.7 1.9 %collective-permute-start.3 = (bf16[64,640]{1,0:T(8,128)(2,1)S(1)}, bf16[64,640]{1,0:T(8,128)(2,1)S(1)}, u32[]{:S(2)}, u32[]{:S(2)}) collective-permute-start(bf16[64,640]{1,0:T(8,128)(2,1)S(1)} %maximum_select_fusion.refs_0_), channel_id=1, source_target_pairs={{0,224},{8,232},{16,240},{24,248},{32,0},{40,8},{48,16},{56,24},{6... | collective-permute-start | bytes 245768 | tf_op jit(solution)/shard_map/ppermute | solution.py:27
  18.6 0.0 collective-permute-done.6.refs_6_
  18.6 2.2 %collective-permute-start.8 = (bf16[64,640]{1,0:T(8,128)(2,1)S(1)}, bf16[64,640]{1,0:T(8,128)(2,1)S(1)}, u32[]{:S(2)}, u32[]{:S(2)}) collective-permute-start(bf16[64,640]{1,0:T(8,128)(2,1)S(1)} %collective-permute-done.6.refs_6_), channel_id=1, source_target_pairs={{0,32},{8,40},{16,48},{24,56},{32,64},{40,72},{48,80},{56,88},{64,... | collective-permute-start | bytes 245768 | tf_op jit(solution)/shard_map/ppermute | solution.py:27
  20.8 0.4 collective-permute-done.4.refs_2_
  21.2 1.9 %collective-permute-start.7 = (bf16[64,640]{1,0:T(8,128)(2,1)S(1)}, bf16[64,640]{1,0:T(8,128)(2,1)S(1)}, u32[]{:S(2)}, u32[]{:S(2)}) collective-permute-start(bf16[64,640]{1,0:T(8,128)(2,1)S(1)} %collective-permute-done.6.refs_6_), channel_id=1, source_target_pairs={{0,64},{8,72},{16,80},{24,88},{32,96},{40,104},{48,112},{56,120},{... | collective-permute-start | bytes 245768 | tf_op jit(solution)/shard_map/ppermute | solution.py:27
  23.1 0.1 collective-permute-start.5
  23.2 2.2 %copy-done.2 = bf16[16,512,256]{2,1,0:T(8,128)(2,1)S(1)} copy-done((bf16[16,512,256]{2,1,0:T(8,128)(2,1)S(1)}, bf16[16,512,256]{2,1,0:T(8,128)(2,1)}, u32[]{:S(2)}) %copy-start.2) | copy-done | bytes 4194328
  25.4 1.4 %shard_map.88 = (bf16[1024,576]{1,0:T(8,128)(2,1)S(1)}, bf16[576,2048]{1,0:T(8,128)(2,1)S(1)}, bf16[8,512,128]{2,1,0:T(8,128)(2,1)S(1)}, bf16[8,512,128]{2,1,0:T(8,128)(2,1)S(1)}) custom-call(s32[16]{0:T(128)S(1)} %stack.67.where_ref, bf16[576,1024]{1,0:T(8,128)(2,1)S(1)} %bitcast.38, bf16[576,1024]{1,0:T(8,128)(2,1)S(1)} %bitcast.37, ...), custom_call_target="tpu_custom_call" | custom-call | flops 589824 | bytes 4718592 | tf_op jit(solution)/shard_map/pallas_call | solution.py:145
  26.8 0.0 collective-permute-done.9.refs_7_
  26.9 0.4 collective-permute-done.7.refs_4_
  27.2 10.2 %shard_map.89 = (bf16[1024,576]{1,0:T(8,128)(2,1)S(1)}, bf16[1024,512]{1,0:T(8,128)(2,1)S(1)}, bf16[2048,1024]{1,0:T(8,128)(2,1)S(1)}, bf16[2048,1024]{1,0:T(8,128)(2,1)S(1)}, f32[4,1024]{1,0:T(4,128)S(1)}) custom-call(s32[16]{0:T(128)S(1)} %stack.67.where_ref, bf16[64,640]{1,0:T(8,128)(2,1)S(1)} %maximum_select_fusion.refs_0_, ...), custom_call_target="tpu_custom_call" | custom-call | flops 4563402752 | bytes 8388608 | tf_op jit(solution)/shard_map/pallas_call | solution.py:248
  37.4 1.7 %collective-permute-start.13 = (f32[4,1024]{1,0:T(4,128)S(1)}, f32[4,1024]{1,0:T(4,128)S(1)}, u32[]{:S(2)}, u32[]{:S(2)}) collective-permute-start(f32[4,1024]{1,0:T(4,128)S(1)} %get-tuple-element.64.refs_0_.refs_4_), channel_id=1, source_target_pairs={{0,48},{8,56},{16,32},{24,40},{32,16},{40,24},{48,0},{56,8},{64,11... | collective-permute-start | bytes 49160 | tf_op jit(solution)/shard_map/ppermute | solution.py:27
  39.2 0.1 collective-permute-start.12
  39.2 1.1 %collective-permute-start.11 = (f32[4,1024]{1,0:T(4,128)S(1)}, f32[4,1024]{1,0:T(4,128)S(1)}, u32[]{:S(2)}, u32[]{:S(2)}) collective-permute-start(f32[4,1024]{1,0:T(4,128)S(1)} %get-tuple-element.64.refs_0_.refs_4_), channel_id=1, source_target_pairs={{0,16},{8,24},{16,0},{24,8},{32,48},{40,56},{48,32},{56,40},{64,80... | collective-permute-start | bytes 49160 | tf_op jit(solution)/shard_map/ppermute | solution.py:27
  40.3 2.6 %shard_map.90 = (f32[576,512]{1,0:T(8,128)S(1)}, f32[576,512]{1,0:T(8,128)S(1)}) custom-call(bf16[576,2048]{1,0:T(8,128)(2,1)S(1)} %get-tuple-element.65.cache_ref, bf16[2048,1024]{1,0:T(8,128)(2,1)S(1)} %get-tuple-element.62.spread_ref, bf16[2048,1024]{1,0:T(8,128)(2,1)S(1)} %get-tuple-element.63.expo_ref), custom_call_target="tpu_custom_call" | custom-call | flops 2415919104 | bytes 4194304 | tf_op jit(solution)/shard_map/pallas_call | solution.py:286
  43.0 0.1 shard_map.91.refs_0_
  43.0 0.0 copy-start.5
  43.0 1.2 %collective-permute-start.16 = (f32[4,1024]{1,0:T(4,128)S(1)}, f32[4,1024]{1,0:T(4,128)S(1)}, u32[]{:S(2)}, u32[]{:S(2)}) collective-permute-start(f32[4,1024]{1,0:T(4,128)S(1)} %shard_map.91.refs_0_), channel_id=1, source_target_pairs={{0,192},{8,200},{16,208},{24,216},{32,224},{40,232},{48,240},{56,2... | collective-permute-start | bytes 49160 | tf_op jit(solution)/shard_map/ppermute | solution.py:27
  44.2 4.9 %collective-permute-start.15 = (f32[4,1024]{1,0:T(4,128)S(1)}, f32[4,1024]{1,0:T(4,128)S(1)}, u32[]{:S(2)}, u32[]{:S(2)}) collective-permute-start(f32[4,1024]{1,0:T(4,128)S(1)} %shard_map.91.refs_0_), channel_id=1, source_target_pairs={{0,128},{8,136},{16,144},{24,152},{32,160},{40,168},{48,176},{56,1... | collective-permute-start | bytes 49160 | tf_op jit(solution)/shard_map/ppermute | solution.py:27
  49.1 0.0 collective-permute-start.14
  49.1 2.6 %shard_map.92 = (f32[576,512]{1,0:T(8,128)S(1)}, f32[576,512]{1,0:T(8,128)S(1)}) custom-call(bf16[576,2048]{1,0:T(8,128)(2,1)S(1)} %get-tuple-element.65.cache_ref, bf16[2048,1024]{1,0:T(8,128)(2,1)S(1)} %get-tuple-element.62.spread_ref, bf16[2048,1024]{1,0:T(8,128)(2,1)S(1)} %get-tuple-element.63.expo_ref), custom_call_target="tpu_custom_call" | custom-call | flops 2415919104 | bytes 4194304 | tf_op jit(solution)/shard_map/pallas_call | solution.py:286
  51.7 1.1 %collective-permute-done.14.refs_1_ = f32[4,1024]{1,0:T(4,128)S(1)} collective-permute-done((f32[4,1024]{1,0:T(4,128)S(1)}, f32[4,1024]{1,0:T(4,128)S(1)}, u32[]{:S(2)}, u32[]{:S(2)}) %collective-permute-start.14) | collective-permute-done | bytes 16416 | tf_op jit(solution)/shard_map/ppermute | solution.py:27
  52.7 1.8 %shard_map.93 = (bf16[1024,576]{1,0:T(8,128)(2,1)S(1)}, bf16[1024,576]{1,0:T(8,128)(2,1)S(1)}, f32[2,1024]{1,0:T(2,128)S(1)}) custom-call(s32[16]{0:T(128)S(1)} %stack.67.where_ref, s32[4]{0:T(128)S(1)} %copy-done.5, f32[4,1024]{1,0:T(4,128)S(1)} %shard_map.91.refs_0_, f32[4,1024]{1,0:T(4,128)S(1)} %collective-permute-done.14.refs_1_, ...), custom_call_target="tpu_custom_call" | custom-call | flops 5898240 | bytes 4718592 | tf_op jit(solution)/shard_map/pallas_call | solution.py:358
  54.5 1.4 %shard_map.98 = (bf16[8,4,16,192]{3,2,1,0:T(8,128)(2,1)S(1)}, bf16[8,4,16,192]{3,2,1,0:T(8,128)(2,1)S(1)}) custom-call(s32[16]{0:T(128)S(1)} %stack.67.where_ref, f32[2,1024]{1,0:T(2,128)S(1)} %get-tuple-element.90.factors_ref, bf16[8,512,128]{2,1,0:T(8,128)(2,1)S(1)} %get-tuple-element.57.refs_8_.key_ref, f32[576,512]{1,0:T(8,128)S(1)} %get-tuple-element.91.refs_0_, ...), custom_call_target="tpu_custom_call" | custom-call | flops 268435456 | bytes 4194304 | tf_op jit(solution)/shard_map/pallas_call | solution.py:410
  55.9 0.2 collective-permute-start.21
  56.1 2.4 %shard_map.94 = (bf16[128,1152]{1,0:T(8,128)(2,1)S(1)}, bf16[128,1152]{1,0:T(8,128)(2,1)S(1)}) custom-call(s32[16]{0:T(128)S(1)} %stack.67.where_ref, bf16[2,2,4,128,1024]{4,3,2,1,0:T(8,128)(2,1)S(1)} %bitcast.32, bf16[2,2,4,128,1024]{4,3,2,1,0:T(8,128)(2,1)S(1)} %bitcast.28, bf16[1024,576]{1,0:T(8,128)(2,1)S(1)} %get-tuple-element.78.with_spread_ref, ...), custom_call_target="tpu_custom_call" | custom-call | flops 1207959552 | bytes 2097152 | tf_op jit(solution)/shard_map/pallas_call | solution.py:460
  58.5 5.7 %collective-permute-start.17 = (bf16[128,1152]{1,0:T(8,128)(2,1)S(1)}, bf16[128,1152]{1,0:T(8,128)(2,1)S(1)}, u32[]{:S(2)}, u32[]{:S(2)}) collective-permute-start(bf16[128,1152]{1,0:T(8,128)(2,1)S(1)} %get-tuple-element.82), channel_id=1, source_target_pairs={{0,8},{8,0},{16,24},{24,16},{32,40},{40,32},{48,56},{56,48},{64,72... | collective-permute-start | bytes 884744 | tf_op jit(solution)/shard_map/ppermute | solution.py:27
  64.3 0.1 collective-permute-start.18
  64.4 2.4 %shard_map.96 = (bf16[128,1152]{1,0:T(8,128)(2,1)S(1)}, bf16[128,1152]{1,0:T(8,128)(2,1)S(1)}) custom-call(s32[16]{0:T(128)S(1)} %stack.67.where_ref, bf16[2,2,4,128,1024]{4,3,2,1,0:T(8,128)(2,1)S(1)} %bitcast.33, bf16[2,2,4,128,1024]{4,3,2,1,0:T(8,128)(2,1)S(1)} %bitcast.29, bf16[1024,576]{1,0:T(8,128)(2,1)S(1)} %get-tuple-element.78.with_spread_ref, ...), custom_call_target="tpu_custom_call" | custom-call | flops 1207959552 | bytes 2097152 | tf_op jit(solution)/shard_map/pallas_call | solution.py:460
  66.8 0.5 collective-permute-start.19
  67.3 0.1 collective-permute-start.20
  67.4 0.8 add_convert_fusion
  68.2 2.4 %shard_map.95 = (bf16[128,1152]{1,0:T(8,128)(2,1)S(1)}, f32[128,1152]{1,0:T(8,128)S(1)}) custom-call(s32[16]{0:T(128)S(1)} %stack.67.where_ref, bf16[2,2,4,128,1024]{4,3,2,1,0:T(8,128)(2,1)S(1)} %bitcast.34, bf16[2,2,4,128,1024]{4,3,2,1,0:T(8,128)(2,1)S(1)} %bitcast.30, bf16[1024,576]{1,0:T(8,128)(2,1)S(1)} %get-tuple-element.78.with_spread_ref, ...), custom_call_target="tpu_custom_call" | custom-call | flops 1207959552 | bytes 2097152 | tf_op jit(solution)/shard_map/pallas_call | solution.py:460
  70.6 2.4 %shard_map.97 = (bf16[128,1152]{1,0:T(8,128)(2,1)S(1)}, f32[128,1152]{1,0:T(8,128)S(1)}) custom-call(s32[16]{0:T(128)S(1)} %stack.67.where_ref, bf16[2,2,4,128,1024]{4,3,2,1,0:T(8,128)(2,1)S(1)} %bitcast.35, bf16[2,2,4,128,1024]{4,3,2,1,0:T(8,128)(2,1)S(1)} %bitcast.31, bf16[1024,576]{1,0:T(8,128)(2,1)S(1)} %get-tuple-element.78.with_spread_ref, ...), custom_call_target="tpu_custom_call" | custom-call | flops 1207959552 | bytes 2097152 | tf_op jit(solution)/shard_map/pallas_call | solution.py:460
  73.0 4.0 %all-to-all-start = ((bf16[8,4,16,192]{3,2,1,0:T(8,128)(2,1)}), bf16[8,4,16,192]{3,2,1,0:T(8,128)(2,1)S(1)}, u32[]{:S(2)}, u32[]{:S(2)}) async-start(bf16[8,4,16,192]{3,2,1,0:T(8,128)(2,1)} %add_convert_fusion), calls=%async_computation | async-start | bytes 524288 | tf_op jit(solution)/shard_map/all_to_all | solution.py:626
  77.0 2.5 %collective-permute-start.24 = (bf16[128,1152]{1,0:T(8,128)(2,1)S(1)}, bf16[128,1152]{1,0:T(8,128)(2,1)S(1)}, u32[]{:S(2)}, u32[]{:S(2)}) collective-permute-start(bf16[128,1152]{1,0:T(8,128)(2,1)S(1)} %get-tuple-element.102), channel_id=1, source_target_pairs={{0,4},{1,5},{2,6},{3,7},{4,0},{5,1},{6,2},{7,3},{8,12},{9,13},{10,... | collective-permute-start | bytes 884744 | tf_op jit(solution)/shard_map/ppermute | solution.py:27
  79.5 2.7 %collective-permute-start.23 = (bf16[128,1152]{1,0:T(8,128)(2,1)S(1)}, bf16[128,1152]{1,0:T(8,128)(2,1)S(1)}, u32[]{:S(2)}, u32[]{:S(2)}) collective-permute-start(bf16[128,1152]{1,0:T(8,128)(2,1)S(1)} %get-tuple-element.99), channel_id=1, source_target_pairs={{0,3},{1,0},{2,1},{3,2},{4,7},{5,4},{6,5},{7,6},{8,11},{9,8},{10,9... | collective-permute-start | bytes 884744 | tf_op jit(solution)/shard_map/ppermute | solution.py:27
  82.2 4.2 %collective-permute-done.24.arrived_ref = bf16[128,1152]{1,0:T(8,128)(2,1)S(1)} collective-permute-done((bf16[128,1152]{1,0:T(8,128)(2,1)S(1)}, bf16[128,1152]{1,0:T(8,128)(2,1)S(1)}, u32[]{:S(2)}, u32[]{:S(2)}) %collective-permute-start.24) | collective-permute-done | bytes 294944 | tf_op jit(solution)/shard_map/ppermute | solution.py:27
  86.4 0.1 shard_map.100
  86.5 3.0 %collective-permute-start.25 = (bf16[64,1152]{1,0:T(8,128)(2,1)S(1)}, bf16[64,1152]{1,0:T(8,128)(2,1)S(1)}, u32[]{:S(2)}, u32[]{:S(2)}) collective-permute-start(bf16[64,1152]{1,0:T(8,128)(2,1)S(1)} %get-tuple-element.103), channel_id=1, source_target_pairs={{0,2},{1,3},{2,0},{3,1},{4,6},{5,7},{6,4},{7,5},{8,10},{9,11},{10,... | collective-permute-start | bytes 442376 | tf_op jit(solution)/shard_map/ppermute | solution.py:27
  89.5 0.4 collective-permute-start.26
  89.9 0.1 shard_map.99
  90.0 2.5 %collective-permute-start.27 = (bf16[64,1152]{1,0:T(8,128)(2,1)S(1)}, bf16[64,1152]{1,0:T(8,128)(2,1)S(1)}, u32[]{:S(2)}, u32[]{:S(2)}) collective-permute-start(bf16[64,1152]{1,0:T(8,128)(2,1)S(1)} %get-tuple-element.105), channel_id=1, source_target_pairs={{0,4},{1,5},{2,6},{3,7},{4,0},{5,1},{6,2},{7,3},{8,12},{9,13},{10,... | collective-permute-start | bytes 442376 | tf_op jit(solution)/shard_map/ppermute | solution.py:27
  92.6 2.5 %collective-permute-start.22 = (bf16[8,4,192]{2,1,0:T(4,128)(2,1)S(1)}, bf16[8,4,192]{2,1,0:T(4,128)(2,1)S(1)}, u32[]{:S(2)}, u32[]{:S(2)}) collective-permute-start(bf16[8,4,192]{2,1,0:T(4,128)(2,1)S(1)} %get-tuple-element.108), channel_id=1, source_target_pairs={{0,8},{8,0},{16,24},{24,16},{32,40},{40,32},{48,56},{56,48},{64,72... | collective-permute-start | bytes 36872 | tf_op jit(solution)/shard_map/ppermute | solution.py:27
  95.1 0.8 collective-permute-done.22
  96.0 0.6 copy.10
  96.6 0.0 collective-permute-done.26.refs_1_
  96.6 0.8 shard_map.101
  (33 shorter events, 0.2 us)
Async XLA Ops:
  0.6 22.5 %collective-permute-start.10 = (bf16[1024,576]{0,1:T(8,128)(2,1)}, bf16[1024,576]{0,1:T(8,128)(2,1)S(1)}, u32[]{:S(2)}, u32[]{:S(2)}) collective-permute-start(bf16[1024,576]{0,1:T(8,128)(2,1)} %param.10), channel_id=1, source_target_pairs={{0,8},{8,0},{16,24},{24,16},{32,40},{40,32},{48,56},{56,48},{64,72... | collective-permute-start | bytes 3538952 | tf_op jit(solution)/shard_map/ppermute | solution.py:27
  4.7 0.8 copy-start.3
  5.5 0.7 copy-start.4
  6.8 1.3 %collective-permute-start = (bf16[16,640]{1,0:T(8,128)(2,1)S(1)}, bf16[16,640]{1,0:T(8,128)(2,1)S(1)}, u32[]{:S(2)}, u32[]{:S(2)}) collective-permute-start(bf16[16,640]{1,0:T(8,128)(2,1)S(1)} %get-tuple-element.55), channel_id=1, source_target_pairs={{0,8},{8,0},{16,24},{24,16},{32,40},{40,32},{48,56},{56,48},{64,72... | collective-permute-start | bytes 61448 | tf_op jit(solution)/shard_map/ppermute | solution.py:27
  8.1 2.9 %collective-permute-start.1 = (bf16[32,640]{1,0:T(8,128)(2,1)S(1)}, bf16[32,640]{1,0:T(8,128)(2,1)S(1)}, u32[]{:S(2)}, u32[]{:S(2)}) collective-permute-start(bf16[32,640]{1,0:T(8,128)(2,1)S(1)} %pad_maximum_fusion), channel_id=1, source_target_pairs={{0,16},{8,24},{16,0},{24,8},{32,48},{40,56},{48,32},{56,40},{64,80... | collective-permute-start | bytes 122888 | tf_op jit(solution)/shard_map/ppermute | solution.py:27
  8.1 1.9 %collective-permute-start.2 = (f32[4]{0:T(128)}, f32[4]{0:T(128)S(1)}, u32[]{:S(2)}, u32[]{:S(2)}) collective-permute-start(f32[4]{0:T(128)} %refs_12_.1), channel_id=1, source_target_pairs={{0,8},{8,0},{16,24},{24,16},{32,40},{40,32},{48,56},{56,48},{64,72... | collective-permute-start | bytes 56 | tf_op jit(solution)/shard_map/ppermute | solution.py:27
  8.3 1.3 %copy-start = (bf16[1024,576]{0,1:T(8,128)(2,1)S(1)}, bf16[1024,576]{0,1:T(8,128)(2,1)}, u32[]{:S(2)}) copy-start(bf16[1024,576]{0,1:T(8,128)(2,1)} %param.10) | copy-start | bytes 3538948
  9.6 13.7 %copy-start.1 = (bf16[1024,576]{0,1:T(8,128)(2,1)S(1)}, bf16[1024,576]{0,1:T(8,128)(2,1)}, u32[]{:S(2)}) copy-start(bf16[1024,576]{0,1:T(8,128)(2,1)} %param.10) | copy-start | bytes 3538948
  11.0 7.6 %collective-permute-start.6 = (bf16[64,640]{1,0:T(8,128)(2,1)S(1)}, bf16[64,640]{1,0:T(8,128)(2,1)S(1)}, u32[]{:S(2)}, u32[]{:S(2)}) collective-permute-start(bf16[64,640]{1,0:T(8,128)(2,1)S(1)} %maximum_select_fusion.refs_0_), channel_id=1, source_target_pairs={{0,64},{8,72},{16,80},{24,88},{32,96},{40,104},{48,112},{56,120},{... | collective-permute-start | bytes 245768 | tf_op jit(solution)/shard_map/ppermute | solution.py:27
  12.8 8.4 %collective-permute-start.4 = (bf16[64,640]{1,0:T(8,128)(2,1)S(1)}, bf16[64,640]{1,0:T(8,128)(2,1)S(1)}, u32[]{:S(2)}, u32[]{:S(2)}) collective-permute-start(bf16[64,640]{1,0:T(8,128)(2,1)S(1)} %maximum_select_fusion.refs_0_), channel_id=1, source_target_pairs={{0,192},{8,200},{16,208},{24,216},{32,224},{40,232},{48,240},{56,2... | collective-permute-start | bytes 245768 | tf_op jit(solution)/shard_map/ppermute | solution.py:27
  15.9 10.9 %collective-permute-start.9 = (bf16[64,640]{1,0:T(8,128)(2,1)S(1)}, bf16[64,640]{1,0:T(8,128)(2,1)S(1)}, u32[]{:S(2)}, u32[]{:S(2)}) collective-permute-start(bf16[64,640]{1,0:T(8,128)(2,1)S(1)} %maximum_select_fusion.refs_0_), channel_id=1, source_target_pairs={{0,32},{8,40},{16,48},{24,56},{32,64},{40,72},{48,80},{56,88},{64,... | collective-permute-start | bytes 245768 | tf_op jit(solution)/shard_map/ppermute | solution.py:27
  16.7 10.2 %collective-permute-start.3 = (bf16[64,640]{1,0:T(8,128)(2,1)S(1)}, bf16[64,640]{1,0:T(8,128)(2,1)S(1)}, u32[]{:S(2)}, u32[]{:S(2)}) collective-permute-start(bf16[64,640]{1,0:T(8,128)(2,1)S(1)} %maximum_select_fusion.refs_0_), channel_id=1, source_target_pairs={{0,224},{8,232},{16,240},{24,248},{32,0},{40,8},{48,16},{56,24},{6... | collective-permute-start | bytes 245768 | tf_op jit(solution)/shard_map/ppermute | solution.py:27
  18.6 8.2 %collective-permute-start.8 = (bf16[64,640]{1,0:T(8,128)(2,1)S(1)}, bf16[64,640]{1,0:T(8,128)(2,1)S(1)}, u32[]{:S(2)}, u32[]{:S(2)}) collective-permute-start(bf16[64,640]{1,0:T(8,128)(2,1)S(1)} %collective-permute-done.6.refs_6_), channel_id=1, source_target_pairs={{0,32},{8,40},{16,48},{24,56},{32,64},{40,72},{48,80},{56,88},{64,... | collective-permute-start | bytes 245768 | tf_op jit(solution)/shard_map/ppermute | solution.py:27
  21.2 6.1 %collective-permute-start.7 = (bf16[64,640]{1,0:T(8,128)(2,1)S(1)}, bf16[64,640]{1,0:T(8,128)(2,1)S(1)}, u32[]{:S(2)}, u32[]{:S(2)}) collective-permute-start(bf16[64,640]{1,0:T(8,128)(2,1)S(1)} %collective-permute-done.6.refs_6_), channel_id=1, source_target_pairs={{0,64},{8,72},{16,80},{24,88},{32,96},{40,104},{48,112},{56,120},{... | collective-permute-start | bytes 245768 | tf_op jit(solution)/shard_map/ppermute | solution.py:27
  23.1 4.1 %collective-permute-start.5 = (bf16[64,640]{1,0:T(8,128)(2,1)S(1)}, bf16[64,640]{1,0:T(8,128)(2,1)S(1)}, u32[]{:S(2)}, u32[]{:S(2)}) collective-permute-start(bf16[64,640]{1,0:T(8,128)(2,1)S(1)} %collective-permute-done.4.refs_2_), channel_id=1, source_target_pairs={{0,224},{8,232},{16,240},{24,248},{32,0},{40,8},{48,16},{56,24},{6... | collective-permute-start | bytes 245768 | tf_op jit(solution)/shard_map/ppermute | solution.py:27
  23.2 2.2 %copy-start.2 = (bf16[16,512,256]{2,1,0:T(8,128)(2,1)S(1)}, bf16[16,512,256]{2,1,0:T(8,128)(2,1)}, u32[]{:S(2)}) copy-start(bf16[16,512,256]{2,1,0:T(8,128)(2,1)} %kv_ref.1) | copy-start | bytes 12582916
  25.4 1.8 %copy-start.6 = (f32[4]{0:T(128)S(1)}, f32[4]{0:T(128)}, u32[]{:S(2)}) copy-start(f32[4]{0:T(128)} %refs_12_.1) | copy-start | bytes 52
  37.4 5.5 %collective-permute-start.13 = (f32[4,1024]{1,0:T(4,128)S(1)}, f32[4,1024]{1,0:T(4,128)S(1)}, u32[]{:S(2)}, u32[]{:S(2)}) collective-permute-start(f32[4,1024]{1,0:T(4,128)S(1)} %get-tuple-element.64.refs_0_.refs_4_), channel_id=1, source_target_pairs={{0,48},{8,56},{16,32},{24,40},{32,16},{40,24},{48,0},{56,8},{64,11... | collective-permute-start | bytes 49160 | tf_op jit(solution)/shard_map/ppermute | solution.py:27
  39.2 3.8 %collective-permute-start.12 = (f32[4,1024]{1,0:T(4,128)S(1)}, f32[4,1024]{1,0:T(4,128)S(1)}, u32[]{:S(2)}, u32[]{:S(2)}) collective-permute-start(f32[4,1024]{1,0:T(4,128)S(1)} %get-tuple-element.64.refs_0_.refs_4_), channel_id=1, source_target_pairs={{0,32},{8,40},{16,48},{24,56},{32,0},{40,8},{48,16},{56,24},{64,96... | collective-permute-start | bytes 49160 | tf_op jit(solution)/shard_map/ppermute | solution.py:27
  39.2 3.7 %collective-permute-start.11 = (f32[4,1024]{1,0:T(4,128)S(1)}, f32[4,1024]{1,0:T(4,128)S(1)}, u32[]{:S(2)}, u32[]{:S(2)}) collective-permute-start(f32[4,1024]{1,0:T(4,128)S(1)} %get-tuple-element.64.refs_0_.refs_4_), channel_id=1, source_target_pairs={{0,16},{8,24},{16,0},{24,8},{32,48},{40,56},{48,32},{56,40},{64,80... | collective-permute-start | bytes 49160 | tf_op jit(solution)/shard_map/ppermute | solution.py:27
  43.0 9.7 %copy-start.5 = (s32[4]{0:T(128)S(1)}, s32[4]{0:T(128)}, u32[]{:S(2)}) copy-start(s32[4]{0:T(128)} %lens_ref.1) | copy-start | bytes 52
  43.0 8.6 %collective-permute-start.16 = (f32[4,1024]{1,0:T(4,128)S(1)}, f32[4,1024]{1,0:T(4,128)S(1)}, u32[]{:S(2)}, u32[]{:S(2)}) collective-permute-start(f32[4,1024]{1,0:T(4,128)S(1)} %shard_map.91.refs_0_), channel_id=1, source_target_pairs={{0,192},{8,200},{16,208},{24,216},{32,224},{40,232},{48,240},{56,2... | collective-permute-start | bytes 49160 | tf_op jit(solution)/shard_map/ppermute | solution.py:27
  44.2 7.5 %collective-permute-start.15 = (f32[4,1024]{1,0:T(4,128)S(1)}, f32[4,1024]{1,0:T(4,128)S(1)}, u32[]{:S(2)}, u32[]{:S(2)}) collective-permute-start(f32[4,1024]{1,0:T(4,128)S(1)} %shard_map.91.refs_0_), channel_id=1, source_target_pairs={{0,128},{8,136},{16,144},{24,152},{32,160},{40,168},{48,176},{56,1... | collective-permute-start | bytes 49160 | tf_op jit(solution)/shard_map/ppermute | solution.py:27
  49.1 3.7 %collective-permute-start.14 = (f32[4,1024]{1,0:T(4,128)S(1)}, f32[4,1024]{1,0:T(4,128)S(1)}, u32[]{:S(2)}, u32[]{:S(2)}) collective-permute-start(f32[4,1024]{1,0:T(4,128)S(1)} %shard_map.91.refs_0_), channel_id=1, source_target_pairs={{0,64},{8,72},{16,80},{24,88},{32,96},{40,104},{48,112},{56,120},{... | collective-permute-start | bytes 49160 | tf_op jit(solution)/shard_map/ppermute | solution.py:27
  55.9 11.5 %collective-permute-start.21 = (bf16[8,4,16,192]{3,2,1,0:T(8,128)(2,1)S(1)}, bf16[8,4,16,192]{3,2,1,0:T(8,128)(2,1)S(1)}, u32[]{:S(2)}, u32[]{:S(2)}) collective-permute-start(bf16[8,4,16,192]{3,2,1,0:T(8,128)(2,1)S(1)} %get-tuple-element.96), channel_id=1, source_target_pairs={{0,16},{8,24},{16,0},{24,8},{32,48},{40,56},{48,32},{56,40},{64,80... | collective-permute-start | bytes 589832 | tf_op jit(solution)/shard_map/ppermute | solution.py:27
  58.5 9.6 %collective-permute-start.17 = (bf16[128,1152]{1,0:T(8,128)(2,1)S(1)}, bf16[128,1152]{1,0:T(8,128)(2,1)S(1)}, u32[]{:S(2)}, u32[]{:S(2)}) collective-permute-start(bf16[128,1152]{1,0:T(8,128)(2,1)S(1)} %get-tuple-element.82), channel_id=1, source_target_pairs={{0,8},{8,0},{16,24},{24,16},{32,40},{40,32},{48,56},{56,48},{64,72... | collective-permute-start | bytes 884744 | tf_op jit(solution)/shard_map/ppermute | solution.py:27
  64.3 3.9 %collective-permute-start.18 = (bf16[128,1152]{1,0:T(8,128)(2,1)S(1)}, bf16[128,1152]{1,0:T(8,128)(2,1)S(1)}, u32[]{:S(2)}, u32[]{:S(2)}) collective-permute-start(bf16[128,1152]{1,0:T(8,128)(2,1)S(1)} %get-tuple-element.83), channel_id=1, source_target_pairs={{0,8},{8,0},{16,24},{24,16},{32,40},{40,32},{48,56},{56,48},{64,72... | collective-permute-start | bytes 884744 | tf_op jit(solution)/shard_map/ppermute | solution.py:27
  66.8 3.8 %collective-permute-start.19 = (bf16[128,1152]{1,0:T(8,128)(2,1)S(1)}, bf16[128,1152]{1,0:T(8,128)(2,1)S(1)}, u32[]{:S(2)}, u32[]{:S(2)}) collective-permute-start(bf16[128,1152]{1,0:T(8,128)(2,1)S(1)} %get-tuple-element.87), channel_id=1, source_target_pairs={{0,8},{8,0},{16,24},{24,16},{32,40},{40,32},{48,56},{56,48},{64,72... | collective-permute-start | bytes 884744 | tf_op jit(solution)/shard_map/ppermute | solution.py:27
  67.3 3.3 %collective-permute-start.20 = (bf16[128,1152]{1,0:T(8,128)(2,1)S(1)}, bf16[128,1152]{1,0:T(8,128)(2,1)S(1)}, u32[]{:S(2)}, u32[]{:S(2)}) collective-permute-start(bf16[128,1152]{1,0:T(8,128)(2,1)S(1)} %get-tuple-element.88), channel_id=1, source_target_pairs={{0,8},{8,0},{16,24},{24,16},{32,40},{40,32},{48,56},{56,48},{64,72... | collective-permute-start | bytes 884744 | tf_op jit(solution)/shard_map/ppermute | solution.py:27
  73.0 19.5 %all-to-all-start = ((bf16[8,4,16,192]{3,2,1,0:T(8,128)(2,1)}), bf16[8,4,16,192]{3,2,1,0:T(8,128)(2,1)S(1)}, u32[]{:S(2)}, u32[]{:S(2)}) async-start(bf16[8,4,16,192]{3,2,1,0:T(8,128)(2,1)} %add_convert_fusion), calls=%async_computation | async-start | bytes 524288 | tf_op jit(solution)/shard_map/all_to_all | solution.py:626
  77.0 9.4 %collective-permute-start.24 = (bf16[128,1152]{1,0:T(8,128)(2,1)S(1)}, bf16[128,1152]{1,0:T(8,128)(2,1)S(1)}, u32[]{:S(2)}, u32[]{:S(2)}) collective-permute-start(bf16[128,1152]{1,0:T(8,128)(2,1)S(1)} %get-tuple-element.102), channel_id=1, source_target_pairs={{0,4},{1,5},{2,6},{3,7},{4,0},{5,1},{6,2},{7,3},{8,12},{9,13},{10,... | collective-permute-start | bytes 884744 | tf_op jit(solution)/shard_map/ppermute | solution.py:27
  79.5 10.4 %collective-permute-start.23 = (bf16[128,1152]{1,0:T(8,128)(2,1)S(1)}, bf16[128,1152]{1,0:T(8,128)(2,1)S(1)}, u32[]{:S(2)}, u32[]{:S(2)}) collective-permute-start(bf16[128,1152]{1,0:T(8,128)(2,1)S(1)} %get-tuple-element.99), channel_id=1, source_target_pairs={{0,3},{1,0},{2,1},{3,2},{4,7},{5,4},{6,5},{7,6},{8,11},{9,8},{10,9... | collective-permute-start | bytes 884744 | tf_op jit(solution)/shard_map/ppermute | solution.py:27
  86.5 10.1 %collective-permute-start.25 = (bf16[64,1152]{1,0:T(8,128)(2,1)S(1)}, bf16[64,1152]{1,0:T(8,128)(2,1)S(1)}, u32[]{:S(2)}, u32[]{:S(2)}) collective-permute-start(bf16[64,1152]{1,0:T(8,128)(2,1)S(1)} %get-tuple-element.103), channel_id=1, source_target_pairs={{0,2},{1,3},{2,0},{3,1},{4,6},{5,7},{6,4},{7,5},{8,10},{9,11},{10,... | collective-permute-start | bytes 442376 | tf_op jit(solution)/shard_map/ppermute | solution.py:27
  89.5 7.1 %collective-permute-start.26 = (bf16[64,1152]{1,0:T(8,128)(2,1)S(1)}, bf16[64,1152]{1,0:T(8,128)(2,1)S(1)}, u32[]{:S(2)}, u32[]{:S(2)}) collective-permute-start(bf16[64,1152]{1,0:T(8,128)(2,1)S(1)} %get-tuple-element.104), channel_id=1, source_target_pairs={{0,1},{1,2},{2,3},{3,0},{4,5},{5,6},{6,7},{7,4},{8,9},{9,10},{10,1... | collective-permute-start | bytes 442376 | tf_op jit(solution)/shard_map/ppermute | solution.py:27
  90.0 6.6 %collective-permute-start.27 = (bf16[64,1152]{1,0:T(8,128)(2,1)S(1)}, bf16[64,1152]{1,0:T(8,128)(2,1)S(1)}, u32[]{:S(2)}, u32[]{:S(2)}) collective-permute-start(bf16[64,1152]{1,0:T(8,128)(2,1)S(1)} %get-tuple-element.105), channel_id=1, source_target_pairs={{0,4},{1,5},{2,6},{3,7},{4,0},{5,1},{6,2},{7,3},{8,12},{9,13},{10,... | collective-permute-start | bytes 442376 | tf_op jit(solution)/shard_map/ppermute | solution.py:27
  92.6 3.3 %collective-permute-start.22 = (bf16[8,4,192]{2,1,0:T(4,128)(2,1)S(1)}, bf16[8,4,192]{2,1,0:T(4,128)(2,1)S(1)}, u32[]{:S(2)}, u32[]{:S(2)}) collective-permute-start(bf16[8,4,192]{2,1,0:T(4,128)(2,1)S(1)} %get-tuple-element.108), channel_id=1, source_target_pairs={{0,8},{8,0},{16,24},{24,16},{32,40},{40,32},{48,56},{56,48},{64,72... | collective-permute-start | bytes 36872 | tf_op jit(solution)/shard_map/ppermute | solution.py:27
